TPU v7x, 32 devices: a whole 2x2x4 slice. The times are simulated.
32 devices in a mesh: blk: 8 (over z, y), rhs: 4 (over x, core).
Axes of the slice: x: 2, y: 2, z: 4, core: 2. Of those that a mesh axis runs over, the one named last changes fastest.
Arguments:
- strips: float32 [64, 25, 128, 128], P('blk'), may hold values from -0.109375 to 0.109375
- near_cols: int32 [64, 25], P('blk'), may hold values from 0 to 63, as said below
- vector_block: float32 [8192, 2048], P(('blk', 'rhs')), may hold values from -6 to 6
- basis: float32 [4, 8192, 2048], P(None, ('blk', 'rhs')), may hold values from -0.0625 to 0.0625
Outputs:
- new_block: float32 [8192, 2048], P(('blk', 'rhs'))
- coeffs: float32 [4, 16, 128, 128], replicated
- factor: float32 [16, 128, 128], replicated
Inputs may be any that keep to these rules, and one draw needn't show every extreme that they name: `near_cols`: each row block has 25 distinct column blocks; slot 0 is the row block itself; every column block lies within 24 blocks of its row block, counted cyclically modulo 64, and some row block has a column block exactly 24 blocks above it.
All inputs are finite; a program needn't handle non-finite values.
Results may differ from a plain program's by a relative error of at most 0.0003.
Values sent between devices are 32-bit elements; how exact they have to be, the bound alone decides.
No kernel may reach another device: no remote copies, remote signals or barrier semaphores. Data moves between devices by JAX's collectives and lax.ppermute only.
A program may use at most 256 MiB of HBM per device.

v0:
```python
import jax
import jax.numpy as jnp
from jax import lax
from jax.sharding import PartitionSpec as P

HOPS = 3
GROUP = 128


HIGHEST = lax.Precision.HIGHEST


def from_behind(value, axis, by):
    devices = lax.axis_size(axis)
    return lax.ppermute(value, axis, [(i, (i + by) % devices) for i in range(devices)])


def apply_strips(window, positions, strips):
    block = strips.shape[2]
    width = window.shape[1]
    pieces = window.reshape(window.shape[0] // block, block, width)
    chosen = pieces[positions]
    result = jnp.einsum("ikab,ikbc->iac", strips, chosen, precision=HIGHEST)
    return result.reshape(strips.shape[0] * block, width)


def local(strips, near_cols, vector_block, basis):
    local_blocks = strips.shape[0]
    total_blocks = local_blocks * lax.axis_size("blk")
    row_form = lax.all_to_all(vector_block, "rhs", split_axis=1, concat_axis=0, tiled=True)
    gathered = []
    for offset in range(-HOPS, HOPS + 1):
        if offset == 0:
            gathered.append(row_form)
        else:
            gathered.append(from_behind(row_form, "blk", -offset))
    window = jnp.concatenate(gathered, axis=0)
    first_block = (lax.axis_index("blk") - HOPS) * local_blocks
    positions = jnp.mod(near_cols - first_block, total_blocks)
    image = apply_strips(window, positions, strips)
    column_form = lax.all_to_all(image, "rhs", split_axis=0, concat_axis=1, tiled=True)
    local_rows, width = column_form.shape
    groups = width // GROUP
    grouped = column_form.reshape(local_rows, groups, GROUP)
    basis_grouped = basis.reshape(basis.shape[0], local_rows, groups, GROUP)
    partial_value = jnp.einsum("mnga,ngb->mgab", basis_grouped, grouped, precision=HIGHEST)
    coeffs = lax.psum(partial_value, ("blk", "rhs"))
    residual = grouped - jnp.einsum("mnga,mgab->ngb", basis_grouped, coeffs, precision=HIGHEST)
    local_gram = jnp.einsum("nga,ngb->gab", residual, residual, precision=HIGHEST)
    gram = lax.psum(local_gram, ("blk", "rhs"))
    factor = jnp.linalg.cholesky(gram)
    solved = jax.scipy.linalg.solve_triangular(
        factor, jnp.transpose(residual, (1, 2, 0)), lower=True
    )
    new_block = jnp.transpose(solved, (2, 0, 1)).reshape(local_rows, width)
    return (new_block, coeffs, factor)


def solution(mesh):
    placed = (
        P("blk", None, None, None),
        P("blk", None),
        P(("blk", "rhs"), None),
        P(None, ("blk", "rhs"), None),
    )
    return jax.shard_map(
        local,
        mesh=mesh,
        in_specs=placed,
        out_specs=(P(("blk", "rhs"), None), P(), P()),
        check_vma=False,
    )
```

profile of v0, /device:TPU:1, one launch (start us, length us, event | category | flops | bytes accessed | tf_op | source)
XLA Modules:
  0.0 1078.9 jit_solution(11922437730446416908)
XLA Ops:
  7.2 0.0 all-reduce.3.cloned.1.call-start
  7.2 1.9 copy.36
  9.2 28.8 %all_to_all.35 = f32[256,4,512]{0,2,1:T(8,128)} all-to-all(f32[256,4,512]{0,2,1:T(8,128)S(1)} %bitcast.75), channel_id=1, replica_groups=mesh['blk'=8,'rhs'=4] {'rhs'}, dimensions={1} | all-to-all | bytes 4194304 | tf_op jit(solution)/shard_map/all_to_all | solution.py:30
  38.0 1.9 copy.37
  39.9 2.9 collective-permute-start
  42.8 1.3 collective-permute-start.1
  44.1 1.2 collective-permute-start.2
  45.3 2.9 collective-permute-start.3
  48.2 0.2 collective-permute-start.4
  48.4 175.3 %collective-permute-done = f32[1024,512]{1,0:T(8,128)S(1)} collective-permute-done((f32[1024,512]{1,0:T(8,128)S(1)}, f32[1024,512]{1,0:T(8,128)S(1)}, u32[]{:S(2)}, u32[]{:S(2)}) %collective-permute-start) | collective-permute-done | bytes 2097184 | tf_op jit(solution)/shard_map/ppermute | solution.py:15
  223.7 1.3 copy-done.1
  225.0 0.0 collective-permute-start.5
  225.1 0.1 reshape.44
  225.1 3.1 constant_dynamic-update-slice_fusion.6
  228.3 0.0 collective-permute-done.1
  228.3 3.1 constant_dynamic-update-slice_fusion.5
  231.4 0.0 collective-permute-done.2
  231.4 3.1 constant_dynamic-update-slice_fusion.4
  234.4 1.5 constant_dynamic-update-slice_fusion.3
  236.0 0.0 collective-permute-done.3
  236.0 3.1 constant_dynamic-update-slice_fusion.2
  239.0 0.0 collective-permute-done.4
  239.0 3.1 constant_dynamic-update-slice_fusion.1
  242.1 28.4 %collective-permute-done.5 = f32[1024,512]{1,0:T(8,128)} collective-permute-done((f32[1024,512]{1,0:T(8,128)S(1)}, f32[1024,512]{1,0:T(8,128)}, u32[]{:S(2)}, u32[]{:S(2)}) %collective-permute-start.5) | collective-permute-done | bytes 2097184 | tf_op jit(solution)/shard_map/ppermute | solution.py:15
  270.5 3.1 constant_dynamic-update-slice_fusion
  273.6 24.8 %gather_fusion = f32[200,128,512]{2,1,0:T(8,128)} fusion(f32[56,128,512]{2,1,0:T(8,128)} %bitcast.3, s32[1024]{0:T(1024)S(1)} %pad_clamp_fusion), kind=kCustom, calls=%fused_computation | custom fusion | bytes 104858400 | tf_op jit(solution)/shard_map/gather | solution.py:22
  298.3 33.5 %fusion.16 = f32[8,512,128,1]{1,2,3,0:T(8,128)S(1)} fusion(f32[8,25,128,512]{3,2,1,0:T(8,128)} %bitcast.61, f32[8,25,128,128]{3,2,1,0:T(8,128)} %param.4), kind=kOutput, calls=%fused_computation.33 | convolution fusion | flops 20132659200 | bytes 67633152 | tf_op jit(solution)/shard_map/ikab,ikbc->iac/dot_general | solution.py:23
  331.9 31.5 %all_to_all.36 = f32[4,256,512]{2,1,0:T(8,128)} all-to-all(f32[4,256,512]{2,1,0:T(8,128)S(1)} %bitcast.64), channel_id=1, replica_groups=mesh['blk'=8,'rhs'=4] {'rhs'}, dimensions={0} | all-to-all | bytes 4194304 | tf_op jit(solution)/shard_map/all_to_all | solution.py:41
  363.4 1.9 copy.38
  365.3 0.0 copy-start
  365.3 11.5 %fusion.6 = f32[4,16,128,128]{2,3,0,1:T(8,128)} fusion(f32[256,16,128,1]{0,2,3,1:T(8,128)S(1)} %bitcast.62, f32[4,256,2048]{2,1,0:T(8,128)} %param.7), kind=kOutput, calls=%fused_computation.7 | convolution fusion | flops 3221225472 | bytes 14680064 | tf_op jit(solution)/shard_map/mnga,ngb->mgab/dot_general | solution.py:46
  376.8 0.0 all-reduce.3.cloned.1.call-update
  376.9 0.3 all-reduce.5.cloned.1.call-start
  377.1 190.4 %all-reduce.3.cloned.1.call-done = f32[4,16,128,128]{2,3,0,1:T(8,128)} async-done(((f32[4,16,128,128]{2,3,0,1:T(8,128)}), f32[4,16,128,128]{2,3,0,1:T(8,128)}) %all-reduce.3.cloned.1.call-update) | async-done | bytes 4194320 | tf_op jit(solution)/shard_map/psum | solution.py:47
  567.5 13.7 %bitcast_subtract_fusion = f32[256,16,128]{0,2,1:T(8,128)S(1)} fusion(f32[256,16,128]{0,2,1:T(8,128)} %bitcast.63, f32[4,16,128,128]{2,3,0,1:T(8,128)} %all-reduce.3.cloned.1.call-done, f32[4,256,2048]{2,1,0:T(8,128)} %param.7), kind=kOutput, calls=%fused_computation.8 | convolution fusion | flops 3221749760 | bytes 16777216 | tf_op jit(solution)/shard_map/mnga,mgab->ngb/dot_general | solution.py:48
  581.2 3.1 fusion.17
  584.3 0.0 all-reduce.5.cloned.1.call-update
  584.4 5.6 copy.46
  590.0 124.1 %all-reduce.5.cloned.1.call-done = f32[16,128,128]{1,2,0:T(8,128)} async-done(((f32[16,128,128]{1,2,0:T(8,128)}), f32[16,128,128]{1,2,0:T(8,128)}) %all-reduce.5.cloned.1.call-update) | async-done | bytes 1048592 | tf_op jit(solution)/shard_map/psum | solution.py:50
  714.1 1.6 copy.43
  715.7 2.3 fusion.14
  718.0 188.3 %custom-call.8 = f32[16,128,128]{2,1,0:T(8,128)S(1)} custom-call(f32[16,128,128]{2,1,0:T(8,128)} %fusion.14), custom_call_target="Cholesky" | custom-call | tf_op jit(solution)/shard_map/jit(cholesky)/cholesky | solution.py:51
  906.3 0.1 select_reduce_fusion
  906.4 0.1 compare_reduce_fusion
  906.5 1.5 select_bitcast_fusion
  908.0 157.9 %custom-call.9 = f32[16,1,128,128]{2,3,1,0:T(8,128)S(1)} custom-call(f32[16,1,128,128]{3,2,1,0:T(8,128)} %get-tuple-element.15), custom_call_target="InvertDiagBlocksLowerTriangular" | custom-call | tf_op jit(solution)/shard_map/jit(_solve_triangular)/vmap()/triangular_solve | solution.py:52
  1066.0 3.2 fusion.9
  1069.2 2.9 copy.45
  (8 shorter events, 0.1 us)
Async XLA Ops:
  7.2 217.9 %copy-start.2 = (s32[8,25]{1,0:T(8,128)S(1)}, s32[8,25]{1,0:T(8,128)}, u32[]{:S(2)}) copy-start(s32[8,25]{1,0:T(8,128)} %param.5) | copy-start | bytes 2404
  7.2 560.4 %all-reduce.3.cloned.1.call-start = ((), (), s32[]{:S(2)}) async-start(), calls=%async_computation.2 | async-start | bytes 8388608 | tf_op jit(solution)/shard_map/psum | solution.py:47
  39.9 183.8 %collective-permute-start = (f32[1024,512]{1,0:T(8,128)S(1)}, f32[1024,512]{1,0:T(8,128)S(1)}, u32[]{:S(2)}, u32[]{:S(2)}) collective-permute-start(f32[1024,512]{1,0:T(8,128)S(1)} %bitcast.65), channel_id=1, source_target_pairs={{0,12},{4,16},{8,20},{12,24},{16,28},{20,0},{24,4},{28,8},{1,13},{... | collective-permute-start | bytes 6291464 | tf_op jit(solution)/shard_map/ppermute | solution.py:15
  42.8 185.5 %collective-permute-start.1 = (f32[1024,512]{1,0:T(8,128)S(1)}, f32[1024,512]{1,0:T(8,128)}, u32[]{:S(2)}, u32[]{:S(2)}) collective-permute-start(f32[1024,512]{1,0:T(8,128)S(1)} %bitcast.66), channel_id=1, source_target_pairs={{0,8},{4,12},{8,16},{12,20},{16,24},{20,28},{24,0},{28,4},{1,9},{5... | collective-permute-start | bytes 6291464 | tf_op jit(solution)/shard_map/ppermute | solution.py:15
  44.1 187.3 %collective-permute-start.2 = (f32[1024,512]{1,0:T(8,128)S(1)}, f32[1024,512]{1,0:T(8,128)}, u32[]{:S(2)}, u32[]{:S(2)}) collective-permute-start(f32[1024,512]{1,0:T(8,128)S(1)} %bitcast.67), channel_id=1, source_target_pairs={{0,4},{4,8},{8,12},{12,16},{16,20},{20,24},{24,28},{28,0},{1,5},{5... | collective-permute-start | bytes 6291464 | tf_op jit(solution)/shard_map/ppermute | solution.py:15
  45.3 190.6 %collective-permute-start.3 = (f32[1024,512]{1,0:T(8,128)S(1)}, f32[1024,512]{1,0:T(8,128)}, u32[]{:S(2)}, u32[]{:S(2)}) collective-permute-start(f32[1024,512]{1,0:T(8,128)S(1)} %bitcast.68), channel_id=1, source_target_pairs={{0,28},{4,0},{8,4},{12,8},{16,12},{20,16},{24,20},{28,24},{1,29},{... | collective-permute-start | bytes 6291464 | tf_op jit(solution)/shard_map/ppermute | solution.py:15
  48.2 190.8 %collective-permute-start.4 = (f32[1024,512]{1,0:T(8,128)S(1)}, f32[1024,512]{1,0:T(8,128)}, u32[]{:S(2)}, u32[]{:S(2)}) collective-permute-start(f32[1024,512]{1,0:T(8,128)S(1)} %bitcast.69), channel_id=1, source_target_pairs={{0,24},{4,28},{8,0},{12,4},{16,8},{20,12},{24,16},{28,20},{1,25},{... | collective-permute-start | bytes 6291464 | tf_op jit(solution)/shard_map/ppermute | solution.py:15
  223.7 1.3 copy-start.1
  225.0 45.5 %collective-permute-start.5 = (f32[1024,512]{1,0:T(8,128)S(1)}, f32[1024,512]{1,0:T(8,128)}, u32[]{:S(2)}, u32[]{:S(2)}) collective-permute-start(f32[1024,512]{1,0:T(8,128)S(1)} %bitcast.70), channel_id=1, source_target_pairs={{0,20},{4,24},{8,28},{12,0},{16,4},{20,8},{24,12},{28,16},{1,21},{... | collective-permute-start | bytes 6291464 | tf_op jit(solution)/shard_map/ppermute | solution.py:15
  365.3 11.6 %copy-start = (f32[256,4,512]{0,2,1:T(8,128)}, f32[256,4,512]{0,2,1:T(8,128)S(1)}, u32[]{:S(2)}) copy-start(f32[256,4,512]{0,2,1:T(8,128)S(1)} %copy.38) | copy-start | bytes 6291460
  376.9 337.3 %all-reduce.5.cloned.1.call-start = ((), (), s32[]{:S(2)}) async-start(), calls=%async_computation.3 | async-start | bytes 2097152 | tf_op jit(solution)/shard_map/psum | solution.py:50
Sparse Core Ops, SparseCore 0:
  377.0 190.5 all-reduce.2
  584.5 129.5 all-reduce.4
where the time goes:
time: 1080 us
  waiting for transfers between devices  518 us (48%)
  other arithmetic  350 us (32%)
  matrix products  65.1 us (6%)
  local copies, waits for them, and re-layouts  62 us (6%)
  blocking collectives  60.3 us (6%)
  between operations  14.2 us (1%)
    ppermute x6, waiting for transfers between devices, from_behind(): lax.ppermute(value, axis, [(i, (i + by) % devices) for i in range(devices)])  204 us
    psum x1, waiting for transfers between devices, local(): coeffs = lax.psum(partial_value, ('blk', 'rhs'))  190 us
    another operation x4, other arithmetic, local(): factor = jnp.linalg.cholesky(gram)  189 us
    another operation x3, other arithmetic, local(): jax.scipy.linalg.solve_triangular(factor, jnp.transpose(residual, (1, 2,...  159 us
    psum x1, waiting for transfers between devices, local(): gram = lax.psum(local_gram, ('blk', 'rhs'))  124 us
    dot_general x1, matrix products, apply_strips(): result = jnp.einsum('ikab,ikbc->iac', strips, chosen, precision=HIGHEST)  33.5 us
    all_to_all x1, blocking collectives, local(): lax.all_to_all(image, 'rhs', split_axis=0, concat_axis=1, tiled=True)  31.5 us
    all_to_all x1, blocking collectives, local(): lax.all_to_all(vector_block, 'rhs', split_axis=1, concat_axis=0, tiled=True)  28.8 us
  transfers between devices with their start and end apart: 8, of which 4 were waited for; matrix products, arithmetic and copies ran while one was open for 2% of the time, Pallas kernels for 0%

commit v1 on v0

v1 whole, which is shorter than its diff:
```python
import functools

import jax
import jax.numpy as jnp
import numpy as np
from jax import lax
from jax.experimental import pallas as pl
from jax.experimental.pallas import tpu as pltpu
from jax.sharding import PartitionSpec as P

GROUP = 128
BAND = 24
PANEL = 32
CHUNKS = (2, 1, 1)

F32 = jnp.float32
BF16 = jnp.bfloat16
ANY = pl.BlockSpec(memory_space=pl.ANY)
SMEM = pl.BlockSpec(memory_space=pltpu.SMEM)
VMEM = pl.BlockSpec(memory_space=pltpu.VMEM)
LIMIT = 50 * 1024 * 1024


def params(**kw):
    return pltpu.CompilerParams(vmem_limit_bytes=LIMIT, **kw)


def permute(value, axis, pairs):
    return lax.ppermute(value, axis, pairs)


def swap(value, axis, k):
    return permute(value, axis, [(i, i ^ k) for i in range(lax.axis_size(axis))])


def split(value):
    high = value.astype(BF16)
    return high, (value - high.astype(F32)).astype(BF16)


def dot3(a, b, dims):
    a_high, a_low = split(a)
    b_high, b_low = split(b)

    def one(x, y):
        return lax.dot_general(x, y, (dims, ((), ())), preferred_element_type=F32)

    return one(a_high, b_high) + (one(a_high, b_low) + one(a_low, b_high))


def run_copies(copies, sems):
    started = [pltpu.make_async_copy(a, b, sems.at[i]) for i, (a, b) in enumerate(copies)]
    for copy in started:
        copy.start()
    for copy in started:
        copy.wait()


def aligned(index, step):
    return pl.ds(pl.multiple_of(index * step, step), step)


def cut_columns(value, me, c0, width, parts, after=()):
    lead, total = value.shape[:-1], value.shape[-1]
    step = total // parts

    def kernel(me_ref, src, *rest):
        outs, sems = rest[len(after):-1], rest[-1]
        copies = []
        for k in range(1, parts):
            start = pl.multiple_of((me_ref[0] ^ k) * step + c0, GROUP)
            at = (slice(None),) * len(lead) + (pl.ds(start, width),)
            copies.append((src.at[at], outs[k - 1]))
        run_copies(copies, sems)

    return pl.pallas_call(
        kernel,
        out_shape=[jax.ShapeDtypeStruct(lead + (width,), value.dtype)] * (parts - 1),
        in_specs=[SMEM, ANY] + [ANY] * len(after),
        out_specs=[ANY] * (parts - 1),
        scratch_shapes=[pltpu.SemaphoreType.DMA((parts - 1,))],
        compiler_params=params(),
        name="cut_columns",
    )(me, value, *after)


def join_rows(value, received, me, c0, widths, parts):
    lead, rows, total = value.shape[:-2], value.shape[-2], value.shape[-1]
    step = total // parts
    whole = (slice(None),) * len(lead)

    def kernel(me_ref, src, *rest):
        got, outs, sems = rest[:parts - 1], rest[parts - 1:-1], rest[-1]
        copies = []
        at = 0
        for out, width in zip(outs, widths):
            for k in range(parts):
                dst = out.at[whole + (aligned(me_ref[0] ^ k, rows), slice(None))]
                if k == 0:
                    start = pl.multiple_of(me_ref[0] * step + c0 + at, GROUP)
                    copies.append((src.at[whole + (slice(None), pl.ds(start, width))], dst))
                else:
                    copies.append((got[k - 1].at[whole + (slice(None), pl.ds(at, width))], dst))
            at += width
        run_copies(copies, sems)

    return pl.pallas_call(
        kernel,
        out_shape=[jax.ShapeDtypeStruct(lead + (rows * parts, w), value.dtype) for w in widths],
        in_specs=[SMEM, ANY] + [ANY] * (parts - 1),
        out_specs=[ANY] * len(widths),
        scratch_shapes=[pltpu.SemaphoreType.DMA((parts * len(widths),))],
        compiler_params=params(),
        name="join_rows",
    )(me, value, *received)


def plan_window(devices, hops):
    if devices == 2 * hops + 2 and devices == 8:
        table = np.full((devices, devices), 0, np.int32)
        for z in range(4):
            for y in range(2):
                inner = z in (1, 2)
                far = 3 - z
                cross = far if inner else (2 if z == 0 else 1)
                order = [
                    (z, y), (z ^ 1, y), (far, y), (cross, 1 - y), (z, 1 - y), (z ^ 1, 1 - y),
                    ((3 if z == 1 else 0) if inner else far, 1 - y),
                ]
                for place, (a, b) in enumerate(order):
                    table[2 * z + y, 2 * a + b] = place
        return table, [1, 1, 2, 2, 1, 1, 2]
    offsets = window_offsets(devices, hops)
    table = np.zeros((devices, devices), np.int32)
    for d in range(devices):
        for place, offset in enumerate(offsets):
            table[d, (d + offset) % devices] = place
    return table, [1] * len(offsets)


def window_offsets(devices, hops):
    seen = []
    for offset in range(-hops, hops + 1):
        if offset % devices not in seen:
            seen.append(offset % devices)
    return seen


def gather_window(own, devices, hops):
    if devices == 2 * hops + 2 and devices == 8:
        def lines(pairs):
            return [(2 * a + y, 2 * b + y) for a, b in pairs for y in (0, 1)]

        outer = lines([(0, 1), (1, 0), (2, 3), (3, 2)])
        middle = lines([(1, 2), (2, 1)])
        to_ends = lines([(1, 0), (2, 3)])
        across = [(i, i ^ 1) for i in range(8)]
        across_inner = [(i, i ^ 1) for i in (2, 3, 4, 5)]
        across_ends = [(i, i ^ 1) for i in (0, 1, 6, 7)]
        q1 = permute(own, "blk", outer)
        y1 = permute(own, "blk", across)
        q2 = permute(own, "blk", middle)
        q3 = permute(q1, "blk", middle)
        y2 = permute(q1, "blk", across)
        q5 = permute(y1, "blk", middle)
        q4 = permute(q3, "blk", to_ends)
        y3a = permute(q3, "blk", across_inner)
        q6 = permute(q5, "blk", to_ends)
        y3b = permute(q4, "blk", across_ends)
        return [[own], [q1], [q2, q4], [q5, q6], [y1], [y2], [y3a, y3b]]
    pieces = []
    for offset in window_offsets(devices, hops):
        if offset == 0:
            pieces.append([own])
        else:
            pairs = [((i + offset) % devices, i) for i in range(devices)]
            pieces.append([permute(own, "blk", pairs)])
    return pieces


def apply_kernel(counts, near, groups, orders, places, ends, strips, basis, *rest):
    pieces = rest[:sum(counts)]
    image, partial, raw, window, sems = rest[sum(counts):]
    step = pl.program_id(0)
    rows, width = raw.shape[1], raw.shape[2]
    block = strips.shape[2]

    @pl.when(step == 0)
    def _():
        at = 0
        for place, count in enumerate(counts):
            if count == 1:
                pltpu.make_async_copy(pieces[at], raw.at[place], sems.at[place]).start()
            else:
                @pl.when(ends[0] == 0)
                def _(at=at, place=place):
                    pltpu.make_async_copy(pieces[at], raw.at[place], sems.at[place]).start()

                @pl.when(ends[0] == 1)
                def _(at=at, place=place):
                    pltpu.make_async_copy(pieces[at + 1], raw.at[place], sems.at[place]).start()
            at += count
        for place in range(len(counts)):
            pltpu.make_async_copy(pieces[0], raw.at[place], sems.at[place]).wait()

            def one(i, carry, place=place):
                high, low = split(raw[place, aligned(i, block), :])
                base = (place * (rows // block) + i) * 2
                window[aligned(base, block), :] = high
                window[aligned(base + 1, block), :] = low
                return carry

            lax.fori_loop(0, rows // block, one, 0)
        partial[...] = jnp.zeros_like(partial)

    total = jnp.zeros((2 * block, width), F32)
    for k in range(near):
        high, low = split(strips[0, k])
        left = jnp.concatenate(
            [jnp.concatenate([high, high], 1), jnp.concatenate([low, low], 1)], 0)
        right = window[aligned(places[step, k], 2 * block), :]
        total = total + jnp.dot(left, right, preferred_element_type=F32)
    result = total[:block] + total[block:]
    image[...] = result
    for g in range(groups):
        cols = slice(g * GROUP, (g + 1) * GROUP)
        wide = jnp.concatenate([basis[m, :, cols] for m in range(orders)], 1)
        partial[g] += dot3(result[:, cols], wide, ((0,), (0,)))


def apply(places, ends, strips, basis_rows, pieces, c0, width):
    row_blocks, near, block, _ = strips.shape
    orders = basis_rows.shape[0]
    groups = width // GROUP
    counts = [len(p) for p in pieces]
    flat = [x for p in pieces for x in p]
    rows = flat[0].shape[0]
    column = c0 // width
    return pl.pallas_call(
        functools.partial(apply_kernel, counts, near, groups, orders),
        grid=(row_blocks,),
        out_shape=[
            jax.ShapeDtypeStruct((rows, width), F32),
            jax.ShapeDtypeStruct((groups, GROUP, orders * GROUP), F32),
        ],
        in_specs=[
            SMEM, SMEM,
            pl.BlockSpec((1, near, block, block), lambda i: (i, 0, 0, 0)),
            pl.BlockSpec((orders, block, width), lambda i: (0, i, column)),
        ] + [ANY] * len(flat),
        out_specs=[
            pl.BlockSpec((block, width), lambda i: (i, 0)),
            pl.BlockSpec((groups, GROUP, orders * GROUP), lambda i: (0, 0, 0)),
        ],
        scratch_shapes=[
            pltpu.VMEM((len(counts), rows, width), F32),
            pltpu.VMEM((len(counts) * rows * 2, width), BF16),
            pltpu.SemaphoreType.DMA((len(counts),)),
        ],
        compiler_params=params(),
        cost_estimate=pl.CostEstimate(
            flops=8 * row_blocks * near * block * block * width,
            bytes_accessed=strips.size * 4 + len(counts) * rows * width * 4, transcendentals=0),
        name="apply",
    )(places, ends, strips, basis_rows, *flat)


def project_kernel(groups, orders, image, basis, coeffs_t, residual, gram, coeffs):
    @pl.when(pl.program_id(0) == 0)
    def _():
        gram[...] = jnp.zeros_like(gram)
        for g in range(groups):
            for m in range(orders):
                coeffs[m, g] = coeffs_t[g, :, m * GROUP:(m + 1) * GROUP].T

    for g in range(groups):
        cols = slice(g * GROUP, (g + 1) * GROUP)
        wide = jnp.concatenate([basis[m, :, cols] for m in range(orders)], 1)
        left = image[:, cols] - dot3(wide, coeffs_t[g], ((1,), (1,)))
        residual[:, cols] = left
        gram[g] += dot3(left, left, ((0,), (0,)))


def project(image, basis_rows, coeffs_t, c0, width):
    orders = basis_rows.shape[0]
    groups = width // GROUP
    rows = image.shape[0]
    tile = 256
    column = c0 // width
    return pl.pallas_call(
        functools.partial(project_kernel, groups, orders),
        grid=(rows // tile,),
        out_shape=[
            jax.ShapeDtypeStruct((rows, width), F32),
            jax.ShapeDtypeStruct((groups, GROUP, GROUP), F32),
            jax.ShapeDtypeStruct((orders, groups, GROUP, GROUP), F32),
        ],
        in_specs=[
            pl.BlockSpec((tile, width), lambda i: (i, 0)),
            pl.BlockSpec((orders, tile, width), lambda i: (0, i, column)),
            pl.BlockSpec(coeffs_t.shape, lambda i: (0, 0, 0)),
        ],
        out_specs=[
            pl.BlockSpec((tile, width), lambda i: (i, 0)),
            pl.BlockSpec((groups, GROUP, GROUP), lambda i: (0, 0, 0)),
            pl.BlockSpec((orders, groups, GROUP, GROUP), lambda i: (0, 0, 0, 0)),
        ],
        compiler_params=params(),
        cost_estimate=pl.CostEstimate(
            flops=30 * rows * width * GROUP, bytes_accessed=6 * rows * width * 4,
            transcendentals=0),
        name="project",
    )(image, basis_rows, coeffs_t)


def eliminate(gram):
    count = len(gram)
    order = gram[0].shape[0]
    row_at = lax.broadcasted_iota(jnp.int32, (order, order), 0)
    col_at = lax.broadcasted_iota(jnp.int32, (order, order), 1)
    eye = jnp.where(row_at == col_at, 1.0, 0.0).astype(F32)
    rest = [jnp.concatenate([g, eye], 1) for g in gram]
    done = [[] for _ in gram]
    panel_row = lax.broadcasted_iota(jnp.int32, (PANEL, 1), 0)
    for p0 in range(0, order, PANEL):
        panels = [r[:PANEL] for r in rest]
        for j in range(PANEL):
            for n in range(count):
                panel = panels[n]
                column = panel[:, p0 + j:p0 + j + 1]
                pivot = column[j:j + 1]
                factor = jnp.where(panel_row > j, column / pivot, 0.0)
                panels[n] = panel - factor * panel[j:j + 1]
        for n in range(count):
            panel = panels[n]
            own = slice(p0, p0 + PANEL)
            diagonal = jnp.sum(jnp.where(
                lax.broadcasted_iota(jnp.int32, (PANEL, PANEL), 0)
                == lax.broadcasted_iota(jnp.int32, (PANEL, PANEL), 1),
                panel[:, own], 0.0), axis=1, keepdims=True)
            panel = panel * lax.rsqrt(diagonal)
            done[n].append(panel)
            if p0 + PANEL < order:
                below = panel[:, p0 + PANEL:order]
                rest[n] = rest[n][PANEL:] - lax.dot_general(
                    below, panel, (((0,), (0,)), ((), ())),
                    precision=lax.Precision.HIGHEST, preferred_element_type=F32)
    lowers, inverses = [], []
    for n in range(count):
        upper = jnp.concatenate(done[n], 0)
        lowers.append(jnp.where(row_at >= col_at, upper[:, :order].T, 0.0))
        inverses.append(upper[:, order:])
    return lowers, inverses


def finish_kernel(groups, parts, me, gram, residual, *outs):
    lowers, inverses = eliminate([gram[g] for g in range(groups)])
    rows = residual.shape[0] // parts
    for k in range(parts):
        for g in range(groups):
            cols = slice(g * GROUP, (g + 1) * GROUP)
            left = residual[aligned(me[0] ^ k, rows), cols]
            outs[k][:rows, cols] = dot3(left, inverses[g], ((1,), (1,)))
            outs[k][rows:, cols] = lowers[g]


def finish(me, gram, residual, parts):
    groups = gram.shape[0]
    rows, width = residual.shape
    shape = jax.ShapeDtypeStruct((rows // parts + GROUP, width), F32)
    return pl.pallas_call(
        functools.partial(finish_kernel, groups, parts),
        out_shape=[shape] * parts,
        in_specs=[SMEM, VMEM, VMEM],
        out_specs=[VMEM] * parts,
        compiler_params=params(),
        cost_estimate=pl.CostEstimate(
            flops=6 * rows * width * GROUP, bytes_accessed=4 * rows * width * 4,
            transcendentals=0),
        name="finish",
    )(me, gram, residual)


def collect(me, blocks, coeffs, chunks, shapes, parts):
    new_shape, coeffs_shape, factor_shape = shapes
    rows = new_shape[0]
    step = new_shape[1] // parts
    count = len(chunks)
    per_part = step // GROUP

    def kernel(me_ref, *rest):
        new_in, coeffs_in = rest[:count * parts], rest[count * parts:2 * count * parts]
        new_out, coeffs_out, factor_out, sems = rest[2 * count * parts:]
        copies = []
        for c, (g0, groups) in enumerate(chunks):
            for k in range(parts):
                src = new_in[c * parts + k]
                at = me_ref[0] ^ k
                start = pl.multiple_of(at * step + g0 * GROUP, GROUP)
                copies.append((src.at[pl.ds(0, rows), :],
                               new_out.at[:, pl.ds(start, groups * GROUP)]))
                copies.append((coeffs_in[c * parts + k],
                               coeffs_out.at[:, pl.ds(at * per_part + g0, groups)]))
                for g in range(groups):
                    copies.append((src.at[pl.ds(rows, GROUP), pl.ds(g * GROUP, GROUP)],
                                   factor_out.at[at * per_part + g0 + g]))
        run_copies(copies, sems)

    total = sum(parts * (2 + groups) for _, groups in chunks)
    return pl.pallas_call(
        kernel,
        out_shape=[jax.ShapeDtypeStruct(s, F32) for s in shapes],
        in_specs=[SMEM] + [ANY] * (2 * count * parts),
        out_specs=[ANY] * 3,
        scratch_shapes=[pltpu.SemaphoreType.DMA((total,))],
        compiler_params=params(),
        name="collect",
    )(me, *[x for c in blocks for x in c], *[x for c in coeffs for x in c])


def sum_blk(value):
    k = 1
    while k < lax.axis_size("blk"):
        value = value + swap(value, "blk", k)
        k *= 2
    return value


def plan_chunks(groups):
    chunks, at = [], 0
    for size in CHUNKS if sum(CHUNKS) == groups else (1,) * groups:
        chunks.append((at, size))
        at += size
    return chunks


def local(strips, near_cols, vector_block, basis):
    local_blocks = strips.shape[0]
    devices = lax.axis_size("blk")
    parts = lax.axis_size("rhs")
    hops = -(-BAND // local_blocks)
    rows, total = vector_block.shape
    step = total // parts
    groups = step // GROUP
    orders = basis.shape[0]
    chunks = plan_chunks(groups)
    me = lax.axis_index("rhs").astype(jnp.int32).reshape(1)
    blk = lax.axis_index("blk")

    table, _ = plan_window(devices, hops)
    row = jnp.asarray(table)[blk]
    places = row[near_cols // local_blocks] * local_blocks + near_cols % local_blocks
    ends = jnp.where((blk < 2) | (blk >= devices - 2), 1, 0).astype(jnp.int32).reshape(1)

    def row_form(value, c0, widths, after=()):
        sent = cut_columns(value, me, c0, sum(widths), parts, after)
        got = [swap(s, "rhs", k + 1) for k, s in enumerate(sent)]
        return join_rows(value, got, me, c0, widths, parts)

    first = chunks[0][1] * GROUP
    own = row_form(vector_block, 0, [first])
    if len(chunks) > 1:
        own = own + row_form(vector_block, first, [n * GROUP for _, n in chunks[1:]])
    basis_rows, = row_form(basis, 0, [step], after=(own[-1],))

    blocks, all_coeffs = [], []
    for (g0, count), mine in zip(chunks, own):
        width = count * GROUP
        pieces = gather_window(mine, devices, hops)
        image, partial = apply(places, ends, strips, basis_rows, pieces, g0 * GROUP, width)
        coeffs_t = sum_blk(partial)
        residual, gram, coeffs = project(image, basis_rows, coeffs_t, g0 * GROUP, width)
        gram = sum_blk(gram)
        all_coeffs.append([coeffs] + [swap(coeffs, "rhs", k) for k in range(1, parts)])
        out = finish(me, gram, residual, parts)
        blocks.append([out[0]] + [swap(out[k], "rhs", k) for k in range(1, parts)])

    shapes = [(rows, total), (orders, total // GROUP, GROUP, GROUP), (total // GROUP, GROUP, GROUP)]
    return tuple(collect(me, blocks, all_coeffs, chunks, shapes, parts))


def solution(mesh):
    placed = (
        P("blk", None, None, None),
        P("blk", None),
        P(("blk", "rhs"), None),
        P(None, ("blk", "rhs"), None),
    )
    return jax.shard_map(
        local,
        mesh=mesh,
        in_specs=placed,
        out_specs=(P(("blk", "rhs"), None), P(), P()),
        check_vma=False,
    )
```

time: 1080 us -> 824 us (0.76)
  Pallas kernels: 0 us -> 524 us
  other arithmetic: 350 us -> 0.62 us
  waiting for transfers between devices: 518 us -> 170 us
  starting transfers between devices: 8.81 us -> 120 us
  matrix products: 65.1 us -> 0 us
  blocking collectives: 60.3 us -> 0 us
  local copies, waits for them, and re-layouts: 62 us -> 6.86 us
  between operations: 14.2 us -> 1.76 us
    pallas_call x0 -> x16, Pallas kernels: none -> 524 us  [the longest x3 192 us: join_rows(): pl.pallas_call(kernel, out_shape=[jax.ShapeDtypeStruct(lead + (rows * par...]
    another operation x7 -> x0, other arithmetic: 348 us -> none  [the longest x4 189 us: local(): factor = jnp.linalg.cholesky(gram)]
    psum x2 -> x0, waiting for transfers between devices: 315 us -> none  [the longest x1 190 us: local(): coeffs = lax.psum(partial_value, ('blk', 'rhs'))]
    ppermute x6 -> x75, starting transfers between devices: 8.51 us -> 120 us  [permute(): return lax.ppermute(value, axis, pairs)]
    dot_general x4 -> x0, matrix products: 61.8 us -> none  [the longest x1 33.5 us: apply_strips(): result = jnp.einsum('ikab,ikbc->iac', strips, chosen, precision=HIGHEST)]
    all_to_all x2 -> x0, blocking collectives: 60.3 us -> none  [the longest x1 31.5 us: local(): lax.all_to_all(image, 'rhs', split_axis=0, concat_axis=1, tiled=True)]
    ppermute x6 -> x75, waiting for transfers between devices: 204 us -> 170 us  [permute(): return lax.ppermute(value, axis, pairs)]
    unnamed x15 -> x62, local copies, waits for them, and re-layouts: 28.7 us -> 4.15 us
  transfers between devices with their start and end apart: 8 -> 75, of which waited for: 4 -> 20; matrix products, arithmetic and copies ran while one was open for 2% -> 0% of each run, Pallas kernels for 0% -> 51%
where the time goes in v1:
time: 824 us; the launch traced here: 823 us
  Pallas kernels  524 us (64%)
  waiting for transfers between devices  170 us (21%)
  starting transfers between devices  120 us (15%)
    pallas_call x3, Pallas kernels, join_rows(): pl.pallas_call(kernel, out_shape=[jax.ShapeDtypeStruct(lead + (rows * par...  192 us
    ppermute x75, waiting for transfers between devices, permute(): return lax.ppermute(value, axis, pairs)  170 us
    pallas_call x3, Pallas kernels, cut_columns(): pl.pallas_call(kernel, out_shape=[jax.ShapeDtypeStruct(lead + (width,), v...  128 us
    ppermute x75, starting transfers between devices, permute(): return lax.ppermute(value, axis, pairs)  120 us
    pallas_call x1, Pallas kernels, collect(): pl.pallas_call(kernel, out_shape=[jax.ShapeDtypeStruct(s, F32) for s in s...  101 us
    pallas_call x3, Pallas kernels, apply(): pl.pallas_call(functools.partial(apply_kernel, counts, near, groups, orde...  50 us
    pallas_call x3, Pallas kernels, finish(): pl.pallas_call(functools.partial(finish_kernel, groups, parts), out_shape...  36.5 us
    pallas_call x3, Pallas kernels, project(): pl.pallas_call(functools.partial(project_kernel, groups, orders), grid=(r...  16.5 us
  transfers between devices with their start and end apart: 75, of which 20 were waited for; matrix products, arithmetic and copies ran while one was open for 0% of the time, Pallas kernels for 51%

profile of v1, /device:TPU:1, one launch (start us, length us, event | category | flops | bytes accessed | tf_op | source)
XLA Modules:
  0.0 822.8 jit_solution(13159153144623396147)
XLA Ops:
  0.6 1.6 copy-done
  2.5 2.7 collective-permute-start.1
  7.5 4.2 collective-permute-done.1.rest_1_
  11.7 5.8 collective-permute-done.2.rest_2_
  17.8 1.8 collective-permute-start.28
  20.3 2.7 collective-permute-done.7.rest_1_
  22.9 5.9 collective-permute-done.8.rest_2_
  29.0 1.6 collective-permute-start.9
  32.6 3.8 collective-permute-start.47
  36.6 128.2 %cut_columns.4 = (f32[4,256,512]{2,1,0:T(8,128)S(1)}, f32[4,256,512]{2,1,0:T(8,128)}, f32[4,256,512]{2,1,0:T(8,128)}) custom-call(s32[1]{0:T(128)} %bitcast.me_ref.me, f32[4,256,2048]{2,1,0:T(8,128)} %src.9, f32[1024,128]{1,0:T(8,128)S(1)} %get-tuple-element.44.rest_0_), custom_call_target="tpu_custom_call" | custom-call | tf_op jit(solution)/shard_map/cut_columns/pallas_call | solution.py:76
  166.2 1.6 collective-permute-start.3
  169.0 1.6 collective-permute-start.11
  171.2 17.2 %collective-permute-done.13.rest_6_ = f32[1024,256]{1,0:T(8,128)S(1)} collective-permute-done((f32[1024,256]{1,0:T(8,128)S(1)}, f32[1024,256]{1,0:T(8,128)S(1)}, u32[]{:S(2)}, u32[]{:S(2)}) %collective-permute-start.13) | collective-permute-done | bytes 1048608 | tf_op jit(solution)/shard_map/ppermute | solution.py:29
  188.4 1.6 collective-permute-start.14
  193.9 21.4 %collective-permute-done.4.rest_1_ = f32[4,256,512]{2,1,0:T(8,128)} collective-permute-done((f32[4,256,512]{2,1,0:T(8,128)}, f32[4,256,512]{2,1,0:T(8,128)}, u32[]{:S(2)}, u32[]{:S(2)}) %collective-permute-start.4) | collective-permute-done | bytes 2097184 | tf_op jit(solution)/shard_map/ppermute | solution.py:29
  215.3 1.6 collective-permute-start.17
  218.5 3.0 collective-permute-start.18
  221.7 38.8 %collective-permute-done.5.rest_2_ = f32[4,256,512]{2,1,0:T(8,128)} collective-permute-done((f32[4,256,512]{2,1,0:T(8,128)}, f32[4,256,512]{2,1,0:T(8,128)}, u32[]{:S(2)}, u32[]{:S(2)}) %collective-permute-start.5) | collective-permute-done | bytes 2097184 | tf_op jit(solution)/shard_map/ppermute | solution.py:29
  262.6 1.9 gather_fusion
  264.6 191.7 %join_rows.4.basis = f32[4,1024,512]{2,1,0:T(8,128)} custom-call(s32[1]{0:T(128)} %bitcast.me_ref.me, f32[4,256,2048]{2,1,0:T(8,128)} %src.9, f32[4,256,512]{2,1,0:T(8,128)S(1)} %collective-permute-done.3.rest_0_, f32[4,256,512]{2,1,0:T(8,128)} %collective-permute-done.4.rest_1_, f32[4,256,512]{2,1,0:T(8,128)} %collective-permute-done.5.rest_2_), custom_call_target="tpu_custom_call" | custom-call | tf_op jit(solution)/shard_map/join_rows/pallas_call | solution.py:107
  460.1 19.5 %apply.3 = (f32[1024,256]{1,0:T(8,128)S(1)}, f32[2,128,512]{2,1,0:T(8,128)S(1)}) custom-call(s32[8,25]{1,0:T(8,128)S(1)} %fusion.places, s32[1]{0:T(128)} %bitcast.2.ends, f32[8,25,128,128]{3,2,1,0:T(8,128)} %strips.5, f32[4,1024,512]{2,1,0:T(8,128)} %join_rows.4.basis, f32[1024,256]{1,0:T(8,128)S(1)} %join_rows.5.rest_0_, ...), custom_call_target="tpu_custom_call" | custom-call | flops 6710886400 | bytes 20447232 | tf_op jit(solution)/shard_map/apply/pallas_call | solution.py:239
  483.0 3.2 collective-permute-start.37
  486.5 12.8 %collective-permute-done.34.rest_5_ = f32[1024,128]{1,0:T(8,128)S(1)} collective-permute-done((f32[1024,128]{1,0:T(8,128)S(1)}, f32[1024,128]{1,0:T(8,128)S(1)}, u32[]{:S(2)}, u32[]{:S(2)}) %collective-permute-start.34) | collective-permute-done | bytes 524320 | tf_op jit(solution)/shard_map/ppermute | solution.py:29
  500.5 10.1 %collective-permute-done.50.rest_3_ = f32[1024,128]{1,0:T(8,128)S(1)} collective-permute-done((f32[1024,128]{1,0:T(8,128)S(1)}, f32[1024,128]{1,0:T(8,128)S(1)}, u32[]{:S(2)}, u32[]{:S(2)}) %collective-permute-start.50) | collective-permute-done | bytes 524320 | tf_op jit(solution)/shard_map/ppermute | solution.py:29
  512.6 2.4 collective-permute-start.56
  515.1 15.2 %apply.4 = (f32[1024,128]{1,0:T(8,128)S(1)}, f32[1,128,512]{2,1,0:T(8,128)S(1)}) custom-call(s32[8,25]{1,0:T(8,128)S(1)} %fusion.places, s32[1]{0:T(128)} %bitcast.2.ends, f32[8,25,128,128]{3,2,1,0:T(8,128)} %strips.5, f32[4,1024,512]{2,1,0:T(8,128)} %join_rows.4.basis, f32[1024,128]{1,0:T(8,128)S(1)} %copy-done.4, f32[1024,128]{1,0:T(8,128)S(1)} %copy-done.6, ...), custom_call_target="tpu_custom_call" | custom-call | flops 3355443200 | bytes 16777216 | tf_op jit(solution)/shard_map/apply/pallas_call | solution.py:239
  533.4 15.2 %apply.5 = (f32[1024,128]{1,0:T(8,128)S(1)}, f32[1,128,512]{2,1,0:T(8,128)S(1)}) custom-call(s32[8,25]{1,0:T(8,128)S(1)} %fusion.places, s32[1]{0:T(128)} %bitcast.2.ends, f32[8,25,128,128]{3,2,1,0:T(8,128)} %strips.5, f32[4,1024,512]{2,1,0:T(8,128)} %join_rows.4.basis, f32[1024,128]{1,0:T(8,128)S(1)} %copy-done.2, f32[1024,128]{1,0:T(8,128)S(1)} %copy-done.8, ...), custom_call_target="tpu_custom_call" | custom-call | flops 3355443200 | bytes 16777216 | tf_op jit(solution)/shard_map/apply/pallas_call | solution.py:239
  549.4 4.3 collective-permute-start.39
  553.9 4.7 collective-permute-start.58
  561.2 11.4 %collective-permute-done.58 = f32[1,128,512]{2,1,0:T(8,128)S(1)} collective-permute-done((f32[1,128,512]{2,1,0:T(8,128)S(1)}, f32[1,128,512]{2,1,0:T(8,128)S(1)}, u32[]{:S(2)}, u32[]{:S(2)}) %collective-permute-start.58) | collective-permute-done | bytes 262176 | tf_op jit(solution)/shard_map/ppermute | solution.py:29
  572.8 4.4 project.4
  577.3 26.4 %collective-permute-start.69 = (f32[4,1,128,128]{3,2,1,0:T(8,128)S(1)}, f32[4,1,128,128]{3,2,1,0:T(8,128)S(1)}, u32[]{:S(2)}, u32[]{:S(2)}) collective-permute-start(f32[4,1,128,128]{3,2,1,0:T(8,128)S(1)} %get-tuple-element.77.rest_16_), channel_id=1, source_target_pairs={{0,1},{1,0},{2,3},{3,2},{4,5},{5,4},{6,7},{7,6},{8,9},{9,8},{10,11... | collective-permute-start | bytes 786440 | tf_op jit(solution)/shard_map/ppermute | solution.py:29
  604.1 4.4 project.5
  614.9 1.8 collective-permute-start.62
  616.7 6.5 collective-permute-start.71
  623.3 2.0 collective-permute-start.72
  625.3 2.9 collective-permute-start.74
  628.2 7.6 project.3
  636.7 3.9 collective-permute-done.22
  641.8 12.1 %finish.4 = (f32[384,128]{1,0:T(8,128)S(1)}, f32[384,128]{1,0:T(8,128)S(1)}, f32[384,128]{1,0:T(8,128)S(1)}, f32[384,128]{1,0:T(8,128)S(1)}) custom-call(s32[1]{0:T(128)} %bitcast.me_ref.me, f32[1,128,128]{2,1,0:T(8,128)S(1)} %add.85.gram, f32[1024,128]{1,0:T(8,128)S(1)} %get-tuple-element.63.residual), custom_call_target="tpu_custom_call" | custom-call | flops 100663296 | bytes 2097152 | tf_op jit(solution)/shard_map/finish/pallas_call | solution.py:371
  656.9 12.1 %finish.5 = (f32[384,128]{1,0:T(8,128)S(1)}, f32[384,128]{1,0:T(8,128)S(1)}, f32[384,128]{1,0:T(8,128)S(1)}, f32[384,128]{1,0:T(8,128)S(1)}) custom-call(s32[1]{0:T(128)} %bitcast.me_ref.me, f32[1,128,128]{2,1,0:T(8,128)S(1)} %add.91.gram, f32[1024,128]{1,0:T(8,128)S(1)} %get-tuple-element.71.residual), custom_call_target="tpu_custom_call" | custom-call | flops 100663296 | bytes 2097152 | tf_op jit(solution)/shard_map/finish/pallas_call | solution.py:371
  669.2 1.7 collective-permute-start.24
  674.3 3.8 collective-permute-done.24
  679.6 12.4 %finish.3 = (f32[384,256]{1,0:T(8,128)S(1)}, f32[384,256]{1,0:T(8,128)S(1)}, f32[384,256]{1,0:T(8,128)S(1)}, f32[384,256]{1,0:T(8,128)S(1)}) custom-call(s32[1]{0:T(128)} %bitcast.me_ref.me, f32[2,128,128]{2,1,0:T(8,128)S(1)} %add.79.gram, f32[1024,256]{1,0:T(8,128)S(1)} %get-tuple-element.54.residual), custom_call_target="tpu_custom_call" | custom-call | flops 201326592 | bytes 4194304 | tf_op jit(solution)/shard_map/finish/pallas_call | solution.py:371
  694.2 11.2 %collective-permute-done.68.rest_15_ = f32[4,2,128,128]{3,2,1,0:T(8,128)S(1)} collective-permute-done((f32[4,2,128,128]{3,2,1,0:T(8,128)S(1)}, f32[4,2,128,128]{3,2,1,0:T(8,128)S(1)}, u32[]{:S(2)}, u32[]{:S(2)}) %collective-permute-start.68) | collective-permute-done | bytes 524320 | tf_op jit(solution)/shard_map/ppermute | solution.py:29
  705.4 6.3 collective-permute-done.26.rest_2_
  711.7 9.4 %collective-permute-done.27.rest_3_ = f32[384,256]{1,0:T(8,128)S(1)} collective-permute-done((f32[384,256]{1,0:T(8,128)S(1)}, f32[384,256]{1,0:T(8,128)S(1)}, u32[]{:S(2)}, u32[]{:S(2)}) %collective-permute-start.27) | collective-permute-done | bytes 393248 | tf_op jit(solution)/shard_map/ppermute | solution.py:29
  721.9 100.8 %collect.1 = (f32[256,2048]{1,0:T(8,128)}, f32[4,16,128,128]{3,2,1,0:T(8,128)}, f32[16,128,128]{2,1,0:T(8,128)}) custom-call(s32[1]{0:T(128)} %bitcast.me_ref.me, f32[384,256]{1,0:T(8,128)S(1)} %get-tuple-element.55.rest_0_, f32[384,256]{1,0:T(8,128)} %copy-done.27, f32[384,256]{1,0:T(8,128)} %copy-done.28, f32[384,256]{1,0:T(8,128)} %copy-done.29, ...), custom_call_target="tpu_custom_call" | custom-call | tf_op jit(solution)/shard_map/collect/pallas_call | solution.py:410
  (206 shorter events, 53.7 us)
Async XLA Ops:
  7.2 21.7 %collective-permute-start.8 = (f32[256,256]{1,0:T(8,128)S(1)}, f32[256,256]{1,0:T(8,128)S(1)}, u32[]{:S(2)}, u32[]{:S(2)}) collective-permute-start(f32[256,256]{1,0:T(8,128)S(1)} %get-tuple-element.50), channel_id=1, source_target_pairs={{0,3},{1,2},{2,1},{3,0},{4,7},{5,6},{6,5},{7,4},{8,11},{9,10},{10,... | collective-permute-start | bytes 786440 | tf_op jit(solution)/shard_map/ppermute | solution.py:29
  29.0 140.1 %collective-permute-start.9 = (f32[1024,256]{1,0:T(8,128)S(1)}, f32[1024,256]{1,0:T(8,128)}, u32[]{:S(2)}, u32[]{:S(2)}) collective-permute-start(f32[1024,256]{1,0:T(8,128)S(1)} %join_rows.5.rest_0_), channel_id=1, source_target_pairs={{0,8},{4,12},{8,0},{12,4},{16,24},{20,28},{24,16},{28,20},{1,9},{5... | collective-permute-start | bytes 3145736 | tf_op jit(solution)/shard_map/ppermute | solution.py:29
  30.6 140.1 %collective-permute-start.10 = (f32[1024,256]{1,0:T(8,128)S(1)}, f32[1024,256]{1,0:T(8,128)S(1)}, u32[]{:S(2)}, u32[]{:S(2)}) collective-permute-start(f32[1024,256]{1,0:T(8,128)S(1)} %join_rows.5.rest_0_), channel_id=1, source_target_pairs={{8,16},{12,20},{16,8},{20,12},{9,17},{13,21},{17,9},{21,13},{10,18... | collective-permute-start | bytes 3145736 | tf_op jit(solution)/shard_map/ppermute | solution.py:29
  31.3 133.6 %collective-permute-start.32 = (f32[1024,128]{1,0:T(8,128)S(1)}, f32[1024,128]{1,0:T(8,128)S(1)}, u32[]{:S(2)}, u32[]{:S(2)}) collective-permute-start(f32[1024,128]{1,0:T(8,128)S(1)} %get-tuple-element.59.rest_0_), channel_id=1, source_target_pairs={{0,4},{4,0},{8,12},{12,8},{16,20},{20,16},{24,28},{28,24},{1,5},{5... | collective-permute-start | bytes 1572872 | tf_op jit(solution)/shard_map/ppermute | solution.py:29
  32.6 133.6 %collective-permute-start.47 = (f32[1024,128]{1,0:T(8,128)S(1)}, f32[1024,128]{1,0:T(8,128)S(1)}, u32[]{:S(2)}, u32[]{:S(2)}) collective-permute-start(f32[1024,128]{1,0:T(8,128)S(1)} %get-tuple-element.44.rest_0_), channel_id=1, source_target_pairs={{0,8},{4,12},{8,0},{12,4},{16,24},{20,28},{24,16},{28,20},{1,9},{5... | collective-permute-start | bytes 1572872 | tf_op jit(solution)/shard_map/ppermute | solution.py:29
  36.4 131.4 %collective-permute-start.51 = (f32[1024,128]{1,0:T(8,128)S(1)}, f32[1024,128]{1,0:T(8,128)S(1)}, u32[]{:S(2)}, u32[]{:S(2)}) collective-permute-start(f32[1024,128]{1,0:T(8,128)S(1)} %get-tuple-element.44.rest_0_), channel_id=1, source_target_pairs={{0,4},{4,0},{8,12},{12,8},{16,20},{20,16},{24,28},{28,24},{1,5},{5... | collective-permute-start | bytes 1572872 | tf_op jit(solution)/shard_map/ppermute | solution.py:29
  164.9 23.5 %collective-permute-start.13 = (f32[1024,256]{1,0:T(8,128)S(1)}, f32[1024,256]{1,0:T(8,128)S(1)}, u32[]{:S(2)}, u32[]{:S(2)}) collective-permute-start(f32[1024,256]{1,0:T(8,128)S(1)} %join_rows.5.rest_0_), channel_id=1, source_target_pairs={{0,4},{4,0},{8,12},{12,8},{16,20},{20,16},{24,28},{28,24},{1,5},{5... | collective-permute-start | bytes 3145736 | tf_op jit(solution)/shard_map/ppermute | solution.py:29
  166.2 25.1 %collective-permute-start.3 = (f32[4,256,512]{2,1,0:T(8,128)S(1)}, f32[4,256,512]{2,1,0:T(8,128)S(1)}, u32[]{:S(2)}, u32[]{:S(2)}) collective-permute-start(f32[4,256,512]{2,1,0:T(8,128)S(1)} %get-tuple-element.45), channel_id=1, source_target_pairs={{0,1},{1,0},{2,3},{3,2},{4,5},{5,4},{6,7},{7,6},{8,9},{9,8},{10,11... | collective-permute-start | bytes 6291464 | tf_op jit(solution)/shard_map/ppermute | solution.py:29
  167.8 47.5 %collective-permute-start.4 = (f32[4,256,512]{2,1,0:T(8,128)}, f32[4,256,512]{2,1,0:T(8,128)}, u32[]{:S(2)}, u32[]{:S(2)}) collective-permute-start(f32[4,256,512]{2,1,0:T(8,128)} %get-tuple-element.46), channel_id=1, source_target_pairs={{0,2},{1,3},{2,0},{3,1},{4,6},{5,7},{6,4},{7,5},{8,10},{9,11},{10,... | collective-permute-start | bytes 6291464 | tf_op jit(solution)/shard_map/ppermute | solution.py:29
  169.0 21.0 %collective-permute-start.11 = (f32[1024,256]{1,0:T(8,128)}, f32[1024,256]{1,0:T(8,128)}, u32[]{:S(2)}, u32[]{:S(2)}) collective-permute-start(f32[1024,256]{1,0:T(8,128)} %collective-permute-done.9.rest_1_), channel_id=1, source_target_pairs={{8,16},{12,20},{16,8},{20,12},{9,17},{13,21},{17,9},{21,13},{10,18... | collective-permute-start | bytes 3145736 | tf_op jit(solution)/shard_map/ppermute | solution.py:29
  170.7 89.8 %collective-permute-start.5 = (f32[4,256,512]{2,1,0:T(8,128)}, f32[4,256,512]{2,1,0:T(8,128)}, u32[]{:S(2)}, u32[]{:S(2)}) collective-permute-start(f32[4,256,512]{2,1,0:T(8,128)} %get-tuple-element.47), channel_id=1, source_target_pairs={{0,3},{1,2},{2,1},{3,0},{4,7},{5,6},{6,5},{7,4},{8,11},{9,10},{10,... | collective-permute-start | bytes 6291464 | tf_op jit(solution)/shard_map/ppermute | solution.py:29
  190.0 28.5 %collective-permute-start.12 = (f32[1024,256]{1,0:T(8,128)}, f32[1024,256]{1,0:T(8,128)}, u32[]{:S(2)}, u32[]{:S(2)}) collective-permute-start(f32[1024,256]{1,0:T(8,128)} %collective-permute-done.11), channel_id=1, source_target_pairs={{8,0},{12,4},{16,24},{20,28},{9,1},{13,5},{17,25},{21,29},{10,2},{... | collective-permute-start | bytes 3145736 | tf_op jit(solution)/shard_map/ppermute | solution.py:29
  191.3 265.3 %collective-permute-start.16 = (f32[1024,256]{1,0:T(8,128)}, f32[1024,256]{1,0:T(8,128)}, u32[]{:S(2)}, u32[]{:S(2)}) collective-permute-start(f32[1024,256]{1,0:T(8,128)} %collective-permute-done.9.rest_1_), channel_id=1, source_target_pairs={{0,4},{4,0},{8,12},{12,8},{16,20},{20,16},{24,28},{28,24},{1,5},{5... | collective-permute-start | bytes 3145736 | tf_op jit(solution)/shard_map/ppermute | solution.py:29
  192.6 264.7 %collective-permute-start.15 = (f32[1024,256]{1,0:T(8,128)}, f32[1024,256]{1,0:T(8,128)}, u32[]{:S(2)}, u32[]{:S(2)}) collective-permute-start(f32[1024,256]{1,0:T(8,128)} %collective-permute-done.14.rest_4_), channel_id=1, source_target_pairs={{8,0},{12,4},{16,24},{20,28},{9,1},{13,5},{17,25},{21,29},{10,2},{... | collective-permute-start | bytes 3145736 | tf_op jit(solution)/shard_map/ppermute | solution.py:29
  215.3 242.8 %collective-permute-start.17 = (f32[1024,256]{1,0:T(8,128)}, f32[1024,256]{1,0:T(8,128)}, u32[]{:S(2)}, u32[]{:S(2)}) collective-permute-start(f32[1024,256]{1,0:T(8,128)} %collective-permute-done.11), channel_id=1, source_target_pairs={{8,12},{12,8},{16,20},{20,16},{9,13},{13,9},{17,21},{21,17},{10,14... | collective-permute-start | bytes 3145736 | tf_op jit(solution)/shard_map/ppermute | solution.py:29
  218.5 240.3 %collective-permute-start.18 = (f32[1024,256]{1,0:T(8,128)}, f32[1024,256]{1,0:T(8,128)}, u32[]{:S(2)}, u32[]{:S(2)}) collective-permute-start(f32[1024,256]{1,0:T(8,128)} %collective-permute-done.12.rest_3_), channel_id=1, source_target_pairs={{0,4},{4,0},{24,28},{28,24},{1,5},{5,1},{25,29},{29,25},{2,6},{6,2... | collective-permute-start | bytes 3145736 | tf_op jit(solution)/shard_map/ppermute | solution.py:29
  260.4 195.9 %collective-permute-start.30 = (f32[1024,128]{1,0:T(8,128)}, f32[1024,128]{1,0:T(8,128)}, u32[]{:S(2)}, u32[]{:S(2)}) collective-permute-start(f32[1024,128]{1,0:T(8,128)} %copy-done.5), channel_id=1, source_target_pairs={{8,16},{12,20},{16,8},{20,12},{9,17},{13,21},{17,9},{21,13},{10,18... | collective-permute-start | bytes 1572872 | tf_op jit(solution)/shard_map/ppermute | solution.py:29
  456.4 24.6 %collective-permute-start.35 = (f32[1024,128]{1,0:T(8,128)S(1)}, f32[1024,128]{1,0:T(8,128)S(1)}, u32[]{:S(2)}, u32[]{:S(2)}) collective-permute-start(f32[1024,128]{1,0:T(8,128)S(1)} %copy-done.6), channel_id=1, source_target_pairs={{0,4},{4,0},{8,12},{12,8},{16,20},{20,16},{24,28},{28,24},{1,5},{5... | collective-permute-start | bytes 1572872 | tf_op jit(solution)/shard_map/ppermute | solution.py:29
  456.7 23.0 %collective-permute-start.33 = (f32[1024,128]{1,0:T(8,128)S(1)}, f32[1024,128]{1,0:T(8,128)S(1)}, u32[]{:S(2)}, u32[]{:S(2)}) collective-permute-start(f32[1024,128]{1,0:T(8,128)S(1)} %copy-done.17), channel_id=1, source_target_pairs={{8,16},{12,20},{16,8},{20,12},{9,17},{13,21},{17,9},{21,13},{10,18... | collective-permute-start | bytes 1572872 | tf_op jit(solution)/shard_map/ppermute | solution.py:29
  457.4 24.3 %collective-permute-start.49 = (f32[1024,128]{1,0:T(8,128)S(1)}, f32[1024,128]{1,0:T(8,128)S(1)}, u32[]{:S(2)}, u32[]{:S(2)}) collective-permute-start(f32[1024,128]{1,0:T(8,128)S(1)} %copy-done.8), channel_id=1, source_target_pairs={{8,16},{12,20},{16,8},{20,12},{9,17},{13,21},{17,9},{21,13},{10,18... | collective-permute-start | bytes 1572872 | tf_op jit(solution)/shard_map/ppermute | solution.py:29
  458.1 28.1 %collective-permute-start.52 = (f32[1024,128]{1,0:T(8,128)S(1)}, f32[1024,128]{1,0:T(8,128)S(1)}, u32[]{:S(2)}, u32[]{:S(2)}) collective-permute-start(f32[1024,128]{1,0:T(8,128)S(1)} %copy-done.15), channel_id=1, source_target_pairs={{8,16},{12,20},{16,8},{20,12},{9,17},{13,21},{17,9},{21,13},{10,18... | collective-permute-start | bytes 1572872 | tf_op jit(solution)/shard_map/ppermute | solution.py:29
  458.8 24.2 %collective-permute-start.31 = (f32[1024,128]{1,0:T(8,128)}, f32[1024,128]{1,0:T(8,128)S(1)}, u32[]{:S(2)}, u32[]{:S(2)}) collective-permute-start(f32[1024,128]{1,0:T(8,128)} %collective-permute-done.30), channel_id=1, source_target_pairs={{8,0},{12,4},{16,24},{20,28},{9,1},{13,5},{17,25},{21,29},{10,2},{... | collective-permute-start | bytes 1572872 | tf_op jit(solution)/shard_map/ppermute | solution.py:29
  479.7 19.6 %collective-permute-start.34 = (f32[1024,128]{1,0:T(8,128)S(1)}, f32[1024,128]{1,0:T(8,128)S(1)}, u32[]{:S(2)}, u32[]{:S(2)}) collective-permute-start(f32[1024,128]{1,0:T(8,128)S(1)} %collective-permute-done.33.rest_4_), channel_id=1, source_target_pairs={{8,0},{12,4},{16,24},{20,28},{9,1},{13,5},{17,25},{21,29},{10,2},{... | collective-permute-start | bytes 1572872 | tf_op jit(solution)/shard_map/ppermute | solution.py:29
  481.0 19.0 %collective-permute-start.36 = (f32[1024,128]{1,0:T(8,128)}, f32[1024,128]{1,0:T(8,128)S(1)}, u32[]{:S(2)}, u32[]{:S(2)}) collective-permute-start(f32[1024,128]{1,0:T(8,128)} %collective-permute-done.30), channel_id=1, source_target_pairs={{8,12},{12,8},{16,20},{20,16},{9,13},{13,9},{17,21},{21,17},{10,14... | collective-permute-start | bytes 1572872 | tf_op jit(solution)/shard_map/ppermute | solution.py:29
  481.7 28.8 %collective-permute-start.50 = (f32[1024,128]{1,0:T(8,128)S(1)}, f32[1024,128]{1,0:T(8,128)S(1)}, u32[]{:S(2)}, u32[]{:S(2)}) collective-permute-start(f32[1024,128]{1,0:T(8,128)S(1)} %collective-permute-done.49), channel_id=1, source_target_pairs={{8,0},{12,4},{16,24},{20,28},{9,1},{13,5},{17,25},{21,29},{10,2},{... | collective-permute-start | bytes 1572872 | tf_op jit(solution)/shard_map/ppermute | solution.py:29
  483.0 28.2 %collective-permute-start.37 = (f32[1024,128]{1,0:T(8,128)S(1)}, f32[1024,128]{1,0:T(8,128)S(1)}, u32[]{:S(2)}, u32[]{:S(2)}) collective-permute-start(f32[1024,128]{1,0:T(8,128)S(1)} %collective-permute-done.31.rest_3_), channel_id=1, source_target_pairs={{0,4},{4,0},{24,28},{28,24},{1,5},{5,1},{25,29},{29,25},{2,6},{6,2... | collective-permute-start | bytes 1572872 | tf_op jit(solution)/shard_map/ppermute | solution.py:29
  486.2 26.4 %collective-permute-start.19 = (f32[2,128,512]{2,1,0:T(8,128)S(1)}, f32[2,128,512]{2,1,0:T(8,128)S(1)}, u32[]{:S(2)}, u32[]{:S(2)}) collective-permute-start(f32[2,128,512]{2,1,0:T(8,128)S(1)} %get-tuple-element.52), channel_id=1, source_target_pairs={{0,4},{4,0},{8,12},{12,8},{16,20},{20,16},{24,28},{28,24},{1,5},{5... | collective-permute-start | bytes 1572872 | tf_op jit(solution)/shard_map/ppermute | solution.py:29
  499.3 31.1 %collective-permute-start.48 = (f32[1024,128]{1,0:T(8,128)S(1)}, f32[1024,128]{1,0:T(8,128)S(1)}, u32[]{:S(2)}, u32[]{:S(2)}) collective-permute-start(f32[1024,128]{1,0:T(8,128)S(1)} %copy-done.2), channel_id=1, source_target_pairs={{8,16},{12,20},{16,8},{20,12},{9,17},{13,21},{17,9},{21,13},{10,18... | collective-permute-start | bytes 1572872 | tf_op jit(solution)/shard_map/ppermute | solution.py:29
  500.0 31.6 %collective-permute-start.54 = (f32[1024,128]{1,0:T(8,128)S(1)}, f32[1024,128]{1,0:T(8,128)S(1)}, u32[]{:S(2)}, u32[]{:S(2)}) collective-permute-start(f32[1024,128]{1,0:T(8,128)S(1)} %copy-done.8), channel_id=1, source_target_pairs={{0,4},{4,0},{8,12},{12,8},{16,20},{20,16},{24,28},{28,24},{1,5},{5... | collective-permute-start | bytes 1572872 | tf_op jit(solution)/shard_map/ppermute | solution.py:29
  510.6 21.1 %collective-permute-start.55 = (f32[1024,128]{1,0:T(8,128)S(1)}, f32[1024,128]{1,0:T(8,128)S(1)}, u32[]{:S(2)}, u32[]{:S(2)}) collective-permute-start(f32[1024,128]{1,0:T(8,128)S(1)} %collective-permute-done.49), channel_id=1, source_target_pairs={{8,12},{12,8},{16,20},{20,16},{9,13},{13,9},{17,21},{21,17},{10,14... | collective-permute-start | bytes 1572872 | tf_op jit(solution)/shard_map/ppermute | solution.py:29
  511.3 20.3 %collective-permute-start.53 = (f32[1024,128]{1,0:T(8,128)S(1)}, f32[1024,128]{1,0:T(8,128)S(1)}, u32[]{:S(2)}, u32[]{:S(2)}) collective-permute-start(f32[1024,128]{1,0:T(8,128)S(1)} %collective-permute-done.52.rest_4_), channel_id=1, source_target_pairs={{8,0},{12,4},{16,24},{20,28},{9,1},{13,5},{17,25},{21,29},{10,2},{... | collective-permute-start | bytes 1572872 | tf_op jit(solution)/shard_map/ppermute | solution.py:29
  512.6 19.1 %collective-permute-start.56 = (f32[1024,128]{1,0:T(8,128)S(1)}, f32[1024,128]{1,0:T(8,128)S(1)}, u32[]{:S(2)}, u32[]{:S(2)}) collective-permute-start(f32[1024,128]{1,0:T(8,128)S(1)} %collective-permute-done.50.rest_3_), channel_id=1, source_target_pairs={{0,4},{4,0},{24,28},{28,24},{1,5},{5,1},{25,29},{29,25},{2,6},{6,2... | collective-permute-start | bytes 1572872 | tf_op jit(solution)/shard_map/ppermute | solution.py:29
  531.6 28.5 %collective-permute-start.20 = (f32[2,128,512]{2,1,0:T(8,128)S(1)}, f32[2,128,512]{2,1,0:T(8,128)S(1)}, u32[]{:S(2)}, u32[]{:S(2)}) collective-permute-start(f32[2,128,512]{2,1,0:T(8,128)S(1)} %add.74), channel_id=1, source_target_pairs={{0,8},{4,12},{8,0},{12,4},{16,24},{20,28},{24,16},{28,20},{1,9},{5... | collective-permute-start | bytes 1572872 | tf_op jit(solution)/shard_map/ppermute | solution.py:29
  560.2 56.5 %collective-permute-start.21 = (f32[2,128,512]{2,1,0:T(8,128)S(1)}, f32[2,128,512]{2,1,0:T(8,128)S(1)}, u32[]{:S(2)}, u32[]{:S(2)}) collective-permute-start(f32[2,128,512]{2,1,0:T(8,128)S(1)} %add.75), channel_id=1, source_target_pairs={{0,16},{4,20},{8,24},{12,28},{16,0},{20,4},{24,8},{28,12},{1,17},{... | collective-permute-start | bytes 1572872 | tf_op jit(solution)/shard_map/ppermute | solution.py:29
  572.7 31.3 %collective-permute-start.59 = (f32[1,128,512]{2,1,0:T(8,128)S(1)}, f32[1,128,512]{2,1,0:T(8,128)S(1)}, u32[]{:S(2)}, u32[]{:S(2)}) collective-permute-start(f32[1,128,512]{2,1,0:T(8,128)S(1)} %add.87), channel_id=1, source_target_pairs={{0,16},{4,20},{8,24},{12,28},{16,0},{20,4},{24,8},{28,12},{1,17},{... | collective-permute-start | bytes 786440 | tf_op jit(solution)/shard_map/ppermute | solution.py:29
  577.3 48.0 %collective-permute-start.69 = (f32[4,1,128,128]{3,2,1,0:T(8,128)S(1)}, f32[4,1,128,128]{3,2,1,0:T(8,128)S(1)}, u32[]{:S(2)}, u32[]{:S(2)}) collective-permute-start(f32[4,1,128,128]{3,2,1,0:T(8,128)S(1)} %get-tuple-element.77.rest_16_), channel_id=1, source_target_pairs={{0,1},{1,0},{2,3},{3,2},{4,5},{5,4},{6,7},{7,6},{8,9},{9,8},{10,11... | collective-permute-start | bytes 786440 | tf_op jit(solution)/shard_map/ppermute | solution.py:29
  609.8 26.1 %collective-permute-start.70 = (f32[4,1,128,128]{3,2,1,0:T(8,128)S(1)}, f32[4,1,128,128]{3,2,1,0:T(8,128)S(1)}, u32[]{:S(2)}, u32[]{:S(2)}) collective-permute-start(f32[4,1,128,128]{3,2,1,0:T(8,128)S(1)} %get-tuple-element.77.rest_16_), channel_id=1, source_target_pairs={{0,2},{1,3},{2,0},{3,1},{4,6},{5,7},{6,4},{7,5},{8,10},{9,11},{10,... | collective-permute-start | bytes 786440 | tf_op jit(solution)/shard_map/ppermute | solution.py:29
  616.7 37.2 %collective-permute-start.71 = (f32[4,1,128,128]{3,2,1,0:T(8,128)S(1)}, f32[4,1,128,128]{3,2,1,0:T(8,128)S(1)}, u32[]{:S(2)}, u32[]{:S(2)}) collective-permute-start(f32[4,1,128,128]{3,2,1,0:T(8,128)S(1)} %get-tuple-element.77.rest_16_), channel_id=1, source_target_pairs={{0,3},{1,2},{2,1},{3,0},{4,7},{5,6},{6,5},{7,4},{8,11},{9,10},{10,... | collective-permute-start | bytes 786440 | tf_op jit(solution)/shard_map/ppermute | solution.py:29
  623.3 31.1 %collective-permute-start.72 = (f32[4,1,128,128]{3,2,1,0:T(8,128)S(1)}, f32[4,1,128,128]{3,2,1,0:T(8,128)S(1)}, u32[]{:S(2)}, u32[]{:S(2)}) collective-permute-start(f32[4,1,128,128]{3,2,1,0:T(8,128)S(1)} %get-tuple-element.78.rest_20_), channel_id=1, source_target_pairs={{0,1},{1,0},{2,3},{3,2},{4,5},{5,4},{6,7},{7,6},{8,9},{9,8},{10,11... | collective-permute-start | bytes 786440 | tf_op jit(solution)/shard_map/ppermute | solution.py:29
  625.2 29.9 %collective-permute-start.73 = (f32[4,1,128,128]{3,2,1,0:T(8,128)S(1)}, f32[4,1,128,128]{3,2,1,0:T(8,128)S(1)}, u32[]{:S(2)}, u32[]{:S(2)}) collective-permute-start(f32[4,1,128,128]{3,2,1,0:T(8,128)S(1)} %get-tuple-element.78.rest_20_), channel_id=1, source_target_pairs={{0,2},{1,3},{2,0},{3,1},{4,6},{5,7},{6,4},{7,5},{8,10},{9,11},{10,... | collective-permute-start | bytes 786440 | tf_op jit(solution)/shard_map/ppermute | solution.py:29
  625.3 30.7 %collective-permute-start.74 = (f32[4,1,128,128]{3,2,1,0:T(8,128)S(1)}, f32[4,1,128,128]{3,2,1,0:T(8,128)S(1)}, u32[]{:S(2)}, u32[]{:S(2)}) collective-permute-start(f32[4,1,128,128]{3,2,1,0:T(8,128)S(1)} %get-tuple-element.78.rest_20_), channel_id=1, source_target_pairs={{0,3},{1,2},{2,1},{3,0},{4,7},{5,6},{6,5},{7,4},{8,11},{9,10},{10,... | collective-permute-start | bytes 786440 | tf_op jit(solution)/shard_map/ppermute | solution.py:29
  640.6 52.2 %collective-permute-start.66 = (f32[4,2,128,128]{3,2,1,0:T(8,128)S(1)}, f32[4,2,128,128]{3,2,1,0:T(8,128)S(1)}, u32[]{:S(2)}, u32[]{:S(2)}) collective-permute-start(f32[4,2,128,128]{3,2,1,0:T(8,128)S(1)} %get-tuple-element.76.rest_12_), channel_id=1, source_target_pairs={{0,1},{1,0},{2,3},{3,2},{4,5},{5,4},{6,7},{7,6},{8,9},{9,8},{10,11... | collective-permute-start | bytes 1572872 | tf_op jit(solution)/shard_map/ppermute | solution.py:29
  670.9 21.1 %collective-permute-start.64 = (f32[384,128]{1,0:T(8,128)S(1)}, f32[384,128]{1,0:T(8,128)S(1)}, u32[]{:S(2)}, u32[]{:S(2)}) collective-permute-start(f32[384,128]{1,0:T(8,128)S(1)} %get-tuple-element.74), channel_id=1, source_target_pairs={{0,2},{1,3},{2,0},{3,1},{4,6},{5,7},{6,4},{7,5},{8,10},{9,11},{10,... | collective-permute-start | bytes 589832 | tf_op jit(solution)/shard_map/ppermute | solution.py:29
  672.0 20.1 %collective-permute-start.65 = (f32[384,128]{1,0:T(8,128)S(1)}, f32[384,128]{1,0:T(8,128)S(1)}, u32[]{:S(2)}, u32[]{:S(2)}) collective-permute-start(f32[384,128]{1,0:T(8,128)S(1)} %get-tuple-element.75), channel_id=1, source_target_pairs={{0,3},{1,2},{2,1},{3,0},{4,7},{5,6},{6,5},{7,4},{8,11},{9,10},{10,... | collective-permute-start | bytes 589832 | tf_op jit(solution)/shard_map/ppermute | solution.py:29
  673.3 20.9 %collective-permute-start.67 = (f32[4,2,128,128]{3,2,1,0:T(8,128)S(1)}, f32[4,2,128,128]{3,2,1,0:T(8,128)S(1)}, u32[]{:S(2)}, u32[]{:S(2)}) collective-permute-start(f32[4,2,128,128]{3,2,1,0:T(8,128)S(1)} %get-tuple-element.76.rest_12_), channel_id=1, source_target_pairs={{0,2},{1,3},{2,0},{3,1},{4,6},{5,7},{6,4},{7,5},{8,10},{9,11},{10,... | collective-permute-start | bytes 1572872 | tf_op jit(solution)/shard_map/ppermute | solution.py:29
  678.1 27.4 %collective-permute-start.68 = (f32[4,2,128,128]{3,2,1,0:T(8,128)S(1)}, f32[4,2,128,128]{3,2,1,0:T(8,128)S(1)}, u32[]{:S(2)}, u32[]{:S(2)}) collective-permute-start(f32[4,2,128,128]{3,2,1,0:T(8,128)S(1)} %get-tuple-element.76.rest_12_), channel_id=1, source_target_pairs={{0,3},{1,2},{2,1},{3,0},{4,7},{5,6},{6,5},{7,4},{8,11},{9,10},{10,... | collective-permute-start | bytes 1572872 | tf_op jit(solution)/shard_map/ppermute | solution.py:29
  692.1 19.6 %collective-permute-start.26 = (f32[384,256]{1,0:T(8,128)S(1)}, f32[384,256]{1,0:T(8,128)S(1)}, u32[]{:S(2)}, u32[]{:S(2)}) collective-permute-start(f32[384,256]{1,0:T(8,128)S(1)} %get-tuple-element.57), channel_id=1, source_target_pairs={{0,2},{1,3},{2,0},{3,1},{4,6},{5,7},{6,4},{7,5},{8,10},{9,11},{10,... | collective-permute-start | bytes 1179656 | tf_op jit(solution)/shard_map/ppermute | solution.py:29
  692.8 28.2 %collective-permute-start.27 = (f32[384,256]{1,0:T(8,128)S(1)}, f32[384,256]{1,0:T(8,128)S(1)}, u32[]{:S(2)}, u32[]{:S(2)}) collective-permute-start(f32[384,256]{1,0:T(8,128)S(1)} %get-tuple-element.58), channel_id=1, source_target_pairs={{0,3},{1,2},{2,1},{3,0},{4,7},{5,6},{6,5},{7,4},{8,11},{9,10},{10,... | collective-permute-start | bytes 1179656 | tf_op jit(solution)/shard_map/ppermute | solution.py:29
  (58 other events, 2320.2 us)

commit v2 on v0

v2 whole, which is shorter than its diff:
```python
import functools

import jax
import jax.numpy as jnp
import numpy as np
from jax import lax
from jax.experimental import pallas as pl
from jax.experimental.pallas import tpu as pltpu
from jax.sharding import PartitionSpec as P

GROUP = 128
BAND = 24
PANEL = 32
HALVED = 128

F32 = jnp.float32
BF16 = jnp.bfloat16
ANY = pl.BlockSpec(memory_space=pl.ANY)
SMEM = pl.BlockSpec(memory_space=pltpu.SMEM)
VMEM = pl.BlockSpec(memory_space=pltpu.VMEM)
LIMIT = 50 * 1024 * 1024


def params(**kw):
    return pltpu.CompilerParams(vmem_limit_bytes=LIMIT, **kw)


def pairs_of(axis, k):
    return [(i, i ^ k) for i in range(lax.axis_size(axis))]


def swap(value, axis, k):
    return lax.ppermute(value, axis, pairs_of(axis, k))


def split(value):
    high = value.astype(BF16)
    return high, (value - high.astype(F32)).astype(BF16)


def dot3(a, b, dims):
    a_high, a_low = split(a)
    b_high, b_low = split(b)

    def one(x, y):
        return lax.dot_general(x, y, (dims, ((), ())), preferred_element_type=F32)

    return one(a_high, b_high) + (one(a_high, b_low) + one(a_low, b_high))


def aligned(index, step):
    return pl.ds(pl.multiple_of(index * step, step), step)


def column_spec(value, layer, parts, k):
    rows, step = value.shape[1], value.shape[2] // parts
    return pl.BlockSpec((1, rows, step), lambda i, me: (layer + i, 0, me[0] ^ k))


def layer_spec(rows, width):
    return pl.BlockSpec((1, rows, width), lambda i, me: (i, 0, 0))


def cut_columns(value, layer, layers, me, ks, c0, width, parts, after=()):
    rows = value.shape[1]

    def kernel(me_ref, *refs):
        for src, dst in zip(refs, refs[-len(ks):]):
            dst[...] = src[:, :, c0:c0 + width]

    return pl.pallas_call(
        kernel,
        grid_spec=pltpu.PrefetchScalarGridSpec(
            num_scalar_prefetch=1,
            grid=(layers,),
            in_specs=[column_spec(value, layer, parts, k) for k in ks] + [ANY] * len(after),
            out_specs=[layer_spec(rows, width)] * len(ks),
        ),
        out_shape=[jax.ShapeDtypeStruct((layers, rows, width), value.dtype)] * len(ks),
        compiler_params=params(),
        name="cut_columns",
    )(me, *[value] * len(ks), *after)


def join_rows(value, layer, layers, received, me, c0, widths, parts):
    rows = value.shape[1]
    width = sum(widths)

    def kernel(me_ref, *refs):
        for k in range(parts):
            at = c0 if k == 0 else 0
            for out, w in zip(refs[parts:], widths):
                out[0, aligned(me_ref[0] ^ k, rows), :] = refs[k][0, :, at:at + w]
                at += w

    return pl.pallas_call(
        kernel,
        grid_spec=pltpu.PrefetchScalarGridSpec(
            num_scalar_prefetch=1,
            grid=(layers,),
            in_specs=[column_spec(value, layer, parts, 0)]
            + [layer_spec(rows, width)] * (parts - 1),
            out_specs=[layer_spec(rows * parts, w) for w in widths],
        ),
        out_shape=[jax.ShapeDtypeStruct((layers, rows * parts, w), value.dtype) for w in widths],
        compiler_params=params(),
        name="join_rows",
    )(me, value, *received)


def two_lines(devices, hops):
    return devices == 8 and devices == 2 * hops + 2


def window_offsets(devices, hops):
    seen = []
    for offset in range(-hops, hops + 1):
        if offset % devices not in seen:
            seen.append(offset % devices)
    return sorted(seen, key=lambda offset: min(offset, devices - offset))


def plan_window(devices, hops):
    table = np.zeros((devices, devices), np.int32)
    if two_lines(devices, hops):
        for z in range(4):
            for y in range(2):
                inner, far, back = z in (1, 2), 3 - z, 1 - y
                places = [
                    (z, y), (z ^ 1, y), (z, back), (z ^ 1, back), (far, back if inner else y),
                    (far, y) if inner else (2 if z == 0 else 1, back),
                    (3 if z == 1 else 0, back) if inner else (far, back),
                ]
                for place, (a, b) in enumerate(places):
                    table[2 * z + y, 2 * a + b] = place
        return table
    for d in range(devices):
        for place, offset in enumerate(window_offsets(devices, hops)):
            table[d, (d + offset) % devices] = place
    return table


def relay_plan():
    def lines(pairs):
        return [(2 * a + y, 2 * b + y) for a, b in pairs for y in (0, 1)]

    outer = lines([(0, 1), (1, 0), (2, 3), (3, 2)])
    middle = lines([(1, 2), (2, 1)])
    to_ends = lines([(1, 0), (2, 3)])
    across = [(i, i ^ 1) for i in range(8)]
    across_inner = [(i, i ^ 1) for i in (2, 3, 4, 5)]
    across_ends = [(i, i ^ 1) for i in (0, 1, 6, 7)]
    return {
        "q1": ("own", outer), "y1": ("own", across), "q2": ("own", middle),
        "q3": ("q1", middle), "y2": ("q1", across), "q5": ("y1", middle),
        "q4": ("q3", to_ends), "y3a": ("q3", across_inner),
        "q6": ("q5", to_ends), "y3b": ("q4", across_ends),
    }


ROUNDS = (
    (("q1", 0), ("y1", 0), ("q2", 0)),
    (("q3", 0), ("y2", 0), ("q1", 1)),
    (("q5", 0), ("q4", 0), ("y1", 1)),
    (("q6", 0), ("y3a", 0), ("y3b", 0), ("q3", 1)),
    (("q5", 1), ("q4", 1), ("y2", 1)),
    (("q6", 1), ("y3a", 1), ("y3b", 1), ("q2", 1)),
)
PLACES = (("own",), ("q1",), ("y1",), ("y2",), ("q5", "q4"), ("q2", "q6"), ("y3a", "y3b"))


def load_window(pieces, counts, ends, raw, window, sems, block):
    rows = raw.shape[1]
    at = 0
    for place, count in enumerate(counts):
        for end in range(count):
            def fetch(at=at, place=place, end=end):
                pltpu.make_async_copy(pieces[at + end], raw.at[place], sems.at[place]).start()

            if count == 1:
                fetch()
            else:
                pl.when(ends[0] == end)(fetch)
        at += count
    for place in range(len(counts)):
        pltpu.make_async_copy(pieces[0], raw.at[place], sems.at[place]).wait()

        def one(i, carry, place=place):
            high, low = split(raw[place, aligned(i, block), :])
            base = (place * (rows // block) + i) * 2
            window[aligned(base, block), :] = high
            window[aligned(base + 1, block), :] = low
            return carry

        lax.fori_loop(0, rows // block, one, 0)


def four_terms(strip):
    high, low = split(strip)
    return jnp.concatenate(
        [jnp.concatenate([high, high], 1), jnp.concatenate([low, low], 1)], 0)


def apply_kernel(counts, near, places, ends, strips, *rest):
    pieces = rest[:sum(counts)]
    image, raw, window, sems = rest[sum(counts):]
    step = pl.program_id(0)
    block = strips.shape[2]

    @pl.when(step == 0)
    def _():
        load_window(pieces, counts, ends, raw, window, sems, block)

    total = jnp.zeros((2 * block, raw.shape[2]), F32)
    for k in range(near):
        right = window[aligned(places[step, k], 2 * block), :]
        total = total + jnp.dot(four_terms(strips[0, k]), right, preferred_element_type=F32)
    image[...] = total[:block] + total[block:]


def group_specs(basis_rows, tile, g0, groups):
    specs, arrays = [], []
    for g in range(g0, g0 + groups):
        for value in basis_rows:
            for m in range(value.shape[0]):
                specs.append(pl.BlockSpec((1, tile, GROUP), lambda i, m=m, g=g: (m, i, g)))
                arrays.append(value)
    return specs, arrays


def apply(places, ends, strips, pieces):
    row_blocks, near, block, _ = strips.shape
    rows, width = pieces[0][0].shape
    counts = [len(p) for p in pieces]
    flat = [x for p in pieces for x in p]
    return pl.pallas_call(
        functools.partial(apply_kernel, counts, near),
        grid=(row_blocks,),
        out_shape=jax.ShapeDtypeStruct((rows, width), F32),
        in_specs=[SMEM, SMEM, pl.BlockSpec((1, near, block, block), lambda i: (i, 0, 0, 0))]
        + [ANY] * len(flat),
        out_specs=pl.BlockSpec((block, width), lambda i: (i, 0)),
        scratch_shapes=[
            pltpu.VMEM((len(counts), rows, width), F32),
            pltpu.VMEM((len(counts) * rows * 2, width), BF16),
            pltpu.SemaphoreType.DMA((len(counts),)),
        ],
        compiler_params=params(),
        cost_estimate=pl.CostEstimate(
            flops=8 * row_blocks * near * block * block * width,
            bytes_accessed=strips.size * 4 + 8 * rows * width * 4, transcendentals=0),
        name="apply",
    )(places, ends, strips, *flat)


def inner_kernel(orders, image, *rest):
    basis, partial = rest[:-1], rest[-1]

    @pl.when(pl.program_id(0) == 0)
    def _():
        partial[...] = jnp.zeros_like(partial)

    for g in range(partial.shape[0]):
        cols = slice(g * GROUP, (g + 1) * GROUP)
        wide = jnp.concatenate([basis[g * orders + m][0] for m in range(orders)], 1)
        partial[g] += dot3(image[:, cols], wide, ((0,), (0,)))


def inner(image, at, basis_rows, g0, groups):
    rows, width = image.shape[0], groups * GROUP
    orders = sum(x.shape[0] for x in basis_rows)
    tile = rows // 4
    specs, arrays = group_specs(basis_rows, tile, g0, groups)
    shape = (groups, GROUP, orders * GROUP)
    return pl.pallas_call(
        functools.partial(inner_kernel, orders),
        grid=(rows // tile,),
        out_shape=jax.ShapeDtypeStruct(shape, F32),
        in_specs=[pl.BlockSpec((tile, width), lambda i: (i, at // groups))] + specs,
        out_specs=pl.BlockSpec(shape, lambda i: (0, 0, 0)),
        compiler_params=params(),
        cost_estimate=pl.CostEstimate(
            flops=24 * rows * width * GROUP, bytes_accessed=5 * rows * width * 4,
            transcendentals=0),
        name="inner",
    )(image, *arrays)


def project_kernel(orders, image, coeffs_t, *rest):
    groups = coeffs_t.shape[0]
    basis, (residual, gram, coeffs) = rest[:groups * orders], rest[groups * orders:]

    @pl.when(pl.program_id(0) == 0)
    def _():
        gram[...] = jnp.zeros_like(gram)
        for g in range(groups):
            for m in range(orders):
                coeffs[m, g] = coeffs_t[g, :, m * GROUP:(m + 1) * GROUP].T

    for g in range(groups):
        cols = slice(g * GROUP, (g + 1) * GROUP)
        wide = jnp.concatenate([basis[g * orders + m][0] for m in range(orders)], 1)
        left = image[:, cols] - dot3(wide, coeffs_t[g], ((1,), (1,)))
        residual[:, cols] = left
        gram[g] += dot3(left, left, ((0,), (0,)))


def project(image, at, basis_rows, coeffs_t, g0, groups):
    orders = sum(x.shape[0] for x in basis_rows)
    rows, width = image.shape[0], groups * GROUP
    tile = rows // 4
    specs, arrays = group_specs(basis_rows, tile, g0, groups)
    return pl.pallas_call(
        functools.partial(project_kernel, orders),
        grid=(rows // tile,),
        out_shape=[
            jax.ShapeDtypeStruct((rows, width), F32),
            jax.ShapeDtypeStruct((groups, GROUP, GROUP), F32),
            jax.ShapeDtypeStruct((orders, groups, GROUP, GROUP), F32),
        ],
        in_specs=[
            pl.BlockSpec((tile, width), lambda i: (i, at // groups)),
            pl.BlockSpec(coeffs_t.shape, lambda i: (0, 0, 0)),
        ] + specs,
        out_specs=[
            pl.BlockSpec((tile, width), lambda i: (i, 0)),
            pl.BlockSpec((groups, GROUP, GROUP), lambda i: (0, 0, 0)),
            pl.BlockSpec((orders, groups, GROUP, GROUP), lambda i: (0, 0, 0, 0)),
        ],
        compiler_params=params(),
        cost_estimate=pl.CostEstimate(
            flops=30 * rows * width * GROUP, bytes_accessed=6 * rows * width * 4,
            transcendentals=0),
        name="project",
    )(image, coeffs_t, *arrays)


def eliminate(gram):
    count = len(gram)
    order = gram[0].shape[0]
    row_at = lax.broadcasted_iota(jnp.int32, (order, order), 0)
    col_at = lax.broadcasted_iota(jnp.int32, (order, order), 1)
    eye = jnp.where(row_at == col_at, 1.0, 0.0).astype(F32)
    rest = [jnp.concatenate([g, eye], 1) for g in gram]
    done = [[] for _ in gram]
    panel_row = lax.broadcasted_iota(jnp.int32, (PANEL, 1), 0)
    for p0 in range(0, order, PANEL):
        panels = [r[:PANEL] for r in rest]
        for j in range(PANEL):
            for n in range(count):
                panel = panels[n]
                column = panel[:, p0 + j:p0 + j + 1]
                pivot = column[j:j + 1]
                factor = jnp.where(panel_row > j, column / pivot, 0.0)
                panels[n] = panel - factor * panel[j:j + 1]
        for n in range(count):
            panel = panels[n]
            own = slice(p0, p0 + PANEL)
            diagonal = jnp.sum(jnp.where(
                lax.broadcasted_iota(jnp.int32, (PANEL, PANEL), 0)
                == lax.broadcasted_iota(jnp.int32, (PANEL, PANEL), 1),
                panel[:, own], 0.0), axis=1, keepdims=True)
            panel = panel * lax.rsqrt(diagonal)
            done[n].append(panel)
            if p0 + PANEL < order:
                below = panel[:, p0 + PANEL:order]
                rest[n] = rest[n][PANEL:] - lax.dot_general(
                    below, panel, (((0,), (0,)), ((), ())),
                    precision=lax.Precision.HIGHEST, preferred_element_type=F32)
    lowers, inverses = [], []
    for n in range(count):
        upper = jnp.concatenate(done[n], 0)
        lowers.append(jnp.where(row_at >= col_at, upper[:, :order].T, 0.0))
        inverses.append(upper[:, order:])
    return lowers, inverses


def finish_kernel(groups, parts, me, gram, residual, *outs):
    lowers, inverses = eliminate([gram[g] for g in range(groups)])
    rows = residual.shape[0] // parts
    for k in range(parts):
        for g in range(groups):
            cols = slice(g * GROUP, (g + 1) * GROUP)
            left = residual[aligned(me[0] ^ k, rows), cols]
            outs[k][:rows, cols] = dot3(left, inverses[g], ((1,), (1,)))
            outs[k][rows:, cols] = lowers[g]


def finish(me, gram, residual, parts):
    groups = gram.shape[0]
    rows, width = residual.shape
    shape = jax.ShapeDtypeStruct((rows // parts + GROUP, width), F32)
    return pl.pallas_call(
        functools.partial(finish_kernel, groups, parts),
        out_shape=[shape] * parts,
        in_specs=[SMEM, VMEM, VMEM],
        out_specs=[VMEM] * parts,
        compiler_params=params(),
        cost_estimate=pl.CostEstimate(
            flops=6 * rows * width * GROUP, bytes_accessed=4 * rows * width * 4,
            transcendentals=0),
        name="finish",
    )(me, gram, residual)


def collect_blocks(me, blocks, chunks, new_shape, factor_shape, parts):
    rows = new_shape[0]
    step = new_shape[1] // parts
    per_part = step // GROUP

    def kernel(me_ref, *refs):
        new_out, factor_out = refs[-2:]
        for c, (g0, groups) in enumerate(chunks):
            for k in range(parts):
                src = refs[c * parts + k]
                at = me_ref[0] ^ k
                for g in range(groups):
                    cols = slice(g * GROUP, (g + 1) * GROUP)
                    group = at * per_part + g0 + g
                    new_out[:, aligned(group, GROUP)] = src[:rows, cols]
                    factor_out[group] = src[rows:, cols]

    return pl.pallas_call(
        kernel,
        out_shape=[jax.ShapeDtypeStruct(new_shape, F32), jax.ShapeDtypeStruct(factor_shape, F32)],
        in_specs=[SMEM] + [VMEM] * (len(chunks) * parts),
        out_specs=[VMEM] * 2,
        compiler_params=params(),
        name="collect_blocks",
    )(me, *[x for c in blocks for x in c])


def collect_coeffs(me, coeffs, chunks, shape, parts):
    per_part = shape[1] // parts

    def kernel(me_ref, *refs):
        for c, (g0, groups) in enumerate(chunks):
            for k in range(parts):
                for g in range(groups):
                    refs[-1][:, (me_ref[0] ^ k) * per_part + g0 + g] = refs[c * parts + k][:, g]

    return pl.pallas_call(
        kernel,
        out_shape=jax.ShapeDtypeStruct(shape, F32),
        in_specs=[SMEM] + [VMEM] * (len(chunks) * parts),
        out_specs=VMEM,
        compiler_params=params(),
        name="collect_coeffs",
    )(me, *[x for c in coeffs for x in c])


def sum_blk(value):
    devices = lax.axis_size("blk")
    half = value.shape[0] // 2
    side = lax.axis_index("blk") % 2
    long = value.shape[0] > HALVED
    if long:
        kept = lax.dynamic_slice_in_dim(value, side * half, half, 0)
        sent = lax.dynamic_slice_in_dim(value, (1 - side) * half, half, 0)
        value = kept + swap(sent, "blk", 1)
    k = 2 if long else 1
    while k < devices:
        value = value + swap(value, "blk", k)
        k *= 2
    if long:
        other = swap(value, "blk", 1)
        value = jnp.concatenate(
            [jnp.where(side == 0, value, other), jnp.where(side == 0, other, value)], 0)
    return value


def sum_groups(value):
    return sum_blk(value.reshape(-1, value.shape[-1])).reshape(value.shape)


def local(strips, near_cols, vector_block, basis):
    local_blocks = strips.shape[0]
    devices = lax.axis_size("blk")
    parts = lax.axis_size("rhs")
    hops = -(-BAND // local_blocks)
    rows, total = vector_block.shape
    step = total // parts
    groups = step // GROUP
    orders = basis.shape[0]
    chunks = [(0, groups - groups // 2), (groups - groups // 2, groups // 2)]
    chunks = [chunk for chunk in chunks if chunk[1]]
    me = lax.axis_index("rhs").astype(jnp.int32).reshape(1)
    blk = lax.axis_index("blk")
    others = list(range(1, parts))
    relayed = two_lines(devices, hops) and len(chunks) == 2

    table = plan_window(devices, hops)
    place = jnp.asarray(table)[blk][near_cols // local_blocks]
    inside = near_cols % local_blocks
    places = place * local_blocks + inside
    ends = jnp.where((blk < 2) | (blk >= devices - 2), 1, 0).astype(jnp.int32).reshape(1)

    vector = vector_block[None]
    half = -(-orders // 2)
    values = {}

    def send(key):
        kind, at, k = key
        values[key] = swap(values["cut", kind, at, k], "rhs", k)

    def cut(kind, at, value, layer, layers, c0, width):
        for k, x in zip(others, cut_columns(
                value, layer, layers, me, others, c0, width, parts)):
            values["cut", kind, at, k] = x

    def join(kind, at, value, layer, layers, c0, width):
        got = [values[kind, at, k] for k in others]
        return join_rows(value, layer, layers, got, me, c0, [width], parts)[0]

    def own_rows(c):
        c0, width = chunks[c][0] * GROUP, chunks[c][1] * GROUP
        values["own", c] = join("v", c, vector, 0, 1, c0, width)[0]

    for c, (g0, n) in enumerate(chunks):
        cut("v", c, vector, 0, 1, g0 * GROUP, n * GROUP)
    layers = [(m, min(half, orders - m)) for m in range(0, orders, half)]
    for h, (m, n) in enumerate(layers):
        cut("b", h, basis, m, n, 0, step)

    def barrier(flying=()):
        keys = [key for key in values if key not in flying]
        for key, x in zip(keys, lax.optimization_barrier(tuple(values[k] for k in keys))):
            values[key] = x

    def window(c):
        return [[values[n, c] for n in alternatives] for alternatives in PLACES]

    for k in others:
        send(("v", 0, k))
    own_rows(0)
    if relayed:
        plan = relay_plan()
        beside = {}
        for h in range(len(layers)):
            for k in others:
                beside.setdefault(1 + h if k == 1 else 2 * h + k - 1, []).append(("b", h, k))
        for r, relays in enumerate(ROUNDS):
            for name, c in relays:
                source, pairs = plan[name]
                values[name, c] = lax.ppermute(values[source, c], "blk", pairs)
            if r == 0:
                for k in others:
                    send(("v", 1, k))
                own_rows(1)
            flying = beside.get(r, ())
            for key in flying:
                send(key)
            if r == 4:
                values["image", 0] = apply(places, ends, strips, window(0))
            if r == 5:
                basis_rows = [join("b", h, basis, m, n, 0, step) for h, (m, n) in enumerate(layers)]
                for h, x in enumerate(basis_rows):
                    values["basis", h] = x
                values["partial", 0] = inner(values["image", 0], 0, basis_rows, *chunks[0])
            barrier(flying if True else ())
        basis_rows = [values["basis", h] for h in range(len(layers))]
        values["image", 1] = apply(places, ends, strips, window(1))
    else:
        for c in range(1, len(chunks)):
            for k in others:
                send(("v", c, k))
            own_rows(c)
        for h in range(len(layers)):
            for k in others:
                send(("b", h, k))
        basis_rows = [join("b", h, basis, m, n, 0, step) for h, (m, n) in enumerate(layers)]
        for c in range(len(chunks)):
            pieces = []
            for offset in window_offsets(devices, hops):
                pairs = [((i + offset) % devices, i) for i in range(devices)]
                own = values["own", c]
                pieces.append([lax.ppermute(own, "blk", pairs) if offset else own])
            values["image", c] = apply(places, ends, strips, pieces)

    tail = [(0, 0, *chunks[0])]
    if len(chunks) == 2:
        tail += [(1, 0, *chunks[1])] if True else [
            (1, g, chunks[1][0] + g, 1) for g in range(chunks[1][1])]
    blocks, all_coeffs, made = [], [], []
    for c, at, g0, n in tail:
        if (c, at) == (0, 0) and ("partial", 0) in values:
            part = values["partial", 0]
        else:
            part = inner(values["image", c], at, basis_rows, g0, n)
        made.append(project(values["image", c], at, basis_rows, sum_groups(part), g0, n))
    for (c, at, g0, n), (residual, gram, coeffs) in zip(tail, made):
        across = [swap(coeffs, "rhs", k) for k in others if k > 1 and not k & 1]
        both = [coeffs] + across
        pair = [swap(x, "rhs", 1) for x in both]
        all_coeffs.append([x for two in zip(both, pair) for x in two])
        out = finish(me, sum_groups(gram), residual, parts)
        blocks.append([out[0]] + [swap(out[k], "rhs", k) for k in others])
    chunks = [(g0, n) for _, _, g0, n in tail]

    coeffs = collect_coeffs(
        me, all_coeffs, chunks, (orders, total // GROUP, GROUP, GROUP), parts)
    new_block, factor = collect_blocks(
        me, blocks, chunks, (rows, total), (total // GROUP, GROUP, GROUP), parts)
    return new_block, coeffs, factor


def solution(mesh):
    placed = (
        P("blk", None, None, None),
        P("blk", None),
        P(("blk", "rhs"), None),
        P(None, ("blk", "rhs"), None),
    )
    return jax.shard_map(
        local,
        mesh=mesh,
        in_specs=placed,
        out_specs=(P(("blk", "rhs"), None), P(), P()),
        check_vma=False,
    )
```

time: 1080 us -> 344 us (0.32)
  waiting for transfers between devices: 518 us -> 127 us
  other arithmetic: 350 us -> 0.52 us
  starting transfers between devices: 8.81 us -> 106 us
  Pallas kernels: 0 us -> 95.4 us
  matrix products: 65.1 us -> 0 us
  blocking collectives: 60.3 us -> 0 us
  local copies, waits for them, and re-layouts: 62 us -> 12.8 us
  between operations: 14.2 us -> 1.12 us
    another operation x7 -> x0, other arithmetic: 348 us -> none  [the longest x4 189 us: local(): factor = jnp.linalg.cholesky(gram)]
    psum x2 -> x0, waiting for transfers between devices: 315 us -> none  [the longest x1 190 us: local(): coeffs = lax.psum(partial_value, ('blk', 'rhs'))]
    ppermute x6 -> x60, starting transfers between devices: 8.51 us -> 106 us  [the longest x40 71.8 us: swap(): return lax.ppermute(value, axis, pairs_of(axis, k))]
    pallas_call x0 -> x18, Pallas kernels: none -> 95.4 us  [the longest x2 28.8 us: apply(): pl.pallas_call(functools.partial(apply_kernel, counts, near), grid=(row_b...]
    ppermute x6 -> x60, waiting for transfers between devices: 204 us -> 127 us  [the longest x20 64.9 us: local(): values[name, c] = lax.ppermute(values[source, c], 'blk', pairs)]
    dot_general x4 -> x0, matrix products: 61.8 us -> none  [the longest x1 33.5 us: apply_strips(): result = jnp.einsum('ikab,ikbc->iac', strips, chosen, precision=HIGHEST)]
    all_to_all x2 -> x0, blocking collectives: 60.3 us -> none  [the longest x1 31.5 us: local(): lax.all_to_all(image, 'rhs', split_axis=0, concat_axis=1, tiled=True)]
    gather x1, local copies, waits for them, and re-layouts: 24.8 us -> 1.87 us  [local(): place = jnp.asarray(table)[blk][near_cols // local_blocks]]
  transfers between devices with their start and end apart: 8 -> 60, of which waited for: 4 -> 24; matrix products, arithmetic and copies ran while one was open for 2% -> 1% of each run, Pallas kernels for 0% -> 27%
where the time goes in v2:
time: 344 us; the launch traced here: 343 us
  waiting for transfers between devices  127 us (37%)
  starting transfers between devices  106 us (31%)
  Pallas kernels  95.4 us (28%)
  local copies, waits for them, and re-layouts  12.8 us (4%)
    ppermute x40, starting transfers between devices, swap(): return lax.ppermute(value, axis, pairs_of(axis, k))  71.8 us
    ppermute x20, waiting for transfers between devices, local(): values[name, c] = lax.ppermute(values[source, c], 'blk', pairs)  64.9 us
    ppermute x40, waiting for transfers between devices, swap(): return lax.ppermute(value, axis, pairs_of(axis, k))  62.2 us
    ppermute x20, starting transfers between devices, local(): values[name, c] = lax.ppermute(values[source, c], 'blk', pairs)  34.1 us
    pallas_call x2, Pallas kernels, apply(): pl.pallas_call(functools.partial(apply_kernel, counts, near), grid=(row_b...  28.8 us
    pallas_call x2, Pallas kernels, finish(): pl.pallas_call(functools.partial(finish_kernel, groups, parts), out_shape...  24.8 us
    pallas_call x2, Pallas kernels, project(): pl.pallas_call(functools.partial(project_kernel, orders), grid=(rows // t...  15.4 us
    unnamed x34, local copies, waits for them, and re-layouts  10 us
  transfers between devices with their start and end apart: 60, of which 24 were waited for; matrix products, arithmetic and copies ran while one was open for 1% of the time, Pallas kernels for 27%

profile of v2, /device:TPU:1, one launch (start us, length us, event | category | flops | bytes accessed | tf_op | source)
XLA Modules:
  0.0 342.9 jit_solution(333702087587598226)
XLA Ops:
  2.4 2.7 collective-permute-start.1
  5.1 6.5 %collective-permute-done.1.refs_2_ = f32[1,256,256]{2,1,0:T(8,128)S(1)} collective-permute-done((f32[1,256,256]{2,1,0:T(8,128)S(1)}, f32[1,256,256]{2,1,0:T(8,128)S(1)}, u32[]{:S(2)}, u32[]{:S(2)}) %collective-permute-start.1) | collective-permute-done | bytes 262176 | tf_op jit(solution)/shard_map/ppermute | solution.py:33
  11.7 5.6 %collective-permute-done.2.refs_3_ = f32[1,256,256]{2,1,0:T(8,128)S(1)} collective-permute-done((f32[1,256,256]{2,1,0:T(8,128)S(1)}, f32[1,256,256]{2,1,0:T(8,128)S(1)}, u32[]{:S(2)}, u32[]{:S(2)}) %collective-permute-start.2) | collective-permute-done | bytes 262176 | tf_op jit(solution)/shard_map/ppermute | solution.py:33
  24.5 2.0 cut_columns.6
  26.5 2.9 cut_columns.7
  30.5 5.5 %collective-permute-done.8.refs_3_ = f32[1,256,256]{2,1,0:T(8,128)S(1)} collective-permute-done((f32[1,256,256]{2,1,0:T(8,128)S(1)}, f32[1,256,256]{2,1,0:T(8,128)S(1)}, u32[]{:S(2)}, u32[]{:S(2)}) %collective-permute-start.8) | collective-permute-done | bytes 262176 | tf_op jit(solution)/shard_map/ppermute | solution.py:33
  37.0 5.1 %collective-permute-done.3.rest_1_ = f32[1024,256]{1,0:T(8,128)S(1)} collective-permute-done((f32[1024,256]{1,0:T(8,128)S(1)}, f32[1024,256]{1,0:T(8,128)S(1)}, u32[]{:S(2)}, u32[]{:S(2)}) %collective-permute-start.3) | collective-permute-done | bytes 1048608 | tf_op jit(solution)/shard_map/ppermute | solution.py:545
  47.2 4.6 %collective-permute-start.11 = (f32[1024,256]{1,0:T(8,128)}, f32[1024,256]{1,0:T(8,128)}, u32[]{:S(2)}, u32[]{:S(2)}) collective-permute-start(f32[1024,256]{1,0:T(8,128)} %bitcast.3.rest_0_), channel_id=1, source_target_pairs={{0,8},{4,12},{8,0},{12,4},{16,24},{20,28},{24,16},{28,20},{1,9},{5... | collective-permute-start | bytes 3145736 | tf_op jit(solution)/shard_map/ppermute | solution.py:545
  51.8 2.5 collective-permute-start.12
  55.5 12.8 %collective-permute-done.10.rest_3_ = f32[1024,256]{1,0:T(8,128)S(1)} collective-permute-done((f32[1024,256]{1,0:T(8,128)S(1)}, f32[1024,256]{1,0:T(8,128)S(1)}, u32[]{:S(2)}, u32[]{:S(2)}) %collective-permute-start.10) | collective-permute-done | bytes 1048608 | tf_op jit(solution)/shard_map/ppermute | solution.py:545
  68.3 5.0 %collective-permute-done.11.rest_1_ = f32[1024,256]{1,0:T(8,128)} collective-permute-done((f32[1024,256]{1,0:T(8,128)}, f32[1024,256]{1,0:T(8,128)}, u32[]{:S(2)}, u32[]{:S(2)}) %collective-permute-start.11) | collective-permute-done | bytes 1048608 | tf_op jit(solution)/shard_map/ppermute | solution.py:545
  77.5 4.3 %collective-permute-start.17 = (f32[2,256,512]{2,1,0:T(8,128)S(1)}, f32[2,256,512]{2,1,0:T(8,128)S(1)}, u32[]{:S(2)}, u32[]{:S(2)}) collective-permute-start(f32[2,256,512]{2,1,0:T(8,128)S(1)} %get-tuple-element.138), channel_id=1, source_target_pairs={{0,3},{1,2},{2,1},{3,0},{4,7},{5,6},{6,5},{7,4},{8,11},{9,10},{10,... | collective-permute-start | bytes 3145736 | tf_op jit(solution)/shard_map/ppermute | solution.py:33
  81.8 17.2 %collective-permute-done.15.rest_5_ = f32[1024,256]{1,0:T(8,128)} collective-permute-done((f32[1024,256]{1,0:T(8,128)}, f32[1024,256]{1,0:T(8,128)}, u32[]{:S(2)}, u32[]{:S(2)}) %collective-permute-start.15) | collective-permute-done | bytes 1048608 | tf_op jit(solution)/shard_map/ppermute | solution.py:545
  101.9 3.1 collective-permute-start.21
  109.3 1.9 gather_fusion
  112.7 9.5 %collective-permute-done.19.rest_7_ = f32[1024,256]{1,0:T(8,128)} collective-permute-done((f32[1024,256]{1,0:T(8,128)}, f32[1024,256]{1,0:T(8,128)}, u32[]{:S(2)}, u32[]{:S(2)}) %collective-permute-start.19) | collective-permute-done | bytes 1048608 | tf_op jit(solution)/shard_map/ppermute | solution.py:545
  122.3 2.7 collective-permute-done.21.rest_9_
  129.4 6.1 %collective-permute-start.27 = (f32[2,256,512]{2,1,0:T(8,128)}, f32[2,256,512]{2,1,0:T(8,128)}, u32[]{:S(2)}, u32[]{:S(2)}) collective-permute-start(f32[2,256,512]{2,1,0:T(8,128)} %copy-done.8), channel_id=1, source_target_pairs={{0,3},{1,2},{2,1},{3,0},{4,7},{5,6},{6,5},{7,4},{8,11},{9,10},{10,... | collective-permute-start | bytes 3145736 | tf_op jit(solution)/shard_map/ppermute | solution.py:33
  138.0 14.1 %apply.2.image = f32[1024,256]{1,0:T(8,128)S(1)} custom-call(s32[8,25]{1,0:T(8,128)S(1)} %fusion.places, s32[1]{0:T(128)} %bitcast.5.ends, f32[8,25,128,128]{3,2,1,0:T(8,128)} %strips.3, f32[1024,256]{1,0:T(8,128)S(1)} %bitcast.32, f32[1024,256]{1,0:T(8,128)S(1)} %copy-done.10, f32[1024,256]{1,0:T(8,128)} %collective-permute-done.4.rest_2_, ...), custom_call_target="tpu_custom_call" | custom-call | flops 6710886400 | bytes 21495808 | tf_op jit(solution)/shard_map/apply/pallas_call | solution.py:236
  152.1 5.4 %collective-permute-done.25.rest_5_ = f32[1024,256]{1,0:T(8,128)} collective-permute-done((f32[1024,256]{1,0:T(8,128)}, f32[1024,256]{1,0:T(8,128)}, u32[]{:S(2)}, u32[]{:S(2)}) %collective-permute-start.25) | collective-permute-done | bytes 1048608 | tf_op jit(solution)/shard_map/ppermute | solution.py:545
  160.5 2.1 collective-permute-start.30
  165.5 3.3 join_rows.6.rest_0_.rest_1_.rest_4_.rest_5_
  168.8 3.5 %join_rows.7.rest_2_.rest_3_.rest_6_.rest_7_ = f32[2,1024,512]{2,1,0:T(8,128)} custom-call(s32[1]{0:T(128)} %bitcast.me_ref.me, f32[4,256,2048]{2,1,0:T(8,128)} %refs_0_.7, f32[2,256,512]{2,1,0:T(8,128)S(1)} %copy-done.5, f32[2,256,512]{2,1,0:T(8,128)} %collective-permute-done.23.refs_2_, f32[2,256,512]{2,1,0:T(8,128)} %collective-permute-done.27.refs_3_), custom_call_target="tpu_custom_call" | custom-call | tf_op jit(solution)/shard_map/join_rows/pallas_call | solution.py:96
  172.3 4.1 %inner.2 = f32[2,128,512]{2,1,0:T(8,128)S(1)} custom-call(f32[1024,256]{1,0:T(8,128)S(1)} %apply.2.image, f32[2,1024,512]{2,1,0:T(8,128)} %join_rows.6.rest_0_.rest_1_.rest_4_.rest_5_, f32[2,1024,512]{2,1,0:T(8,128)} %join_rows.6.rest_0_.rest_1_.rest_4_.rest_5_, f32[2,1024,512]{2,1,0:T(8,128)} %join_rows.7.rest_2_.rest_3_.rest_6_.rest_7_, ...), custom_call_target="tpu_custom_call" | custom-call | flops 805306368 | bytes 5242880 | tf_op jit(solution)/shard_map/inner/pallas_call | solution.py:275
  176.5 4.6 %collective-permute-done.28.rest_7_ = f32[1024,256]{1,0:T(8,128)} collective-permute-done((f32[1024,256]{1,0:T(8,128)}, f32[1024,256]{1,0:T(8,128)}, u32[]{:S(2)}, u32[]{:S(2)}) %collective-permute-start.28) | collective-permute-done | bytes 1048608 | tf_op jit(solution)/shard_map/ppermute | solution.py:545
  183.5 14.6 %apply.3.image = f32[1024,256]{1,0:T(8,128)S(1)} custom-call(s32[8,25]{1,0:T(8,128)S(1)} %fusion.places, s32[1]{0:T(128)} %bitcast.5.ends, f32[8,25,128,128]{3,2,1,0:T(8,128)} %strips.3, f32[1024,256]{1,0:T(8,128)} %bitcast.3.rest_0_, f32[1024,256]{1,0:T(8,128)} %collective-permute-done.11.rest_1_, f32[1024,256]{1,0:T(8,128)} %copy-done.14, ...), custom_call_target="tpu_custom_call" | custom-call | flops 6710886400 | bytes 21495808 | tf_op jit(solution)/shard_map/apply/pallas_call | solution.py:236
  198.1 4.1 %inner.3 = f32[2,128,512]{2,1,0:T(8,128)S(1)} custom-call(f32[1024,256]{1,0:T(8,128)S(1)} %apply.3.image, f32[2,1024,512]{2,1,0:T(8,128)} %join_rows.6.rest_0_.rest_1_.rest_4_.rest_5_, f32[2,1024,512]{2,1,0:T(8,128)} %join_rows.6.rest_0_.rest_1_.rest_4_.rest_5_, f32[2,1024,512]{2,1,0:T(8,128)} %join_rows.7.rest_2_.rest_3_.rest_6_.rest_7_, ...), custom_call_target="tpu_custom_call" | custom-call | flops 805306368 | bytes 5242880 | tf_op jit(solution)/shard_map/inner/pallas_call | solution.py:275
  202.8 8.4 %collective-permute-start.33 = (f32[128,512]{1,0:T(8,128)S(1)}, f32[128,512]{1,0:T(8,128)S(1)}, u32[]{:S(2)}, u32[]{:S(2)}) collective-permute-start(f32[128,512]{1,0:T(8,128)S(1)} %dynamic-slice_add_fusion.1), channel_id=1, source_target_pairs={{0,8},{4,12},{8,0},{12,4},{16,24},{20,28},{24,16},{28,20},{1,9},{5... | collective-permute-start | bytes 786440 | tf_op jit(solution)/shard_map/ppermute | solution.py:33
  211.3 3.7 %collective-permute-start.44 = (f32[128,512]{1,0:T(8,128)S(1)}, f32[128,512]{1,0:T(8,128)S(1)}, u32[]{:S(2)}, u32[]{:S(2)}) collective-permute-start(f32[128,512]{1,0:T(8,128)S(1)} %dynamic-slice_add_fusion), channel_id=1, source_target_pairs={{0,8},{4,12},{8,0},{12,4},{16,24},{20,28},{24,16},{28,20},{1,9},{5... | collective-permute-start | bytes 786440 | tf_op jit(solution)/shard_map/ppermute | solution.py:33
  215.3 2.7 collective-permute-start.34
  218.0 5.0 %collective-permute-done.44 = f32[128,512]{1,0:T(8,128)S(1)} collective-permute-done((f32[128,512]{1,0:T(8,128)S(1)}, f32[128,512]{1,0:T(8,128)S(1)}, u32[]{:S(2)}, u32[]{:S(2)}) %collective-permute-start.44) | collective-permute-done | bytes 262176 | tf_op jit(solution)/shard_map/ppermute | solution.py:33
  224.9 2.5 collective-permute-start.35
  227.3 13.3 %collective-permute-done.45 = f32[128,512]{1,0:T(8,128)S(1)} collective-permute-done((f32[128,512]{1,0:T(8,128)S(1)}, f32[128,512]{1,0:T(8,128)S(1)}, u32[]{:S(2)}, u32[]{:S(2)}) %collective-permute-start.45) | collective-permute-done | bytes 262176 | tf_op jit(solution)/shard_map/ppermute | solution.py:33
  240.7 3.2 collective-permute-start.46
  243.9 7.6 %project.2 = (f32[1024,256]{1,0:T(8,128)S(1)}, f32[2,128,128]{2,1,0:T(8,128)S(1)}, f32[4,2,128,128]{3,2,1,0:T(8,128)S(1)}) custom-call(f32[1024,256]{1,0:T(8,128)S(1)} %apply.2.image, f32[2,128,512]{2,1,0:T(8,128)S(1)} %bitcast.28, f32[2,1024,512]{2,1,0:T(8,128)} %join_rows.6.rest_0_.rest_1_.rest_4_.rest_5_, ...), custom_call_target="tpu_custom_call" | custom-call | flops 1006632960 | bytes 6291456 | tf_op jit(solution)/shard_map/project/pallas_call | solution.py:313
  251.7 7.8 %project.3 = (f32[1024,256]{1,0:T(8,128)S(1)}, f32[2,128,128]{2,1,0:T(8,128)S(1)}, f32[4,2,128,128]{3,2,1,0:T(8,128)S(1)}) custom-call(f32[1024,256]{1,0:T(8,128)S(1)} %apply.3.image, f32[2,128,512]{2,1,0:T(8,128)S(1)} %bitcast.27, f32[2,1024,512]{2,1,0:T(8,128)} %join_rows.6.rest_0_.rest_1_.rest_4_.rest_5_, ...), custom_call_target="tpu_custom_call" | custom-call | flops 1006632960 | bytes 6291456 | tf_op jit(solution)/shard_map/project/pallas_call | solution.py:313
  261.2 2.0 collective-permute-done.47
  269.1 3.8 %collective-permute-start.55 = (f32[4,2,128,128]{3,2,1,0:T(8,128)S(1)}, f32[4,2,128,128]{3,2,1,0:T(8,128)S(1)}, u32[]{:S(2)}, u32[]{:S(2)}) collective-permute-start(f32[4,2,128,128]{3,2,1,0:T(8,128)S(1)} %get-tuple-element.224.refs_0_), channel_id=1, source_target_pairs={{0,2},{1,3},{2,0},{3,1},{4,6},{5,7},{6,4},{7,5},{8,10},{9,11},{10,... | collective-permute-start | bytes 1572872 | tf_op jit(solution)/shard_map/ppermute | solution.py:33
  273.2 12.4 %finish.2 = (f32[384,256]{1,0:T(8,128)S(1)}, f32[384,256]{1,0:T(8,128)S(1)}, f32[384,256]{1,0:T(8,128)S(1)}, f32[384,256]{1,0:T(8,128)S(1)}) custom-call(s32[1]{0:T(128)} %bitcast.me_ref.me, f32[2,128,128]{2,1,0:T(8,128)S(1)} %bitcast.33, f32[1024,256]{1,0:T(8,128)S(1)} %get-tuple-element.202.residual), custom_call_target="tpu_custom_call" | custom-call | flops 201326592 | bytes 4194304 | tf_op jit(solution)/shard_map/finish/pallas_call | solution.py:393
  285.6 11.6 %collective-permute-start.40 = (f32[384,256]{1,0:T(8,128)S(1)}, f32[384,256]{1,0:T(8,128)S(1)}, u32[]{:S(2)}, u32[]{:S(2)}) collective-permute-start(f32[384,256]{1,0:T(8,128)S(1)} %get-tuple-element.204), channel_id=1, source_target_pairs={{0,1},{1,0},{2,3},{3,2},{4,5},{5,4},{6,7},{7,6},{8,9},{9,8},{10,11... | collective-permute-start | bytes 1179656 | tf_op jit(solution)/shard_map/ppermute | solution.py:33
  297.2 1.9 collective-permute-start.41
  299.2 12.4 %finish.3 = (f32[384,256]{1,0:T(8,128)S(1)}, f32[384,256]{1,0:T(8,128)S(1)}, f32[384,256]{1,0:T(8,128)S(1)}, f32[384,256]{1,0:T(8,128)S(1)}) custom-call(s32[1]{0:T(128)} %bitcast.me_ref.me, f32[2,128,128]{2,1,0:T(8,128)S(1)} %bitcast.34, f32[1024,256]{1,0:T(8,128)S(1)} %get-tuple-element.218.residual), custom_call_target="tpu_custom_call" | custom-call | flops 201326592 | bytes 4194304 | tf_op jit(solution)/shard_map/finish/pallas_call | solution.py:393
  314.2 3.0 collective-permute-done.42.refs_3_
  317.6 7.7 %collective-permute-done.52.refs_6_ = f32[384,256]{1,0:T(8,128)S(1)} collective-permute-done((f32[384,256]{1,0:T(8,128)S(1)}, f32[384,256]{1,0:T(8,128)S(1)}, u32[]{:S(2)}, u32[]{:S(2)}) %collective-permute-start.52) | collective-permute-done | bytes 393248 | tf_op jit(solution)/shard_map/ppermute | solution.py:33
  325.3 2.0 collective-permute-start.53
  327.3 9.4 %collective-permute-done.53.refs_7_ = f32[384,256]{1,0:T(8,128)S(1)} collective-permute-done((f32[384,256]{1,0:T(8,128)S(1)}, f32[384,256]{1,0:T(8,128)S(1)}, u32[]{:S(2)}, u32[]{:S(2)}) %collective-permute-start.53) | collective-permute-done | bytes 393248 | tf_op jit(solution)/shard_map/ppermute | solution.py:33
  336.7 2.0 collect_blocks.1
  339.5 3.3 collect_coeffs.1
  (156 shorter events, 60.1 us)
Async XLA Ops:
  2.4 9.3 %collective-permute-start.1 = (f32[1,256,256]{2,1,0:T(8,128)S(1)}, f32[1,256,256]{2,1,0:T(8,128)S(1)}, u32[]{:S(2)}, u32[]{:S(2)}) collective-permute-start(f32[1,256,256]{2,1,0:T(8,128)S(1)} %get-tuple-element.116), channel_id=1, source_target_pairs={{0,2},{1,3},{2,0},{3,1},{4,6},{5,7},{6,4},{7,5},{8,10},{9,11},{10,... | collective-permute-start | bytes 786440 | tf_op jit(solution)/shard_map/ppermute | solution.py:33
  5.1 12.2 %collective-permute-start.2 = (f32[1,256,256]{2,1,0:T(8,128)S(1)}, f32[1,256,256]{2,1,0:T(8,128)S(1)}, u32[]{:S(2)}, u32[]{:S(2)}) collective-permute-start(f32[1,256,256]{2,1,0:T(8,128)S(1)} %get-tuple-element.117), channel_id=1, source_target_pairs={{0,3},{1,2},{2,1},{3,0},{4,7},{5,6},{6,5},{7,4},{8,11},{9,10},{10,... | collective-permute-start | bytes 786440 | tf_op jit(solution)/shard_map/ppermute | solution.py:33
  17.4 24.7 %collective-permute-start.3 = (f32[1024,256]{1,0:T(8,128)S(1)}, f32[1024,256]{1,0:T(8,128)S(1)}, u32[]{:S(2)}, u32[]{:S(2)}) collective-permute-start(f32[1024,256]{1,0:T(8,128)S(1)} %bitcast.29), channel_id=1, source_target_pairs={{0,8},{4,12},{8,0},{12,4},{16,24},{20,28},{24,16},{28,20},{1,9},{5... | collective-permute-start | bytes 3145736 | tf_op jit(solution)/shard_map/ppermute | solution.py:545
  19.0 24.3 %collective-permute-start.4 = (f32[1024,256]{1,0:T(8,128)S(1)}, f32[1024,256]{1,0:T(8,128)}, u32[]{:S(2)}, u32[]{:S(2)}) collective-permute-start(f32[1024,256]{1,0:T(8,128)S(1)} %bitcast.30), channel_id=1, source_target_pairs={{0,4},{4,0},{8,12},{12,8},{16,20},{20,16},{24,28},{28,24},{1,5},{5... | collective-permute-start | bytes 3145736 | tf_op jit(solution)/shard_map/ppermute | solution.py:545
  20.2 23.1 %collective-permute-start.5 = (f32[1024,256]{1,0:T(8,128)S(1)}, f32[1024,256]{1,0:T(8,128)S(1)}, u32[]{:S(2)}, u32[]{:S(2)}) collective-permute-start(f32[1024,256]{1,0:T(8,128)S(1)} %bitcast.31), channel_id=1, source_target_pairs={{8,16},{12,20},{16,8},{20,12},{9,17},{13,21},{17,9},{21,13},{10,18... | collective-permute-start | bytes 3145736 | tf_op jit(solution)/shard_map/ppermute | solution.py:545
  23.1 12.8 %collective-permute-start.8 = (f32[1,256,256]{2,1,0:T(8,128)S(1)}, f32[1,256,256]{2,1,0:T(8,128)S(1)}, u32[]{:S(2)}, u32[]{:S(2)}) collective-permute-start(f32[1,256,256]{2,1,0:T(8,128)S(1)} %get-tuple-element.120), channel_id=1, source_target_pairs={{0,3},{1,2},{2,1},{3,0},{4,7},{5,6},{6,5},{7,4},{8,11},{9,10},{10,... | collective-permute-start | bytes 786440 | tf_op jit(solution)/shard_map/ppermute | solution.py:33
  43.3 12.2 %collective-permute-start.9 = (f32[1024,256]{1,0:T(8,128)S(1)}, f32[1024,256]{1,0:T(8,128)}, u32[]{:S(2)}, u32[]{:S(2)}) collective-permute-start(f32[1024,256]{1,0:T(8,128)S(1)} %collective-permute-done.3.rest_1_), channel_id=1, source_target_pairs={{8,16},{12,20},{16,8},{20,12},{9,17},{13,21},{17,9},{21,13},{10,18... | collective-permute-start | bytes 3145736 | tf_op jit(solution)/shard_map/ppermute | solution.py:545
  44.9 23.4 %collective-permute-start.10 = (f32[1024,256]{1,0:T(8,128)S(1)}, f32[1024,256]{1,0:T(8,128)S(1)}, u32[]{:S(2)}, u32[]{:S(2)}) collective-permute-start(f32[1024,256]{1,0:T(8,128)S(1)} %collective-permute-done.3.rest_1_), channel_id=1, source_target_pairs={{0,4},{4,0},{8,12},{12,8},{16,20},{20,16},{24,28},{28,24},{1,5},{5... | collective-permute-start | bytes 3145736 | tf_op jit(solution)/shard_map/ppermute | solution.py:545
  47.2 26.1 %collective-permute-start.11 = (f32[1024,256]{1,0:T(8,128)}, f32[1024,256]{1,0:T(8,128)}, u32[]{:S(2)}, u32[]{:S(2)}) collective-permute-start(f32[1024,256]{1,0:T(8,128)} %bitcast.3.rest_0_), channel_id=1, source_target_pairs={{0,8},{4,12},{8,0},{12,4},{16,24},{20,28},{24,16},{28,20},{1,9},{5... | collective-permute-start | bytes 3145736 | tf_op jit(solution)/shard_map/ppermute | solution.py:545
  51.8 25.8 %collective-permute-start.12 = (f32[2,256,512]{2,1,0:T(8,128)S(1)}, f32[2,256,512]{2,1,0:T(8,128)S(1)}, u32[]{:S(2)}, u32[]{:S(2)}) collective-permute-start(f32[2,256,512]{2,1,0:T(8,128)S(1)} %get-tuple-element.127), channel_id=1, source_target_pairs={{0,1},{1,0},{2,3},{3,2},{4,5},{5,4},{6,7},{7,6},{8,9},{9,8},{10,11... | collective-permute-start | bytes 3145736 | tf_op jit(solution)/shard_map/ppermute | solution.py:33
  54.3 27.5 %collective-permute-start.13 = (f32[2,256,512]{2,1,0:T(8,128)S(1)}, f32[2,256,512]{2,1,0:T(8,128)S(1)}, u32[]{:S(2)}, u32[]{:S(2)}) collective-permute-start(f32[2,256,512]{2,1,0:T(8,128)S(1)} %get-tuple-element.128), channel_id=1, source_target_pairs={{0,2},{1,3},{2,0},{3,1},{4,6},{5,7},{6,4},{7,5},{8,10},{9,11},{10,... | collective-permute-start | bytes 3145736 | tf_op jit(solution)/shard_map/ppermute | solution.py:33
  74.9 24.1 %collective-permute-start.15 = (f32[1024,256]{1,0:T(8,128)}, f32[1024,256]{1,0:T(8,128)}, u32[]{:S(2)}, u32[]{:S(2)}) collective-permute-start(f32[1024,256]{1,0:T(8,128)} %collective-permute-done.9), channel_id=1, source_target_pairs={{8,0},{12,4},{16,24},{20,28},{9,1},{13,5},{17,25},{21,29},{10,2},{... | collective-permute-start | bytes 3145736 | tf_op jit(solution)/shard_map/ppermute | solution.py:545
  76.2 22.8 %collective-permute-start.16 = (f32[1024,256]{1,0:T(8,128)}, f32[1024,256]{1,0:T(8,128)S(1)}, u32[]{:S(2)}, u32[]{:S(2)}) collective-permute-start(f32[1024,256]{1,0:T(8,128)} %bitcast.3.rest_0_), channel_id=1, source_target_pairs={{0,4},{4,0},{8,12},{12,8},{16,20},{20,16},{24,28},{28,24},{1,5},{5... | collective-permute-start | bytes 3145736 | tf_op jit(solution)/shard_map/ppermute | solution.py:545
  77.5 28.2 %collective-permute-start.17 = (f32[2,256,512]{2,1,0:T(8,128)S(1)}, f32[2,256,512]{2,1,0:T(8,128)S(1)}, u32[]{:S(2)}, u32[]{:S(2)}) collective-permute-start(f32[2,256,512]{2,1,0:T(8,128)S(1)} %get-tuple-element.138), channel_id=1, source_target_pairs={{0,3},{1,2},{2,1},{3,0},{4,7},{5,6},{6,5},{7,4},{8,11},{9,10},{10,... | collective-permute-start | bytes 3145736 | tf_op jit(solution)/shard_map/ppermute | solution.py:33
  81.8 29.3 %collective-permute-start.18 = (f32[2,256,512]{2,1,0:T(8,128)}, f32[2,256,512]{2,1,0:T(8,128)S(1)}, u32[]{:S(2)}, u32[]{:S(2)}) collective-permute-start(f32[2,256,512]{2,1,0:T(8,128)} %get-tuple-element.139), channel_id=1, source_target_pairs={{0,1},{1,0},{2,3},{3,2},{4,5},{5,4},{6,7},{7,6},{8,9},{9,8},{10,11... | collective-permute-start | bytes 3145736 | tf_op jit(solution)/shard_map/ppermute | solution.py:33
  99.0 23.3 %collective-permute-start.19 = (f32[1024,256]{1,0:T(8,128)}, f32[1024,256]{1,0:T(8,128)}, u32[]{:S(2)}, u32[]{:S(2)}) collective-permute-start(f32[1024,256]{1,0:T(8,128)} %collective-permute-done.14.rest_4_), channel_id=1, source_target_pairs={{8,0},{12,4},{16,24},{20,28},{9,1},{13,5},{17,25},{21,29},{10,2},{... | collective-permute-start | bytes 3145736 | tf_op jit(solution)/shard_map/ppermute | solution.py:545
  100.3 22.0 %collective-permute-start.20 = (f32[1024,256]{1,0:T(8,128)}, f32[1024,256]{1,0:T(8,128)}, u32[]{:S(2)}, u32[]{:S(2)}) collective-permute-start(f32[1024,256]{1,0:T(8,128)} %collective-permute-done.9), channel_id=1, source_target_pairs={{8,12},{12,8},{16,20},{20,16},{9,13},{13,9},{17,21},{21,17},{10,14... | collective-permute-start | bytes 3145736 | tf_op jit(solution)/shard_map/ppermute | solution.py:545
  101.9 23.1 %collective-permute-start.21 = (f32[1024,256]{1,0:T(8,128)}, f32[1024,256]{1,0:T(8,128)}, u32[]{:S(2)}, u32[]{:S(2)}) collective-permute-start(f32[1024,256]{1,0:T(8,128)} %collective-permute-done.15.rest_5_), channel_id=1, source_target_pairs={{0,4},{4,0},{24,28},{28,24},{1,5},{5,1},{25,29},{29,25},{2,6},{6,2... | collective-permute-start | bytes 3145736 | tf_op jit(solution)/shard_map/ppermute | solution.py:545
  106.7 18.3 %collective-permute-start.22 = (f32[1024,256]{1,0:T(8,128)}, f32[1024,256]{1,0:T(8,128)}, u32[]{:S(2)}, u32[]{:S(2)}) collective-permute-start(f32[1024,256]{1,0:T(8,128)} %collective-permute-done.11.rest_1_), channel_id=1, source_target_pairs={{8,16},{12,20},{16,8},{20,12},{9,17},{13,21},{17,9},{21,13},{10,18... | collective-permute-start | bytes 3145736 | tf_op jit(solution)/shard_map/ppermute | solution.py:545
  112.1 40.0 %collective-permute-start.23 = (f32[2,256,512]{2,1,0:T(8,128)}, f32[2,256,512]{2,1,0:T(8,128)}, u32[]{:S(2)}, u32[]{:S(2)}) collective-permute-start(f32[2,256,512]{2,1,0:T(8,128)} %copy-done.11), channel_id=1, source_target_pairs={{0,2},{1,3},{2,0},{3,1},{4,6},{5,7},{6,4},{7,5},{8,10},{9,11},{10,... | collective-permute-start | bytes 3145736 | tf_op jit(solution)/shard_map/ppermute | solution.py:33
  125.0 27.1 %collective-permute-start.24 = (f32[1024,256]{1,0:T(8,128)}, f32[1024,256]{1,0:T(8,128)}, u32[]{:S(2)}, u32[]{:S(2)}) collective-permute-start(f32[1024,256]{1,0:T(8,128)} %copy-done.14), channel_id=1, source_target_pairs={{8,16},{12,20},{16,8},{20,12},{9,17},{13,21},{17,9},{21,13},{10,18... | collective-permute-start | bytes 3145736 | tf_op jit(solution)/shard_map/ppermute | solution.py:545
  126.7 30.8 %collective-permute-start.25 = (f32[1024,256]{1,0:T(8,128)}, f32[1024,256]{1,0:T(8,128)}, u32[]{:S(2)}, u32[]{:S(2)}) collective-permute-start(f32[1024,256]{1,0:T(8,128)} %collective-permute-done.22), channel_id=1, source_target_pairs={{8,0},{12,4},{16,24},{20,28},{9,1},{13,5},{17,25},{21,29},{10,2},{... | collective-permute-start | bytes 3145736 | tf_op jit(solution)/shard_map/ppermute | solution.py:545
  128.0 29.6 %collective-permute-start.26 = (f32[1024,256]{1,0:T(8,128)}, f32[1024,256]{1,0:T(8,128)}, u32[]{:S(2)}, u32[]{:S(2)}) collective-permute-start(f32[1024,256]{1,0:T(8,128)} %collective-permute-done.11.rest_1_), channel_id=1, source_target_pairs={{0,4},{4,0},{8,12},{12,8},{16,20},{20,16},{24,28},{28,24},{1,5},{5... | collective-permute-start | bytes 3145736 | tf_op jit(solution)/shard_map/ppermute | solution.py:545
  129.4 39.4 %collective-permute-start.27 = (f32[2,256,512]{2,1,0:T(8,128)}, f32[2,256,512]{2,1,0:T(8,128)}, u32[]{:S(2)}, u32[]{:S(2)}) collective-permute-start(f32[2,256,512]{2,1,0:T(8,128)} %copy-done.8), channel_id=1, source_target_pairs={{0,3},{1,2},{2,1},{3,0},{4,7},{5,6},{6,5},{7,4},{8,11},{9,10},{10,... | collective-permute-start | bytes 3145736 | tf_op jit(solution)/shard_map/ppermute | solution.py:33
  157.5 23.6 %collective-permute-start.28 = (f32[1024,256]{1,0:T(8,128)}, f32[1024,256]{1,0:T(8,128)}, u32[]{:S(2)}, u32[]{:S(2)}) collective-permute-start(f32[1024,256]{1,0:T(8,128)} %collective-permute-done.24.rest_4_), channel_id=1, source_target_pairs={{8,0},{12,4},{16,24},{20,28},{9,1},{13,5},{17,25},{21,29},{10,2},{... | collective-permute-start | bytes 3145736 | tf_op jit(solution)/shard_map/ppermute | solution.py:545
  158.8 22.3 %collective-permute-start.29 = (f32[1024,256]{1,0:T(8,128)}, f32[1024,256]{1,0:T(8,128)}, u32[]{:S(2)}, u32[]{:S(2)}) collective-permute-start(f32[1024,256]{1,0:T(8,128)} %collective-permute-done.22), channel_id=1, source_target_pairs={{8,12},{12,8},{16,20},{20,16},{9,13},{13,9},{17,21},{21,17},{10,14... | collective-permute-start | bytes 3145736 | tf_op jit(solution)/shard_map/ppermute | solution.py:545
  160.5 21.9 %collective-permute-start.30 = (f32[1024,256]{1,0:T(8,128)}, f32[1024,256]{1,0:T(8,128)}, u32[]{:S(2)}, u32[]{:S(2)}) collective-permute-start(f32[1024,256]{1,0:T(8,128)} %collective-permute-done.25.rest_5_), channel_id=1, source_target_pairs={{0,4},{4,0},{24,28},{28,24},{1,5},{5,1},{25,29},{29,25},{2,6},{6,2... | collective-permute-start | bytes 3145736 | tf_op jit(solution)/shard_map/ppermute | solution.py:545
  162.6 19.7 %collective-permute-start.31 = (f32[1024,256]{1,0:T(8,128)}, f32[1024,256]{1,0:T(8,128)}, u32[]{:S(2)}, u32[]{:S(2)}) collective-permute-start(f32[1024,256]{1,0:T(8,128)} %bitcast.3.rest_0_), channel_id=1, source_target_pairs={{8,16},{12,20},{16,8},{20,12},{9,17},{13,21},{17,9},{21,13},{10,18... | collective-permute-start | bytes 3145736 | tf_op jit(solution)/shard_map/ppermute | solution.py:545
  182.4 20.4 %collective-permute-start.32 = (f32[128,512]{1,0:T(8,128)S(1)}, f32[128,512]{1,0:T(8,128)S(1)}, u32[]{:S(2)}, u32[]{:S(2)}) collective-permute-start(f32[128,512]{1,0:T(8,128)S(1)} %constant_dynamic-slice_fusion.3), channel_id=1, source_target_pairs={{0,4},{4,0},{8,12},{12,8},{16,20},{20,16},{24,28},{28,24},{1,5},{5... | collective-permute-start | bytes 786440 | tf_op jit(solution)/shard_map/ppermute | solution.py:33
  202.8 12.5 %collective-permute-start.33 = (f32[128,512]{1,0:T(8,128)S(1)}, f32[128,512]{1,0:T(8,128)S(1)}, u32[]{:S(2)}, u32[]{:S(2)}) collective-permute-start(f32[128,512]{1,0:T(8,128)S(1)} %dynamic-slice_add_fusion.1), channel_id=1, source_target_pairs={{0,8},{4,12},{8,0},{12,4},{16,24},{20,28},{24,16},{28,20},{1,9},{5... | collective-permute-start | bytes 786440 | tf_op jit(solution)/shard_map/ppermute | solution.py:33
  211.3 11.8 %collective-permute-start.44 = (f32[128,512]{1,0:T(8,128)S(1)}, f32[128,512]{1,0:T(8,128)S(1)}, u32[]{:S(2)}, u32[]{:S(2)}) collective-permute-start(f32[128,512]{1,0:T(8,128)S(1)} %dynamic-slice_add_fusion), channel_id=1, source_target_pairs={{0,8},{4,12},{8,0},{12,4},{16,24},{20,28},{24,16},{28,20},{1,9},{5... | collective-permute-start | bytes 786440 | tf_op jit(solution)/shard_map/ppermute | solution.py:33
  215.3 9.5 %collective-permute-start.34 = (f32[128,512]{1,0:T(8,128)S(1)}, f32[128,512]{1,0:T(8,128)S(1)}, u32[]{:S(2)}, u32[]{:S(2)}) collective-permute-start(f32[128,512]{1,0:T(8,128)S(1)} %add.79), channel_id=1, source_target_pairs={{0,16},{4,20},{8,24},{12,28},{16,0},{20,4},{24,8},{28,12},{1,17},{... | collective-permute-start | bytes 786440 | tf_op jit(solution)/shard_map/ppermute | solution.py:33
  223.1 17.6 %collective-permute-start.45 = (f32[128,512]{1,0:T(8,128)S(1)}, f32[128,512]{1,0:T(8,128)S(1)}, u32[]{:S(2)}, u32[]{:S(2)}) collective-permute-start(f32[128,512]{1,0:T(8,128)S(1)} %add.85), channel_id=1, source_target_pairs={{0,16},{4,20},{8,24},{12,28},{16,0},{20,4},{24,8},{28,12},{1,17},{... | collective-permute-start | bytes 786440 | tf_op jit(solution)/shard_map/ppermute | solution.py:33
  224.9 19.0 %collective-permute-start.35 = (f32[128,512]{1,0:T(8,128)S(1)}, f32[128,512]{1,0:T(8,128)S(1)}, u32[]{:S(2)}, u32[]{:S(2)}) collective-permute-start(f32[128,512]{1,0:T(8,128)S(1)} %add.80), channel_id=1, source_target_pairs={{0,4},{4,0},{8,12},{12,8},{16,20},{20,16},{24,28},{28,24},{1,5},{5... | collective-permute-start | bytes 786440 | tf_op jit(solution)/shard_map/ppermute | solution.py:33
  240.7 11.0 %collective-permute-start.46 = (f32[128,512]{1,0:T(8,128)S(1)}, f32[128,512]{1,0:T(8,128)S(1)}, u32[]{:S(2)}, u32[]{:S(2)}) collective-permute-start(f32[128,512]{1,0:T(8,128)S(1)} %add.86), channel_id=1, source_target_pairs={{0,4},{4,0},{8,12},{12,8},{16,20},{20,16},{24,28},{28,24},{1,5},{5... | collective-permute-start | bytes 786440 | tf_op jit(solution)/shard_map/ppermute | solution.py:33
  251.6 9.5 %collective-permute-start.36 = (f32[128,128]{1,0:T(8,128)S(1)}, f32[128,128]{1,0:T(8,128)S(1)}, u32[]{:S(2)}, u32[]{:S(2)}) collective-permute-start(f32[128,128]{1,0:T(8,128)S(1)} %constant_dynamic-slice_fusion.2), channel_id=1, source_target_pairs={{0,4},{4,0},{8,12},{12,8},{16,20},{20,16},{24,28},{28,24},{1,5},{5... | collective-permute-start | bytes 196616 | tf_op jit(solution)/shard_map/ppermute | solution.py:33
  269.1 42.4 %collective-permute-start.55 = (f32[4,2,128,128]{3,2,1,0:T(8,128)S(1)}, f32[4,2,128,128]{3,2,1,0:T(8,128)S(1)}, u32[]{:S(2)}, u32[]{:S(2)}) collective-permute-start(f32[4,2,128,128]{3,2,1,0:T(8,128)S(1)} %get-tuple-element.224.refs_0_), channel_id=1, source_target_pairs={{0,2},{1,3},{2,0},{3,1},{4,6},{5,7},{6,4},{7,5},{8,10},{9,11},{10,... | collective-permute-start | bytes 1572872 | tf_op jit(solution)/shard_map/ppermute | solution.py:33
  273.0 39.0 %collective-permute-start.58 = (f32[4,2,128,128]{3,2,1,0:T(8,128)S(1)}, f32[4,2,128,128]{3,2,1,0:T(8,128)S(1)}, u32[]{:S(2)}, u32[]{:S(2)}) collective-permute-start(f32[4,2,128,128]{3,2,1,0:T(8,128)S(1)} %get-tuple-element.225.refs_4_), channel_id=1, source_target_pairs={{0,2},{1,3},{2,0},{3,1},{4,6},{5,7},{6,4},{7,5},{8,10},{9,11},{10,... | collective-permute-start | bytes 1572872 | tf_op jit(solution)/shard_map/ppermute | solution.py:33
  273.0 26.1 %collective-permute-start.50 = (f32[128,128]{1,0:T(8,128)S(1)}, f32[128,128]{1,0:T(8,128)S(1)}, u32[]{:S(2)}, u32[]{:S(2)}) collective-permute-start(f32[128,128]{1,0:T(8,128)S(1)} %add.89), channel_id=1, source_target_pairs={{0,4},{4,0},{8,12},{12,8},{16,20},{20,16},{24,28},{28,24},{1,5},{5... | collective-permute-start | bytes 196616 | tf_op jit(solution)/shard_map/ppermute | solution.py:33
  285.6 27.8 %collective-permute-start.40 = (f32[384,256]{1,0:T(8,128)S(1)}, f32[384,256]{1,0:T(8,128)S(1)}, u32[]{:S(2)}, u32[]{:S(2)}) collective-permute-start(f32[384,256]{1,0:T(8,128)S(1)} %get-tuple-element.204), channel_id=1, source_target_pairs={{0,1},{1,0},{2,3},{3,2},{4,5},{5,4},{6,7},{7,6},{8,9},{9,8},{10,11... | collective-permute-start | bytes 1179656 | tf_op jit(solution)/shard_map/ppermute | solution.py:33
  297.2 16.9 %collective-permute-start.41 = (f32[384,256]{1,0:T(8,128)S(1)}, f32[384,256]{1,0:T(8,128)S(1)}, u32[]{:S(2)}, u32[]{:S(2)}) collective-permute-start(f32[384,256]{1,0:T(8,128)S(1)} %get-tuple-element.205), channel_id=1, source_target_pairs={{0,2},{1,3},{2,0},{3,1},{4,6},{5,7},{6,4},{7,5},{8,10},{9,11},{10,... | collective-permute-start | bytes 1179656 | tf_op jit(solution)/shard_map/ppermute | solution.py:33
  299.1 18.0 %collective-permute-start.42 = (f32[384,256]{1,0:T(8,128)S(1)}, f32[384,256]{1,0:T(8,128)S(1)}, u32[]{:S(2)}, u32[]{:S(2)}) collective-permute-start(f32[384,256]{1,0:T(8,128)S(1)} %get-tuple-element.206), channel_id=1, source_target_pairs={{0,3},{1,2},{2,1},{3,0},{4,7},{5,6},{6,5},{7,4},{8,11},{9,10},{10,... | collective-permute-start | bytes 1179656 | tf_op jit(solution)/shard_map/ppermute | solution.py:33
  312.0 13.3 %collective-permute-start.52 = (f32[384,256]{1,0:T(8,128)S(1)}, f32[384,256]{1,0:T(8,128)S(1)}, u32[]{:S(2)}, u32[]{:S(2)}) collective-permute-start(f32[384,256]{1,0:T(8,128)S(1)} %get-tuple-element.221), channel_id=1, source_target_pairs={{0,2},{1,3},{2,0},{3,1},{4,6},{5,7},{6,4},{7,5},{8,10},{9,11},{10,... | collective-permute-start | bytes 1179656 | tf_op jit(solution)/shard_map/ppermute | solution.py:33
  313.5 25.3 %collective-permute-start.54 = (f32[4,2,128,128]{3,2,1,0:T(8,128)S(1)}, f32[4,2,128,128]{3,2,1,0:T(8,128)S(1)}, u32[]{:S(2)}, u32[]{:S(2)}) collective-permute-start(f32[4,2,128,128]{3,2,1,0:T(8,128)S(1)} %get-tuple-element.224.refs_0_), channel_id=1, source_target_pairs={{0,1},{1,0},{2,3},{3,2},{4,5},{5,4},{6,7},{7,6},{8,9},{9,8},{10,11... | collective-permute-start | bytes 1572872 | tf_op jit(solution)/shard_map/ppermute | solution.py:33
  314.1 24.6 %collective-permute-start.57 = (f32[4,2,128,128]{3,2,1,0:T(8,128)S(1)}, f32[4,2,128,128]{3,2,1,0:T(8,128)S(1)}, u32[]{:S(2)}, u32[]{:S(2)}) collective-permute-start(f32[4,2,128,128]{3,2,1,0:T(8,128)S(1)} %get-tuple-element.225.refs_4_), channel_id=1, source_target_pairs={{0,1},{1,0},{2,3},{3,2},{4,5},{5,4},{6,7},{7,6},{8,9},{9,8},{10,11... | collective-permute-start | bytes 1572872 | tf_op jit(solution)/shard_map/ppermute | solution.py:33
  317.1 21.6 %collective-permute-start.56 = (f32[4,2,128,128]{3,2,1,0:T(8,128)S(1)}, f32[4,2,128,128]{3,2,1,0:T(8,128)S(1)}, u32[]{:S(2)}, u32[]{:S(2)}) collective-permute-start(f32[4,2,128,128]{3,2,1,0:T(8,128)S(1)} %collective-permute-done.55.refs_2_), channel_id=1, source_target_pairs={{0,1},{1,0},{2,3},{3,2},{4,5},{5,4},{6,7},{7,6},{8,9},{9,8},{10,11... | collective-permute-start | bytes 1572872 | tf_op jit(solution)/shard_map/ppermute | solution.py:33
  317.3 21.4 %collective-permute-start.59 = (f32[4,2,128,128]{3,2,1,0:T(8,128)S(1)}, f32[4,2,128,128]{3,2,1,0:T(8,128)S(1)}, u32[]{:S(2)}, u32[]{:S(2)}) collective-permute-start(f32[4,2,128,128]{3,2,1,0:T(8,128)S(1)} %collective-permute-done.58.refs_6_), channel_id=1, source_target_pairs={{0,1},{1,0},{2,3},{3,2},{4,5},{5,4},{6,7},{7,6},{8,9},{9,8},{10,11... | collective-permute-start | bytes 1572872 | tf_op jit(solution)/shard_map/ppermute | solution.py:33
  325.3 11.4 %collective-permute-start.53 = (f32[384,256]{1,0:T(8,128)S(1)}, f32[384,256]{1,0:T(8,128)S(1)}, u32[]{:S(2)}, u32[]{:S(2)}) collective-permute-start(f32[384,256]{1,0:T(8,128)S(1)} %get-tuple-element.222), channel_id=1, source_target_pairs={{0,3},{1,2},{2,1},{3,0},{4,7},{5,6},{6,5},{7,4},{8,11},{9,10},{10,... | collective-permute-start | bytes 1179656 | tf_op jit(solution)/shard_map/ppermute | solution.py:33
  (29 other events, 267.5 us)

commit v3 on v2

--- a/solution.py
+++ b/solution.py
@@ -11,6 +11,8 @@
 GROUP = 128
 BAND = 24
 PANEL = 32
+AHEAD = 8
+TOGETHER = 4
 HALVED = 128
 
 F32 = jnp.float32
@@ -39,8 +41,11 @@
 
 
 def dot3(a, b, dims):
-    a_high, a_low = split(a)
-    b_high, b_low = split(b)
+    return dot3_parts(split(a), split(b), dims)
+
+
+def dot3_parts(a, b, dims):
+    (a_high, a_low), (b_high, b_low) = a, b
 
     def one(x, y):
         return lax.dot_general(x, y, (dims, ((), ())), preferred_element_type=F32)
@@ -82,16 +87,16 @@
     )(me, *[value] * len(ks), *after)
 
 
-def join_rows(value, layer, layers, received, me, c0, widths, parts):
+def join_rows(value, layer, layers, received, me, c0, width, parts, halves=False):
     rows = value.shape[1]
-    width = sum(widths)
+    types = [BF16, BF16] if halves else [value.dtype]
 
     def kernel(me_ref, *refs):
         for k in range(parts):
             at = c0 if k == 0 else 0
-            for out, w in zip(refs[parts:], widths):
-                out[0, aligned(me_ref[0] ^ k, rows), :] = refs[k][0, :, at:at + w]
-                at += w
+            piece = refs[k][0, :, at:at + width]
+            for out, x in zip(refs[parts:], split(piece) if halves else [piece]):
+                out[0, aligned(me_ref[0] ^ k, rows), :] = x
 
     return pl.pallas_call(
         kernel,
@@ -100,9 +105,9 @@
             grid=(layers,),
             in_specs=[column_spec(value, layer, parts, 0)]
             + [layer_spec(rows, width)] * (parts - 1),
-            out_specs=[layer_spec(rows * parts, w) for w in widths],
+            out_specs=[layer_spec(rows * parts, width)] * len(types),
         ),
-        out_shape=[jax.ShapeDtypeStruct((layers, rows * parts, w), value.dtype) for w in widths],
+        out_shape=[jax.ShapeDtypeStruct((layers, rows * parts, width), t) for t in types],
         compiler_params=params(),
         name="join_rows",
     )(me, value, *received)
@@ -148,13 +153,11 @@
     middle = lines([(1, 2), (2, 1)])
     to_ends = lines([(1, 0), (2, 3)])
     across = [(i, i ^ 1) for i in range(8)]
-    across_inner = [(i, i ^ 1) for i in (2, 3, 4, 5)]
-    across_ends = [(i, i ^ 1) for i in (0, 1, 6, 7)]
     return {
         "q1": ("own", outer), "y1": ("own", across), "q2": ("own", middle),
         "q3": ("q1", middle), "y2": ("q1", across), "q5": ("y1", middle),
-        "q4": ("q3", to_ends), "y3a": ("q3", across_inner),
-        "q6": ("q5", to_ends), "y3b": ("q4", across_ends),
+        "q4": ("q3", to_ends), "q6": ("q5", to_ends),
+        "y3": (("q3", "q4"), across),
     }
 
 
@@ -162,11 +165,11 @@
     (("q1", 0), ("y1", 0), ("q2", 0)),
     (("q3", 0), ("y2", 0), ("q1", 1)),
     (("q5", 0), ("q4", 0), ("y1", 1)),
-    (("q6", 0), ("y3a", 0), ("y3b", 0), ("q3", 1)),
+    (("q6", 0), ("y3", 0), ("q3", 1)),
     (("q5", 1), ("q4", 1), ("y2", 1)),
-    (("q6", 1), ("y3a", 1), ("y3b", 1), ("q2", 1)),
+    (("q6", 1), ("y3", 1), ("q2", 1)),
 )
-PLACES = (("own",), ("q1",), ("y1",), ("y2",), ("q5", "q4"), ("q2", "q6"), ("y3a", "y3b"))
+PLACES = (("own",), ("q1",), ("y1",), ("y2",), ("q5", "q4"), ("q2", "q6"), ("y3",))
 
 
 def load_window(pieces, counts, ends, raw, window, sems, block):
@@ -210,6 +213,7 @@
     @pl.when(step == 0)
     def _():
         load_window(pieces, counts, ends, raw, window, sems, block)
+        window[len(counts) * raw.shape[1] * 2:, :] = jnp.zeros((2 * block, raw.shape[2]), BF16)
 
     total = jnp.zeros((2 * block, raw.shape[2]), F32)
     for k in range(near):
@@ -221,11 +225,19 @@
 def group_specs(basis_rows, tile, g0, groups):
     specs, arrays = [], []
     for g in range(g0, g0 + groups):
-        for value in basis_rows:
-            for m in range(value.shape[0]):
-                specs.append(pl.BlockSpec((1, tile, GROUP), lambda i, m=m, g=g: (m, i, g)))
-                arrays.append(value)
+        for part in (0, 1):
+            for two in basis_rows:
+                for m in range(two[part].shape[0]):
+                    specs.append(pl.BlockSpec((1, tile, GROUP), lambda i, m=m, g=g: (m, i, g)))
+                    arrays.append(two[part])
     return specs, arrays
+
+
+def wide_parts(basis, orders, g):
+    at = 2 * orders * g
+    return [
+        jnp.concatenate([x[0] for x in basis[at + p * orders:at + (p + 1) * orders]], 1)
+        for p in (0, 1)]
 
 
 def apply(places, ends, strips, pieces):
@@ -242,7 +254,7 @@
         out_specs=pl.BlockSpec((block, width), lambda i: (i, 0)),
         scratch_shapes=[
             pltpu.VMEM((len(counts), rows, width), F32),
-            pltpu.VMEM((len(counts) * rows * 2, width), BF16),
+            pltpu.VMEM((len(counts) * rows * 2 + 2 * block, width), BF16),
             pltpu.SemaphoreType.DMA((len(counts),)),
         ],
         compiler_params=params(),
@@ -253,6 +265,94 @@
     )(places, ends, strips, *flat)
 
 
+def apply_late_kernel(counts, chosen, found, number, ends, begun, strips, *rest):
+    pieces = rest[:sum(counts)]
+    image, raw, window, held, total, sems, strip_sems = rest[sum(counts):]
+    row_blocks, room, block, _ = held.shape
+    rows, width = raw.shape[1], raw.shape[2]
+
+    def copy(i, j):
+        return pltpu.make_async_copy(strips.at[i, chosen[i, j]], held.at[i, j], strip_sems.at[i, j])
+
+    def each(i, do):
+        for j0 in range(0, room, TOGETHER):
+            @pl.when(j0 < number[i])
+            def _(j0=j0):
+                do(range(j0, j0 + TOGETHER))
+
+    def start(i, carry):
+        def do(js):
+            for j in js:
+                copy(i, j).start()
+
+        each(i, do)
+        return carry
+
+    lax.fori_loop(0, row_blocks, start, 0)
+    load_window(pieces, counts, ends, raw, window, sems, block)
+    window[len(counts) * rows * 2:, :] = jnp.zeros((2 * block, width), BF16)
+
+    def one(i, carry):
+        total[:block] = begun[aligned(i, block), :]
+        total[block:] = jnp.zeros((block, width), F32)
+
+        def do(js):
+            for j in js:
+                copy(i, j).wait()
+            left = jnp.concatenate([four_terms(held[i, j]) for j in js], 1)
+            right = jnp.concatenate(
+                [window[aligned(found[i, j], 2 * block), :] for j in js], 0)
+            total[...] += jnp.dot(left, right, preferred_element_type=F32)
+
+        each(i, do)
+        image[aligned(i, block), :] = total[:block] + total[block:]
+        return carry
+
+    lax.fori_loop(0, row_blocks, one, 0)
+
+
+def apply_late(listed, ends, strips, pieces, begun):
+    row_blocks, _, block, _ = strips.shape
+    rows, width = begun.shape
+    room = listed[0].shape[1]
+    counts = [len(p) for p in pieces]
+    flat = [x for p in pieces for x in p]
+    return pl.pallas_call(
+        functools.partial(apply_late_kernel, counts),
+        out_shape=jax.ShapeDtypeStruct((rows, width), F32),
+        in_specs=[SMEM] * 4 + [VMEM] + [ANY] * (1 + len(flat)),
+        out_specs=VMEM,
+        scratch_shapes=[
+            pltpu.VMEM((len(counts), rows, width), F32),
+            pltpu.VMEM((len(counts) * rows * 2 + 2 * block, width), BF16),
+            pltpu.VMEM((row_blocks, room, block, block), F32),
+            pltpu.VMEM((2 * block, width), F32),
+            pltpu.SemaphoreType.DMA((len(counts),)),
+            pltpu.SemaphoreType.DMA((row_blocks, room)),
+        ],
+        compiler_params=params(),
+        cost_estimate=pl.CostEstimate(
+            flops=4 * row_blocks * room * block * block * width,
+            bytes_accessed=8 * rows * width * 4, transcendentals=0),
+        name="apply_late",
+    )(*listed, ends, begun, strips, *flat)
+
+
+def list_late(place, inside, early, count, local_blocks):
+    near = place.shape[1]
+    most = min(near, (count - early) * local_blocks)
+    room = -(-most // TOGETHER) * TOGETHER
+    late = place >= early
+    number = jnp.sum(late, axis=1, dtype=jnp.int32)
+    rank = jnp.cumsum(late, axis=1, dtype=jnp.int32) - 1
+    slots = jnp.arange(room)
+    picked = (late & (slots[:, None, None] == rank)).astype(jnp.int32)
+    chosen = jnp.sum(picked * jnp.arange(near), axis=2, dtype=jnp.int32).T
+    found = jnp.sum(picked * ((place - early) * local_blocks + inside), axis=2, dtype=jnp.int32).T
+    found = jnp.where(slots < number[:, None], found, (count - early) * local_blocks)
+    return chosen, found, number
+
+
 def inner_kernel(orders, image, *rest):
     basis, partial = rest[:-1], rest[-1]
 
@@ -262,13 +362,13 @@
 
     for g in range(partial.shape[0]):
         cols = slice(g * GROUP, (g + 1) * GROUP)
-        wide = jnp.concatenate([basis[g * orders + m][0] for m in range(orders)], 1)
-        partial[g] += dot3(image[:, cols], wide, ((0,), (0,)))
+        partial[g] += dot3_parts(
+            split(image[:, cols]), wide_parts(basis, orders, g), ((0,), (0,)))
 
 
 def inner(image, at, basis_rows, g0, groups):
     rows, width = image.shape[0], groups * GROUP
-    orders = sum(x.shape[0] for x in basis_rows)
+    orders = sum(two[0].shape[0] for two in basis_rows)
     tile = rows // 4
     specs, arrays = group_specs(basis_rows, tile, g0, groups)
     shape = (groups, GROUP, orders * GROUP)
@@ -288,25 +388,23 @@
 
 def project_kernel(orders, image, coeffs_t, *rest):
     groups = coeffs_t.shape[0]
-    basis, (residual, gram, coeffs) = rest[:groups * orders], rest[groups * orders:]
+    basis, (residual, gram) = rest[:-2], rest[-2:]
 
     @pl.when(pl.program_id(0) == 0)
     def _():
         gram[...] = jnp.zeros_like(gram)
-        for g in range(groups):
-            for m in range(orders):
-                coeffs[m, g] = coeffs_t[g, :, m * GROUP:(m + 1) * GROUP].T
 
     for g in range(groups):
         cols = slice(g * GROUP, (g + 1) * GROUP)
-        wide = jnp.concatenate([basis[g * orders + m][0] for m in range(orders)], 1)
-        left = image[:, cols] - dot3(wide, coeffs_t[g], ((1,), (1,)))
+        left = image[:, cols] - dot3_parts(
+            wide_parts(basis, orders, g), split(coeffs_t[g]), ((1,), (1,)))
         residual[:, cols] = left
-        gram[g] += dot3(left, left, ((0,), (0,)))
+        parts = split(left)
+        gram[g] += dot3_parts(parts, parts, ((0,), (0,)))
 
 
 def project(image, at, basis_rows, coeffs_t, g0, groups):
-    orders = sum(x.shape[0] for x in basis_rows)
+    orders = sum(two[0].shape[0] for two in basis_rows)
     rows, width = image.shape[0], groups * GROUP
     tile = rows // 4
     specs, arrays = group_specs(basis_rows, tile, g0, groups)
@@ -316,7 +414,6 @@
         out_shape=[
             jax.ShapeDtypeStruct((rows, width), F32),
             jax.ShapeDtypeStruct((groups, GROUP, GROUP), F32),
-            jax.ShapeDtypeStruct((orders, groups, GROUP, GROUP), F32),
         ],
         in_specs=[
             pl.BlockSpec((tile, width), lambda i: (i, at // groups)),
@@ -325,7 +422,6 @@
         out_specs=[
             pl.BlockSpec((tile, width), lambda i: (i, 0)),
             pl.BlockSpec((groups, GROUP, GROUP), lambda i: (0, 0, 0)),
-            pl.BlockSpec((orders, groups, GROUP, GROUP), lambda i: (0, 0, 0, 0)),
         ],
         compiler_params=params(),
         cost_estimate=pl.CostEstimate(
@@ -343,24 +439,27 @@
     eye = jnp.where(row_at == col_at, 1.0, 0.0).astype(F32)
     rest = [jnp.concatenate([g, eye], 1) for g in gram]
     done = [[] for _ in gram]
-    panel_row = lax.broadcasted_iota(jnp.int32, (PANEL, 1), 0)
+    panel_row = lax.broadcasted_iota(jnp.int32, (PANEL, order), 0)
     for p0 in range(0, order, PANEL):
         panels = [r[:PANEL] for r in rest]
-        for j in range(PANEL):
-            for n in range(count):
-                panel = panels[n]
-                column = panel[:, p0 + j:p0 + j + 1]
-                pivot = column[j:j + 1]
-                factor = jnp.where(panel_row > j, column / pivot, 0.0)
-                panels[n] = panel - factor * panel[j:j + 1]
+        inverse_pivots = [[] for _ in gram]
+        for j0 in range(0, PANEL, AHEAD):
+            ahead = [
+                [jnp.broadcast_to(panel[:, p0 + j:p0 + j + 1], (PANEL, order))
+                 for j in range(j0, j0 + AHEAD)] for panel in panels]
+            for t in range(AHEAD):
+                j = j0 + t
+                for n in range(count):
+                    columns, panel = ahead[n], panels[n]
+                    inverse = 1.0 / columns[t][j:j + 1]
+                    factor = jnp.where(panel_row > j, columns[t] * inverse, 0.0)
+                    for u in range(t + 1, AHEAD):
+                        columns[u] = columns[u] - factor * columns[u][j:j + 1]
+                    panels[n] = panel - jnp.concatenate([factor, factor], 1) * panel[j:j + 1]
+                    inverse_pivots[n].append(inverse)
         for n in range(count):
-            panel = panels[n]
-            own = slice(p0, p0 + PANEL)
-            diagonal = jnp.sum(jnp.where(
-                lax.broadcasted_iota(jnp.int32, (PANEL, PANEL), 0)
-                == lax.broadcasted_iota(jnp.int32, (PANEL, PANEL), 1),
-                panel[:, own], 0.0), axis=1, keepdims=True)
-            panel = panel * lax.rsqrt(diagonal)
+            scale = jnp.sqrt(jnp.concatenate(inverse_pivots[n], 0))
+            panel = panels[n] * jnp.concatenate([scale, scale], 1)
             done[n].append(panel)
             if p0 + PANEL < order:
                 below = panel[:, p0 + PANEL:order]
@@ -375,6 +474,10 @@
     return lowers, inverses
 
 
+def with_factor(k):
+    return k < 2 or not k & 1
+
+
 def finish_kernel(groups, parts, me, gram, residual, *outs):
     lowers, inverses = eliminate([gram[g] for g in range(groups)])
     rows = residual.shape[0] // parts
@@ -383,16 +486,19 @@
             cols = slice(g * GROUP, (g + 1) * GROUP)
             left = residual[aligned(me[0] ^ k, rows), cols]
             outs[k][:rows, cols] = dot3(left, inverses[g], ((1,), (1,)))
-            outs[k][rows:, cols] = lowers[g]
+            if with_factor(k):
+                outs[k][rows:, cols] = lowers[g]
 
 
 def finish(me, gram, residual, parts):
     groups = gram.shape[0]
     rows, width = residual.shape
-    shape = jax.ShapeDtypeStruct((rows // parts + GROUP, width), F32)
+    shapes = [
+        jax.ShapeDtypeStruct((rows // parts + GROUP * with_factor(k), width), F32)
+        for k in range(parts)]
     return pl.pallas_call(
         functools.partial(finish_kernel, groups, parts),
-        out_shape=[shape] * parts,
+        out_shape=shapes,
         in_specs=[SMEM, VMEM, VMEM],
         out_specs=[VMEM] * parts,
         compiler_params=params(),
@@ -403,10 +509,11 @@
     )(me, gram, residual)
 
 
-def collect_blocks(me, blocks, chunks, new_shape, factor_shape, parts):
+def collect_blocks(me, blocks, factors, chunks, new_shape, factor_shape, parts):
     rows = new_shape[0]
     step = new_shape[1] // parts
     per_part = step // GROUP
+    alone = [(c, k) for c in range(len(chunks)) for k in range(parts) if not with_factor(k)]
 
     def kernel(me_ref, *refs):
         new_out, factor_out = refs[-2:]
@@ -414,20 +521,24 @@
             for k in range(parts):
                 src = refs[c * parts + k]
                 at = me_ref[0] ^ k
+                if (c, k) in alone:
+                    factor = refs[len(chunks) * parts + alone.index((c, k))]
+                else:
+                    factor = src.at[pl.ds(rows, GROUP), :]
                 for g in range(groups):
                     cols = slice(g * GROUP, (g + 1) * GROUP)
                     group = at * per_part + g0 + g
                     new_out[:, aligned(group, GROUP)] = src[:rows, cols]
-                    factor_out[group] = src[rows:, cols]
+                    factor_out[group] = factor[:, cols]
 
     return pl.pallas_call(
         kernel,
         out_shape=[jax.ShapeDtypeStruct(new_shape, F32), jax.ShapeDtypeStruct(factor_shape, F32)],
-        in_specs=[SMEM] + [VMEM] * (len(chunks) * parts),
+        in_specs=[SMEM] + [VMEM] * (len(chunks) * parts + len(alone)),
         out_specs=[VMEM] * 2,
         compiler_params=params(),
         name="collect_blocks",
-    )(me, *[x for c in blocks for x in c])
+    )(me, *[x for c in blocks for x in c], *[factors[c][k] for c, k in alone])
 
 
 def collect_coeffs(me, coeffs, chunks, shape, parts):
@@ -437,7 +548,9 @@
         for c, (g0, groups) in enumerate(chunks):
             for k in range(parts):
                 for g in range(groups):
-                    refs[-1][:, (me_ref[0] ^ k) * per_part + g0 + g] = refs[c * parts + k][:, g]
+                    for m in range(shape[0]):
+                        refs[-1][m, (me_ref[0] ^ k) * per_part + g0 + g] = (
+                            refs[c * parts + k][g, :, m * GROUP:(m + 1) * GROUP].T)
 
     return pl.pallas_call(
         kernel,
@@ -449,28 +562,34 @@
     )(me, *[x for c in coeffs for x in c])
 
 
-def sum_blk(value):
-    devices = lax.axis_size("blk")
-    half = value.shape[0] // 2
-    side = lax.axis_index("blk") % 2
-    long = value.shape[0] > HALVED
-    if long:
-        kept = lax.dynamic_slice_in_dim(value, side * half, half, 0)
-        sent = lax.dynamic_slice_in_dim(value, (1 - side) * half, half, 0)
-        value = kept + swap(sent, "blk", 1)
-    k = 2 if long else 1
-    while k < devices:
-        value = value + swap(value, "blk", k)
-        k *= 2
-    if long:
-        other = swap(value, "blk", 1)
-        value = jnp.concatenate(
-            [jnp.where(side == 0, value, other), jnp.where(side == 0, other, value)], 0)
-    return value
-
-
-def sum_groups(value):
-    return sum_blk(value.reshape(-1, value.shape[-1])).reshape(value.shape)
+class Sum:
+    def __init__(self, value):
+        self.shape = value.shape
+        self.value = value.reshape(-1, value.shape[-1])
+        self.side = lax.axis_index("blk") % 2
+        whole = [k for k in (1 << i for i in range(16)) if k < lax.axis_size("blk")]
+        long = self.value.shape[0] > HALVED and len(whole) > 1
+        self.steps = ["halve", *whole[1:], "join"] if long else whole
+
+    def step(self):
+        kind = self.steps.pop(0)
+        if kind == "halve":
+            half = self.value.shape[0] // 2
+            kept = lax.dynamic_slice_in_dim(self.value, self.side * half, half, 0)
+            sent = lax.dynamic_slice_in_dim(self.value, (1 - self.side) * half, half, 0)
+            self.value = kept + swap(sent, "blk", 1)
+        elif kind == "join":
+            other = swap(self.value, "blk", 1)
+            first = self.side == 0
+            self.value = jnp.concatenate(
+                [jnp.where(first, self.value, other), jnp.where(first, other, self.value)], 0)
+        else:
+            self.value = self.value + swap(self.value, "blk", kind)
+
+    def result(self):
+        while self.steps:
+            self.step()
+        return self.value.reshape(self.shape)
 
 
 def local(strips, near_cols, vector_block, basis):
@@ -493,6 +612,10 @@
     place = jnp.asarray(table)[blk][near_cols // local_blocks]
     inside = near_cols % local_blocks
     places = place * local_blocks + inside
+    count = int(table.max()) + 1
+    early = count - 2
+    early_places = jnp.where(place < early, places, early * local_blocks)
+    listed = list_late(place, inside, early, count, local_blocks)
     ends = jnp.where((blk < 2) | (blk >= devices - 2), 1, 0).astype(jnp.int32).reshape(1)
 
     vector = vector_block[None]
@@ -510,11 +633,11 @@
 
     def join(kind, at, value, layer, layers, c0, width):
         got = [values[kind, at, k] for k in others]
-        return join_rows(value, layer, layers, got, me, c0, [width], parts)[0]
+        return join_rows(value, layer, layers, got, me, c0, width, parts, kind == "b")
 
     def own_rows(c):
         c0, width = chunks[c][0] * GROUP, chunks[c][1] * GROUP
-        values["own", c] = join("v", c, vector, 0, 1, c0, width)[0]
+        values["own", c] = join("v", c, vector, 0, 1, c0, width)[0][0]
 
     for c, (g0, n) in enumerate(chunks):
         cut("v", c, vector, 0, 1, g0 * GROUP, n * GROUP)
@@ -527,39 +650,74 @@
         for key, x in zip(keys, lax.optimization_barrier(tuple(values[k] for k in keys))):
             values[key] = x
 
-    def window(c):
-        return [[values[n, c] for n in alternatives] for alternatives in PLACES]
+    def window(c, names=PLACES):
+        return [[values[n, c] for n in alternatives] for alternatives in names]
 
     for k in others:
         send(("v", 0, k))
     own_rows(0)
     if relayed:
         plan = relay_plan()
-        beside = {}
-        for h in range(len(layers)):
-            for k in others:
-                beside.setdefault(1 + h if k == 1 else 2 * h + k - 1, []).append(("b", h, k))
+        beside = {h: [("b", h, 1)] for h in range(len(layers))}
+        for i, (h, k) in enumerate((h, k) for h in range(len(layers)) for k in others if k > 1):
+            beside.setdefault(i, []).append(("b", h, k))
+        def join_basis(h):
+            values["high", h], values["low", h] = join("b", h, basis, *layers[h], 0, step)
+
+        def basis_parts():
+            return [(values["high", h], values["low", h]) for h in range(len(layers))]
+
+        def early_part(c):
+            values["begun", c] = apply(early_places, ends, strips, window(c, PLACES[:early]))
+
+        def late_part(c):
+            return apply_late(
+                listed, ends, strips, window(c, PLACES[early:]), values.pop(("begun", c)))
+
+        def early_part(c):
+            values["begun", c] = apply(early_places, ends, strips, window(c, PLACES[:early]))
+
+        def late_part(c):
+            values["image", c] = apply_late(
+                listed, ends, strips, window(c, PLACES[early:]), values.pop(("begun", c)))
+
+        def relay(name, c):
+            source, pairs = plan[name]
+            if isinstance(source, tuple):
+                value = jnp.where(ends[0] == 0, *[values[x, c] for x in source])
+            else:
+                value = values[source, c]
+            values[name, c] = lax.ppermute(value, "blk", pairs)
+
+        def add_step(running):
+            running.value = values["sum"]
+            running.step()
+            values["sum"] = running.value
+
         for r, relays in enumerate(ROUNDS):
+            flying = list(beside.get(r, ()))
             for name, c in relays:
-                source, pairs = plan[name]
-                values[name, c] = lax.ppermute(values[source, c], "blk", pairs)
+                relay(name, c)
             if r == 0:
                 for k in others:
                     send(("v", 1, k))
                 own_rows(1)
-            flying = beside.get(r, ())
             for key in flying:
                 send(key)
+            if r == 3:
+                join_basis(0)
             if r == 4:
+                for h in range(1, len(layers)):
+                    join_basis(h)
                 values["image", 0] = apply(places, ends, strips, window(0))
+                values["sum"] = inner(values["image", 0], 0, basis_parts(), *chunks[0])
             if r == 5:
-                basis_rows = [join("b", h, basis, m, n, 0, step) for h, (m, n) in enumerate(layers)]
-                for h, x in enumerate(basis_rows):
-                    values["basis", h] = x
-                values["partial", 0] = inner(values["image", 0], 0, basis_rows, *chunks[0])
-            barrier(flying if True else ())
-        basis_rows = [values["basis", h] for h in range(len(layers))]
-        values["image", 1] = apply(places, ends, strips, window(1))
+                first = Sum(values["sum"])
+                first.step()
+                values["sum"] = first.value
+                early_part(1)
+            barrier(flying)
+        basis_rows = basis_parts()
     else:
         for c in range(1, len(chunks)):
             for k in others:
@@ -577,30 +735,74 @@
                 pieces.append([lax.ppermute(own, "blk", pairs) if offset else own])
             values["image", c] = apply(places, ends, strips, pieces)
 
-    tail = [(0, 0, *chunks[0])]
-    if len(chunks) == 2:
-        tail += [(1, 0, *chunks[1])] if True else [
-            (1, g, chunks[1][0] + g, 1) for g in range(chunks[1][1])]
-    blocks, all_coeffs, made = [], [], []
-    for c, at, g0, n in tail:
-        if (c, at) == (0, 0) and ("partial", 0) in values:
-            part = values["partial", 0]
-        else:
-            part = inner(values["image", c], at, basis_rows, g0, n)
-        made.append(project(values["image", c], at, basis_rows, sum_groups(part), g0, n))
-    for (c, at, g0, n), (residual, gram, coeffs) in zip(tail, made):
-        across = [swap(coeffs, "rhs", k) for k in others if k > 1 and not k & 1]
-        both = [coeffs] + across
-        pair = [swap(x, "rhs", 1) for x in both]
-        all_coeffs.append([x for two in zip(both, pair) for x in two])
-        out = finish(me, sum_groups(gram), residual, parts)
-        blocks.append([out[0]] + [swap(out[k], "rhs", k) for k in others])
-    chunks = [(g0, n) for _, _, g0, n in tail]
+    def spread(value):
+        got = [value]
+        for k in (1 << i for i in range(16)):
+            if 1 < k < parts:
+                got += [swap(x, "rhs", k) for x in got]
+        pair = [swap(x, "rhs", 1) for x in got]
+        return [x for two in zip(got, pair) for x in two]
+
+    def tied(*xs):
+        return lax.optimization_barrier(tuple(xs))
+
+    def tie(*running):
+        for one, x in zip(running, tied(*[one.value for one in running])):
+            one.value = x
+
+    def projected(c, coeffs_t):
+        g0, n = chunks[c]
+        all_coeffs.append(spread(coeffs_t))
+        residual, gram = project(values["image", c], 0, basis_rows, coeffs_t, g0, n)
+        residuals.append(residual)
+        return Sum(gram)
+
+    all_coeffs, residuals, blocks = [], [], []
+    last = len(chunks) - 1
+    if relayed:
+        first.value = values["sum"]
+        first.step()
+        late_part(1)
+        first.value, values["image", 1] = tied(first.value, values["image", 1])
+        first.step()
+        second = Sum(inner(values["image", 1], 0, basis_rows, *chunks[1]))
+        second.step()
+        second.step()
+        first.step()
+        tie(first, second)
+        second.step()
+        grams = [projected(0, first.result())]
+        tie(second, grams[0])
+        second.step()
+        grams[0].step()
+        tie(second, grams[0])
+        grams.append(projected(1, second.result()))
+        grams[0].step()
+        tie(*grams)
+    else:
+        grams = [
+            projected(c, Sum(inner(values["image", c], 0, basis_rows, *chunks[c])).result())
+            for c in range(len(chunks))]
+    grams = [gram.result() for gram in grams]
+    held = [x for got in all_coeffs for x in got]
+    grams[-1], *held = tied(grams[-1], *held)
+    all_coeffs = [held[c * parts:(c + 1) * parts] for c in range(len(chunks))]
+    for residual, gram in zip(residuals, grams):
+        out = finish(me, gram, residual, parts)
+        got = [out[0]] + [swap(out[k], "rhs", k) for k in others]
+        blocks.append(got)
 
     coeffs = collect_coeffs(
         me, all_coeffs, chunks, (orders, total // GROUP, GROUP, GROUP), parts)
+    factors = []
+    for c, got in enumerate(blocks):
+        far = {k: got[k ^ 1][rows:] for k in others if not with_factor(k)}
+        if c == last and far:
+            k = max(far)
+            far[k], coeffs = tied(far[k], coeffs)
+        factors.append({k: swap(x, "rhs", 1) for k, x in far.items()})
     new_block, factor = collect_blocks(
-        me, blocks, chunks, (rows, total), (total // GROUP, GROUP, GROUP), parts)
+        me, blocks, factors, chunks, (rows, total), (total // GROUP, GROUP, GROUP), parts)
     return new_block, coeffs, factor
 
 

time: 344 us -> 316 us (0.919)
  starting transfers between devices: 106 us -> 81.8 us
  waiting for transfers between devices: 127 us -> 119 us
  other arithmetic: 0.52 us -> 7.18 us
  Pallas kernels: 95.4 us -> 91.3 us
    ppermute x20 -> x18, waiting for transfers between devices: 64.9 us -> 31.1 us  [relay(): values[name, c] = lax.ppermute(value, 'blk', pairs)]
    ppermute x40 -> x42, waiting for transfers between devices: 62.2 us -> 87.9 us  [swap(): return lax.ppermute(value, axis, pairs_of(axis, k))]
    ppermute x40 -> x42, starting transfers between devices: 71.8 us -> 55.9 us  [swap(): return lax.ppermute(value, axis, pairs_of(axis, k))]
    pallas_call x2, Pallas kernels: 24.8 us -> 10.2 us  [finish(): pl.pallas_call(functools.partial(finish_kernel, groups, parts), out_shape...]
    pallas_call x0 -> x1, Pallas kernels: none -> 9.75 us  [apply_late(): pl.pallas_call(functools.partial(apply_late_kernel, counts), out_shape=ja...]
    ppermute x20 -> x18, starting transfers between devices: 34.1 us -> 25.9 us  [relay(): values[name, c] = lax.ppermute(value, 'blk', pairs)]
    select_n x4 -> x8, other arithmetic: 0.11 us -> 3.95 us  [the longest x2 3.75 us: relay(): value = jnp.where(ends[0] == 0, *[values[x, c] for x in source])]
    unnamed x34 -> x48, local copies, waits for them, and re-layouts: 10 us -> 12 us
  transfers between devices with their start and end apart: 60 -> 60, of which waited for: 24 -> 23; matrix products, arithmetic and copies ran while one was open for 1% -> 3% of each run, Pallas kernels for 27% -> 28%
where the time goes in v3:
time: 316 us
  waiting for transfers between devices  119 us (38%)
  Pallas kernels  91.3 us (29%)
  starting transfers between devices  81.8 us (26%)
  local copies, waits for them, and re-layouts  15.1 us (5%)
  other arithmetic  7.18 us (2%)
    ppermute x42, waiting for transfers between devices, swap(): return lax.ppermute(value, axis, pairs_of(axis, k))  87.9 us
    ppermute x42, starting transfers between devices, swap(): return lax.ppermute(value, axis, pairs_of(axis, k))  55.9 us
    ppermute x18, waiting for transfers between devices, relay(): values[name, c] = lax.ppermute(value, 'blk', pairs)  31.1 us
    pallas_call x2, Pallas kernels, apply(): pl.pallas_call(functools.partial(apply_kernel, counts, near), grid=(row_b...  28.3 us
    ppermute x18, starting transfers between devices, relay(): values[name, c] = lax.ppermute(value, 'blk', pairs)  25.9 us
    pallas_call x2, Pallas kernels, project(): pl.pallas_call(functools.partial(project_kernel, orders), grid=(rows // t...  14.9 us
    unnamed x48, local copies, waits for them, and re-layouts  12 us
    pallas_call x2, Pallas kernels, finish(): pl.pallas_call(functools.partial(finish_kernel, groups, parts), out_shape...  10.2 us
  transfers between devices with their start and end apart: 60, of which 23 were waited for; matrix products, arithmetic and copies ran while one was open for 3% of the time, Pallas kernels for 28%

profile of v3, /device:TPU:1, one launch (start us, length us, event | category | flops | bytes accessed | tf_op | source)
XLA Modules:
  0.0 315.8 jit_solution(3998026837494422357)
XLA Ops:
  2.4 2.7 collective-permute-start.1
  5.1 6.5 %collective-permute-done.1.refs_2_ = f32[1,256,256]{2,1,0:T(8,128)S(1)} collective-permute-done((f32[1,256,256]{2,1,0:T(8,128)S(1)}, f32[1,256,256]{2,1,0:T(8,128)S(1)}, u32[]{:S(2)}, u32[]{:S(2)}) %collective-permute-start.1) | collective-permute-done | bytes 262176 | tf_op jit(solution)/shard_map/ppermute | solution.py:35
  11.7 5.6 %collective-permute-done.2.refs_3_ = f32[1,256,256]{2,1,0:T(8,128)S(1)} collective-permute-done((f32[1,256,256]{2,1,0:T(8,128)S(1)}, f32[1,256,256]{2,1,0:T(8,128)S(1)}, u32[]{:S(2)}, u32[]{:S(2)}) %collective-permute-start.2) | collective-permute-done | bytes 262176 | tf_op jit(solution)/shard_map/ppermute | solution.py:35
  24.5 2.7 cut_columns.6
  27.3 2.9 cut_columns.7
  32.2 3.7 %collective-permute-done.8.refs_3_ = f32[1,256,256]{2,1,0:T(8,128)S(1)} collective-permute-done((f32[1,256,256]{2,1,0:T(8,128)S(1)}, f32[1,256,256]{2,1,0:T(8,128)S(1)}, u32[]{:S(2)}, u32[]{:S(2)}) %collective-permute-start.8) | collective-permute-done | bytes 262176 | tf_op jit(solution)/shard_map/ppermute | solution.py:35
  38.2 3.8 %collective-permute-done.3.rest_1_ = f32[1024,256]{1,0:T(8,128)S(1)} collective-permute-done((f32[1024,256]{1,0:T(8,128)S(1)}, f32[1024,256]{1,0:T(8,128)S(1)}, u32[]{:S(2)}, u32[]{:S(2)}) %collective-permute-start.3) | collective-permute-done | bytes 1048608 | tf_op jit(solution)/shard_map/ppermute | solution.py:690
  47.1 4.6 %collective-permute-start.13 = (f32[1024,256]{1,0:T(8,128)}, f32[1024,256]{1,0:T(8,128)}, u32[]{:S(2)}, u32[]{:S(2)}) collective-permute-start(f32[1024,256]{1,0:T(8,128)} %bitcast.3.rest_0_), channel_id=1, source_target_pairs={{0,8},{4,12},{8,0},{12,4},{16,24},{20,28},{24,16},{28,20},{1,9},{5... | collective-permute-start | bytes 3145736 | tf_op jit(solution)/shard_map/ppermute | solution.py:690
  51.8 2.5 collective-permute-start.14
  54.3 6.6 %collective-permute-done.10.refs_2_ = f32[2,256,512]{2,1,0:T(8,128)S(1)} collective-permute-done((f32[2,256,512]{2,1,0:T(8,128)S(1)}, f32[2,256,512]{2,1,0:T(8,128)S(1)}, u32[]{:S(2)}, u32[]{:S(2)}) %collective-permute-start.10) | collective-permute-done | bytes 1048608 | tf_op jit(solution)/shard_map/ppermute | solution.py:35
  63.6 4.7 %collective-permute-done.12.rest_3_ = f32[1024,256]{1,0:T(8,128)S(1)} collective-permute-done((f32[1024,256]{1,0:T(8,128)S(1)}, f32[1024,256]{1,0:T(8,128)S(1)}, u32[]{:S(2)}, u32[]{:S(2)}) %collective-permute-start.12) | collective-permute-done | bytes 1048608 | tf_op jit(solution)/shard_map/ppermute | solution.py:690
  68.3 5.0 %collective-permute-done.13.rest_1_ = f32[1024,256]{1,0:T(8,128)} collective-permute-done((f32[1024,256]{1,0:T(8,128)}, f32[1024,256]{1,0:T(8,128)}, u32[]{:S(2)}, u32[]{:S(2)}) %collective-permute-start.13) | collective-permute-done | bytes 1048608 | tf_op jit(solution)/shard_map/ppermute | solution.py:690
  78.8 9.2 %collective-permute-done.15.refs_3_ = f32[2,256,512]{2,1,0:T(8,128)} collective-permute-done((f32[2,256,512]{2,1,0:T(8,128)}, f32[2,256,512]{2,1,0:T(8,128)}, u32[]{:S(2)}, u32[]{:S(2)}) %collective-permute-start.15) | collective-permute-done | bytes 1048608 | tf_op jit(solution)/shard_map/ppermute | solution.py:35
  88.0 11.0 %collective-permute-done.17.rest_5_ = f32[1024,256]{1,0:T(8,128)} collective-permute-done((f32[1024,256]{1,0:T(8,128)}, f32[1024,256]{1,0:T(8,128)}, u32[]{:S(2)}, u32[]{:S(2)}) %collective-permute-start.17) | collective-permute-done | bytes 1048608 | tf_op jit(solution)/shard_map/ppermute | solution.py:690
  100.2 2.4 broadcast_select_fusion.1
  105.6 5.2 %collective-permute-start.23 = (f32[2,256,512]{2,1,0:T(8,128)}, f32[2,256,512]{2,1,0:T(8,128)}, u32[]{:S(2)}, u32[]{:S(2)}) collective-permute-start(f32[2,256,512]{2,1,0:T(8,128)} %copy-done.16), channel_id=1, source_target_pairs={{0,3},{1,2},{2,1},{3,0},{4,7},{5,6},{6,5},{7,4},{8,11},{9,10},{10,... | collective-permute-start | bytes 3145736 | tf_op jit(solution)/shard_map/ppermute | solution.py:35
  111.5 1.9 gather_fusion
  114.9 3.5 %join_rows.6 = (bf16[2,1024,512]{2,1,0:T(8,128)(2,1)}, bf16[2,1024,512]{2,1,0:T(8,128)(2,1)}) custom-call(s32[1]{0:T(128)} %bitcast.me_ref.me, f32[4,256,2048]{2,1,0:T(8,128)} %refs_0_.7, f32[2,256,512]{2,1,0:T(8,128)S(1)} %collective-permute-done.9.refs_1_, f32[2,256,512]{2,1,0:T(8,128)S(1)} %copy-done.7, f32[2,256,512]{2,1,0:T(8,128)} %collective-permute-done.15.refs_3_), custom_call_target="tpu_custom_call" | custom-call | tf_op jit(solution)/shard_map/join_rows/pallas_call | solution.py:101
  118.5 3.6 %collective-permute-done.20.rest_7_ = f32[1024,256]{1,0:T(8,128)} collective-permute-done((f32[1024,256]{1,0:T(8,128)}, f32[1024,256]{1,0:T(8,128)}, u32[]{:S(2)}, u32[]{:S(2)}) %collective-permute-start.20) | collective-permute-done | bytes 1048608 | tf_op jit(solution)/shard_map/ppermute | solution.py:690
  129.0 6.1 %collective-permute-done.23.refs_3_ = f32[2,256,512]{2,1,0:T(8,128)} collective-permute-done((f32[2,256,512]{2,1,0:T(8,128)}, f32[2,256,512]{2,1,0:T(8,128)}, u32[]{:S(2)}, u32[]{:S(2)}) %collective-permute-start.23) | collective-permute-done | bytes 1048608 | tf_op jit(solution)/shard_map/ppermute | solution.py:35
  135.1 3.6 %join_rows.7 = (bf16[2,1024,512]{2,1,0:T(8,128)(2,1)}, bf16[2,1024,512]{2,1,0:T(8,128)(2,1)}) custom-call(s32[1]{0:T(128)} %bitcast.me_ref.me, f32[4,256,2048]{2,1,0:T(8,128)} %refs_0_.7, f32[2,256,512]{2,1,0:T(8,128)S(1)} %collective-permute-done.14.refs_1_, f32[2,256,512]{2,1,0:T(8,128)S(1)} %collective-permute-done.19.refs_2_, ...), custom_call_target="tpu_custom_call" | custom-call | tf_op jit(solution)/shard_map/join_rows/pallas_call | solution.py:101
  138.7 14.3 %apply.2.image = f32[1024,256]{1,0:T(8,128)S(1)} custom-call(s32[8,25]{1,0:T(8,128)S(1)} %get-tuple-element.262.places, s32[1]{0:T(128)} %bitcast.5.ends, f32[8,25,128,128]{3,2,1,0:T(8,128)} %strips.5, f32[1024,256]{1,0:T(8,128)S(1)} %bitcast.41, f32[1024,256]{1,0:T(8,128)S(1)} %copy-done.15, f32[1024,256]{1,0:T(8,128)} %collective-permute-done.4.rest_2_, ...), custom_call_target="tpu_custom_call" | custom-call | flops 6710886400 | bytes 21495808 | tf_op jit(solution)/shard_map/apply/pallas_call | solution.py:248
  153.0 4.2 %inner.2 = f32[2,128,512]{2,1,0:T(8,128)S(1)} custom-call(f32[1024,256]{1,0:T(8,128)S(1)} %apply.2.image, bf16[2,1024,512]{2,1,0:T(8,128)(2,1)S(1)} %copy-done, bf16[2,1024,512]{2,1,0:T(8,128)(2,1)S(1)} %copy-done, bf16[2,1024,512]{2,1,0:T(8,128)(2,1)} %get-tuple-element.222.rest_2_.rest_3_.rest_10_.rest_11_, ...), custom_call_target="tpu_custom_call" | custom-call | flops 805306368 | bytes 5242880 | tf_op jit(solution)/shard_map/inner/pallas_call | solution.py:375
  162.4 14.0 %apply.3.begun = f32[1024,256]{1,0:T(8,128)S(1)} custom-call(s32[8,25]{1,0:T(8,128)S(1)} %get-tuple-element.261.places, s32[1]{0:T(128)} %bitcast.5.ends, f32[8,25,128,128]{3,2,1,0:T(8,128)} %strips.5, f32[1024,256]{1,0:T(8,128)} %bitcast.3.rest_0_, f32[1024,256]{1,0:T(8,128)} %collective-permute-done.13.rest_1_, ...), custom_call_target="tpu_custom_call" | custom-call | flops 6710886400 | bytes 21495808 | tf_op jit(solution)/shard_map/apply/pallas_call | solution.py:248
  177.3 12.6 %collective-permute-done.27 = f32[128,512]{1,0:T(8,128)S(1)} collective-permute-done((f32[128,512]{1,0:T(8,128)S(1)}, f32[128,512]{1,0:T(8,128)S(1)}, u32[]{:S(2)}, u32[]{:S(2)}) %collective-permute-start.27) | collective-permute-done | bytes 262176 | tf_op jit(solution)/shard_map/ppermute | solution.py:35
  191.1 3.4 %collective-permute-start.31 = (f32[128,512]{1,0:T(8,128)S(1)}, f32[128,512]{1,0:T(8,128)}, u32[]{:S(2)}, u32[]{:S(2)}) collective-permute-start(f32[128,512]{1,0:T(8,128)S(1)} %dynamic-slice_add_fusion.1), channel_id=1, source_target_pairs={{0,8},{4,12},{8,0},{12,4},{16,24},{20,28},{24,16},{28,20},{1,9},{5... | collective-permute-start | bytes 786440 | tf_op jit(solution)/shard_map/ppermute | solution.py:35
  197.1 9.8 %apply_late.1.image = f32[1024,256]{1,0:T(8,128)S(1)} custom-call(s32[8,16]{1,0:T(8,128)S(1)} %bitcast.48, s32[8,16]{1,0:T(8,128)S(1)} %bitcast_select_fusion.found, s32[8]{0:T(128)S(1)} %convert_reduce_fusion.number, s32[1]{0:T(128)} %bitcast.5.ends, f32[1024,256]{1,0:T(8,128)S(1)} %copy-done.11, f32[8,25,128,128]{3,2,1,0:T(8,128)} %strips.5, ...), custom_call_target="tpu_custom_call" | custom-call | flops 2147483648 | bytes 8388608 | tf_op jit(solution)/shard_map/apply_late/pallas_call | solution.py:320
  208.9 3.8 %inner.3 = f32[2,128,512]{2,1,0:T(8,128)S(1)} custom-call(f32[1024,256]{1,0:T(8,128)S(1)} %apply_late.1.image, bf16[2,1024,512]{2,1,0:T(8,128)(2,1)S(1)} %copy-done, bf16[2,1024,512]{2,1,0:T(8,128)(2,1)S(1)} %copy-done, bf16[2,1024,512]{2,1,0:T(8,128)(2,1)} %get-tuple-element.222.rest_2_.rest_3_.rest_10_.rest_11_, ...), custom_call_target="tpu_custom_call" | custom-call | flops 805306368 | bytes 5242880 | tf_op jit(solution)/shard_map/inner/pallas_call | solution.py:375
  213.7 8.1 %collective-permute-done.32 = f32[128,512]{1,0:T(8,128)S(1)} collective-permute-done((f32[128,512]{1,0:T(8,128)S(1)}, f32[128,512]{1,0:T(8,128)S(1)}, u32[]{:S(2)}, u32[]{:S(2)}) %collective-permute-start.32) | collective-permute-done | bytes 262176 | tf_op jit(solution)/shard_map/ppermute | solution.py:35
  223.0 5.4 %collective-permute-done.33 = f32[128,512]{1,0:T(8,128)S(1)} collective-permute-done((f32[128,512]{1,0:T(8,128)S(1)}, f32[128,512]{1,0:T(8,128)S(1)}, u32[]{:S(2)}, u32[]{:S(2)}) %collective-permute-start.33) | collective-permute-done | bytes 262176 | tf_op jit(solution)/shard_map/ppermute | solution.py:35
  230.6 7.4 %project.2 = (f32[1024,256]{1,0:T(8,128)S(1)}, f32[2,128,128]{2,1,0:T(8,128)S(1)}) custom-call(f32[1024,256]{1,0:T(8,128)S(1)} %copy-done.4, f32[2,128,512]{2,1,0:T(8,128)S(1)} %bitcast.26, bf16[2,1024,512]{2,1,0:T(8,128)(2,1)} %get-tuple-element.221.rest_0_.rest_1_.rest_8_.rest_9_, bf16[2,1024,512]{2,1,0:T(8,128)(2,1)} %get-tuple-element.221.rest_0_.rest_1_.rest_8_.rest_9_, ...), custom_call_target="tpu_custom_call" | custom-call | flops 1006632960 | bytes 6291456 | tf_op jit(solution)/shard_map/project/pallas_call | solution.py:411
  238.0 5.6 %collective-permute-done.36 = f32[128,512]{1,0:T(8,128)S(1)} collective-permute-done((f32[128,512]{1,0:T(8,128)S(1)}, f32[128,512]{1,0:T(8,128)S(1)}, u32[]{:S(2)}, u32[]{:S(2)}) %collective-permute-start.36) | collective-permute-done | bytes 262176 | tf_op jit(solution)/shard_map/ppermute | solution.py:35
  246.9 5.9 %collective-permute-done.37 = f32[128,512]{1,0:T(8,128)S(1)} collective-permute-done((f32[128,512]{1,0:T(8,128)S(1)}, f32[128,512]{1,0:T(8,128)S(1)}, u32[]{:S(2)}, u32[]{:S(2)}) %collective-permute-start.37) | collective-permute-done | bytes 262176 | tf_op jit(solution)/shard_map/ppermute | solution.py:35
  253.0 7.5 %project.3 = (f32[1024,256]{1,0:T(8,128)S(1)}, f32[2,128,128]{2,1,0:T(8,128)S(1)}) custom-call(f32[1024,256]{1,0:T(8,128)S(1)} %apply_late.1.image, f32[2,128,512]{2,1,0:T(8,128)S(1)} %bitcast.31, bf16[2,1024,512]{2,1,0:T(8,128)(2,1)} %get-tuple-element.221.rest_0_.rest_1_.rest_8_.rest_9_, ...), custom_call_target="tpu_custom_call" | custom-call | flops 1006632960 | bytes 6291456 | tf_op jit(solution)/shard_map/project/pallas_call | solution.py:411
  262.1 3.1 collective-permute-start.40
  265.5 1.9 collective-permute-done.40
  267.7 2.8 collective-permute-start.49
  271.8 2.4 collective-permute-start.47
  274.2 2.8 collective-permute-start.54
  277.8 5.1 %finish.2 = (f32[384,256]{1,0:T(8,128)S(1)}, f32[384,256]{1,0:T(8,128)S(1)}, f32[384,256]{1,0:T(8,128)S(1)}, f32[256,256]{1,0:T(8,128)S(1)}) custom-call(s32[1]{0:T(128)} %bitcast.me_ref.me, f32[2,128,128]{2,1,0:T(8,128)S(1)} %bitcast.43, f32[1024,256]{1,0:T(8,128)S(1)} %get-tuple-element.235.residual), custom_call_target="tpu_custom_call" | custom-call | flops 201326592 | bytes 4194304 | tf_op jit(solution)/shard_map/finish/pallas_call | solution.py:499
  284.8 5.1 %finish.3 = (f32[384,256]{1,0:T(8,128)S(1)}, f32[384,256]{1,0:T(8,128)S(1)}, f32[384,256]{1,0:T(8,128)S(1)}, f32[256,256]{1,0:T(8,128)S(1)}) custom-call(s32[1]{0:T(128)} %bitcast.me_ref.me, f32[2,128,128]{2,1,0:T(8,128)S(1)} %bitcast.42, f32[1024,256]{1,0:T(8,128)S(1)} %get-tuple-element.242.residual), custom_call_target="tpu_custom_call" | custom-call | flops 201326592 | bytes 4194304 | tf_op jit(solution)/shard_map/finish/pallas_call | solution.py:499
  290.0 3.2 %collective-permute-start.42 = (f32[384,256]{1,0:T(8,128)S(1)}, f32[384,256]{1,0:T(8,128)S(1)}, u32[]{:S(2)}, u32[]{:S(2)}) collective-permute-start(f32[384,256]{1,0:T(8,128)S(1)} %get-tuple-element.237), channel_id=1, source_target_pairs={{0,1},{1,0},{2,3},{3,2},{4,5},{5,4},{6,7},{7,6},{8,9},{9,8},{10,11... | collective-permute-start | bytes 1179656 | tf_op jit(solution)/shard_map/ppermute | solution.py:35
  295.3 3.9 %collective-permute-start.57 = (f32[256,256]{1,0:T(8,128)S(1)}, f32[256,256]{1,0:T(8,128)S(1)}, u32[]{:S(2)}, u32[]{:S(2)}) collective-permute-start(f32[256,256]{1,0:T(8,128)S(1)} %get-tuple-element.246), channel_id=1, source_target_pairs={{0,3},{1,2},{2,1},{3,0},{4,7},{5,6},{6,5},{7,4},{8,11},{9,10},{10,... | collective-permute-start | bytes 786440 | tf_op jit(solution)/shard_map/ppermute | solution.py:35
  299.2 4.2 %collect_coeffs.1 = f32[4,16,128,128]{3,2,1,0:T(8,128)} custom-call(s32[1]{0:T(128)} %bitcast.me_ref.me, f32[2,128,512]{2,1,0:T(8,128)S(1)} %bitcast.29, f32[2,128,512]{2,1,0:T(8,128)S(1)} %collective-permute-done.49.refs_1_, f32[2,128,512]{2,1,0:T(8,128)S(1)} %collective-permute-done.50.refs_2_, f32[2,128,512]{2,1,0:T(8,128)S(1)} %collective-permute-done.51.refs_3_, ...), custom_call_target="tpu_custom_call" | custom-call | tf_op jit(solution)/shard_map/collect_coeffs/pallas_call | solution.py:555
  303.4 2.1 collective-permute-start.58
  305.6 4.9 %collective-permute-done.44.refs_3_ = f32[256,256]{1,0:T(8,128)S(1)} collective-permute-done((f32[256,256]{1,0:T(8,128)S(1)}, f32[256,256]{1,0:T(8,128)S(1)}, u32[]{:S(2)}, u32[]{:S(2)}) %collective-permute-start.44) | collective-permute-done | bytes 262176 | tf_op jit(solution)/shard_map/ppermute | solution.py:35
  310.9 2.9 collective-permute-done.57.refs_7_
  313.8 2.0 collect_blocks.1
  (187 shorter events, 68.1 us)
Async XLA Ops:
  2.4 9.3 %collective-permute-start.1 = (f32[1,256,256]{2,1,0:T(8,128)S(1)}, f32[1,256,256]{2,1,0:T(8,128)S(1)}, u32[]{:S(2)}, u32[]{:S(2)}) collective-permute-start(f32[1,256,256]{2,1,0:T(8,128)S(1)} %get-tuple-element.132), channel_id=1, source_target_pairs={{0,2},{1,3},{2,0},{3,1},{4,6},{5,7},{6,4},{7,5},{8,10},{9,11},{10,... | collective-permute-start | bytes 786440 | tf_op jit(solution)/shard_map/ppermute | solution.py:35
  5.1 12.2 %collective-permute-start.2 = (f32[1,256,256]{2,1,0:T(8,128)S(1)}, f32[1,256,256]{2,1,0:T(8,128)S(1)}, u32[]{:S(2)}, u32[]{:S(2)}) collective-permute-start(f32[1,256,256]{2,1,0:T(8,128)S(1)} %get-tuple-element.133), channel_id=1, source_target_pairs={{0,3},{1,2},{2,1},{3,0},{4,7},{5,6},{6,5},{7,4},{8,11},{9,10},{10,... | collective-permute-start | bytes 786440 | tf_op jit(solution)/shard_map/ppermute | solution.py:35
  17.4 24.7 %collective-permute-start.3 = (f32[1024,256]{1,0:T(8,128)S(1)}, f32[1024,256]{1,0:T(8,128)S(1)}, u32[]{:S(2)}, u32[]{:S(2)}) collective-permute-start(f32[1024,256]{1,0:T(8,128)S(1)} %bitcast.38), channel_id=1, source_target_pairs={{0,8},{4,12},{8,0},{12,4},{16,24},{20,28},{24,16},{28,20},{1,9},{5... | collective-permute-start | bytes 3145736 | tf_op jit(solution)/shard_map/ppermute | solution.py:690
  19.0 24.3 %collective-permute-start.4 = (f32[1024,256]{1,0:T(8,128)S(1)}, f32[1024,256]{1,0:T(8,128)}, u32[]{:S(2)}, u32[]{:S(2)}) collective-permute-start(f32[1024,256]{1,0:T(8,128)S(1)} %bitcast.39), channel_id=1, source_target_pairs={{0,4},{4,0},{8,12},{12,8},{16,20},{20,16},{24,28},{28,24},{1,5},{5... | collective-permute-start | bytes 3145736 | tf_op jit(solution)/shard_map/ppermute | solution.py:690
  20.2 23.1 %collective-permute-start.5 = (f32[1024,256]{1,0:T(8,128)S(1)}, f32[1024,256]{1,0:T(8,128)S(1)}, u32[]{:S(2)}, u32[]{:S(2)}) collective-permute-start(f32[1024,256]{1,0:T(8,128)S(1)} %bitcast.40), channel_id=1, source_target_pairs={{8,16},{12,20},{16,8},{20,12},{9,17},{13,21},{17,9},{21,13},{10,18... | collective-permute-start | bytes 3145736 | tf_op jit(solution)/shard_map/ppermute | solution.py:690
  21.9 10.2 %collective-permute-start.7 = (f32[1,256,256]{2,1,0:T(8,128)S(1)}, f32[1,256,256]{2,1,0:T(8,128)S(1)}, u32[]{:S(2)}, u32[]{:S(2)}) collective-permute-start(f32[1,256,256]{2,1,0:T(8,128)S(1)} %get-tuple-element.135), channel_id=1, source_target_pairs={{0,2},{1,3},{2,0},{3,1},{4,6},{5,7},{6,4},{7,5},{8,10},{9,11},{10,... | collective-permute-start | bytes 786440 | tf_op jit(solution)/shard_map/ppermute | solution.py:35
  23.1 12.8 %collective-permute-start.8 = (f32[1,256,256]{2,1,0:T(8,128)S(1)}, f32[1,256,256]{2,1,0:T(8,128)S(1)}, u32[]{:S(2)}, u32[]{:S(2)}) collective-permute-start(f32[1,256,256]{2,1,0:T(8,128)S(1)} %get-tuple-element.136), channel_id=1, source_target_pairs={{0,3},{1,2},{2,1},{3,0},{4,7},{5,6},{6,5},{7,4},{8,11},{9,10},{10,... | collective-permute-start | bytes 786440 | tf_op jit(solution)/shard_map/ppermute | solution.py:35
  32.1 19.7 %collective-permute-start.9 = (f32[2,256,512]{2,1,0:T(8,128)S(1)}, f32[2,256,512]{2,1,0:T(8,128)S(1)}, u32[]{:S(2)}, u32[]{:S(2)}) collective-permute-start(f32[2,256,512]{2,1,0:T(8,128)S(1)} %get-tuple-element.137), channel_id=1, source_target_pairs={{0,1},{1,0},{2,3},{3,2},{4,5},{5,4},{6,7},{7,6},{8,9},{9,8},{10,11... | collective-permute-start | bytes 3145736 | tf_op jit(solution)/shard_map/ppermute | solution.py:35
  35.9 25.0 %collective-permute-start.10 = (f32[2,256,512]{2,1,0:T(8,128)S(1)}, f32[2,256,512]{2,1,0:T(8,128)S(1)}, u32[]{:S(2)}, u32[]{:S(2)}) collective-permute-start(f32[2,256,512]{2,1,0:T(8,128)S(1)} %get-tuple-element.138), channel_id=1, source_target_pairs={{0,2},{1,3},{2,0},{3,1},{4,6},{5,7},{6,4},{7,5},{8,10},{9,11},{10,... | collective-permute-start | bytes 3145736 | tf_op jit(solution)/shard_map/ppermute | solution.py:35
  43.3 20.3 %collective-permute-start.11 = (f32[1024,256]{1,0:T(8,128)S(1)}, f32[1024,256]{1,0:T(8,128)}, u32[]{:S(2)}, u32[]{:S(2)}) collective-permute-start(f32[1024,256]{1,0:T(8,128)S(1)} %collective-permute-done.3.rest_1_), channel_id=1, source_target_pairs={{8,16},{12,20},{16,8},{20,12},{9,17},{13,21},{17,9},{21,13},{10,18... | collective-permute-start | bytes 3145736 | tf_op jit(solution)/shard_map/ppermute | solution.py:690
  44.9 23.4 %collective-permute-start.12 = (f32[1024,256]{1,0:T(8,128)S(1)}, f32[1024,256]{1,0:T(8,128)S(1)}, u32[]{:S(2)}, u32[]{:S(2)}) collective-permute-start(f32[1024,256]{1,0:T(8,128)S(1)} %collective-permute-done.3.rest_1_), channel_id=1, source_target_pairs={{0,4},{4,0},{8,12},{12,8},{16,20},{20,16},{24,28},{28,24},{1,5},{5... | collective-permute-start | bytes 3145736 | tf_op jit(solution)/shard_map/ppermute | solution.py:690
  47.1 26.2 %collective-permute-start.13 = (f32[1024,256]{1,0:T(8,128)}, f32[1024,256]{1,0:T(8,128)}, u32[]{:S(2)}, u32[]{:S(2)}) collective-permute-start(f32[1024,256]{1,0:T(8,128)} %bitcast.3.rest_0_), channel_id=1, source_target_pairs={{0,8},{4,12},{8,0},{12,4},{16,24},{20,28},{24,16},{28,20},{1,9},{5... | collective-permute-start | bytes 3145736 | tf_op jit(solution)/shard_map/ppermute | solution.py:690
  51.8 25.8 %collective-permute-start.14 = (f32[2,256,512]{2,1,0:T(8,128)}, f32[2,256,512]{2,1,0:T(8,128)S(1)}, u32[]{:S(2)}, u32[]{:S(2)}) collective-permute-start(f32[2,256,512]{2,1,0:T(8,128)} %get-tuple-element.144), channel_id=1, source_target_pairs={{0,1},{1,0},{2,3},{3,2},{4,5},{5,4},{6,7},{7,6},{8,9},{9,8},{10,11... | collective-permute-start | bytes 3145736 | tf_op jit(solution)/shard_map/ppermute | solution.py:35
  61.9 26.1 %collective-permute-start.15 = (f32[2,256,512]{2,1,0:T(8,128)}, f32[2,256,512]{2,1,0:T(8,128)}, u32[]{:S(2)}, u32[]{:S(2)}) collective-permute-start(f32[2,256,512]{2,1,0:T(8,128)} %get-tuple-element.143), channel_id=1, source_target_pairs={{0,3},{1,2},{2,1},{3,0},{4,7},{5,6},{6,5},{7,4},{8,11},{9,10},{10,... | collective-permute-start | bytes 3145736 | tf_op jit(solution)/shard_map/ppermute | solution.py:35
  73.3 14.7 %collective-permute-start.16 = (f32[1024,256]{1,0:T(8,128)}, f32[1024,256]{1,0:T(8,128)}, u32[]{:S(2)}, u32[]{:S(2)}) collective-permute-start(f32[1024,256]{1,0:T(8,128)} %collective-permute-done.4.rest_2_), channel_id=1, source_target_pairs={{8,16},{12,20},{16,8},{20,12},{9,17},{13,21},{17,9},{21,13},{10,18... | collective-permute-start | bytes 3145736 | tf_op jit(solution)/shard_map/ppermute | solution.py:690
  75.0 24.0 %collective-permute-start.17 = (f32[1024,256]{1,0:T(8,128)}, f32[1024,256]{1,0:T(8,128)}, u32[]{:S(2)}, u32[]{:S(2)}) collective-permute-start(f32[1024,256]{1,0:T(8,128)} %collective-permute-done.11), channel_id=1, source_target_pairs={{8,0},{12,4},{16,24},{20,28},{9,1},{13,5},{17,25},{21,29},{10,2},{... | collective-permute-start | bytes 3145736 | tf_op jit(solution)/shard_map/ppermute | solution.py:690
  76.3 22.7 %collective-permute-start.18 = (f32[1024,256]{1,0:T(8,128)}, f32[1024,256]{1,0:T(8,128)}, u32[]{:S(2)}, u32[]{:S(2)}) collective-permute-start(f32[1024,256]{1,0:T(8,128)} %bitcast.3.rest_0_), channel_id=1, source_target_pairs={{0,4},{4,0},{8,12},{12,8},{16,20},{20,16},{24,28},{28,24},{1,5},{5... | collective-permute-start | bytes 3145736 | tf_op jit(solution)/shard_map/ppermute | solution.py:690
  77.6 40.9 %collective-permute-start.19 = (f32[2,256,512]{2,1,0:T(8,128)}, f32[2,256,512]{2,1,0:T(8,128)S(1)}, u32[]{:S(2)}, u32[]{:S(2)}) collective-permute-start(f32[2,256,512]{2,1,0:T(8,128)} %copy-done.17), channel_id=1, source_target_pairs={{0,2},{1,3},{2,0},{3,1},{4,6},{5,7},{6,4},{7,5},{8,10},{9,11},{10,... | collective-permute-start | bytes 3145736 | tf_op jit(solution)/shard_map/ppermute | solution.py:35
  99.0 23.1 %collective-permute-start.20 = (f32[1024,256]{1,0:T(8,128)}, f32[1024,256]{1,0:T(8,128)}, u32[]{:S(2)}, u32[]{:S(2)}) collective-permute-start(f32[1024,256]{1,0:T(8,128)} %collective-permute-done.16.rest_4_), channel_id=1, source_target_pairs={{8,0},{12,4},{16,24},{20,28},{9,1},{13,5},{17,25},{21,29},{10,2},{... | collective-permute-start | bytes 3145736 | tf_op jit(solution)/shard_map/ppermute | solution.py:690
  102.6 21.2 %collective-permute-start.21 = (f32[1024,256]{1,0:T(8,128)}, f32[1024,256]{1,0:T(8,128)}, u32[]{:S(2)}, u32[]{:S(2)}) collective-permute-start(f32[1024,256]{1,0:T(8,128)} %broadcast_select_fusion.1), channel_id=1, source_target_pairs={{0,4},{4,0},{8,12},{12,8},{16,20},{20,16},{24,28},{28,24},{1,5},{5... | collective-permute-start | bytes 3145736 | tf_op jit(solution)/shard_map/ppermute | solution.py:690
  103.9 19.9 %collective-permute-start.22 = (f32[1024,256]{1,0:T(8,128)}, f32[1024,256]{1,0:T(8,128)}, u32[]{:S(2)}, u32[]{:S(2)}) collective-permute-start(f32[1024,256]{1,0:T(8,128)} %collective-permute-done.13.rest_1_), channel_id=1, source_target_pairs={{8,16},{12,20},{16,8},{20,12},{9,17},{13,21},{17,9},{21,13},{10,18... | collective-permute-start | bytes 3145736 | tf_op jit(solution)/shard_map/ppermute | solution.py:690
  105.6 29.5 %collective-permute-start.23 = (f32[2,256,512]{2,1,0:T(8,128)}, f32[2,256,512]{2,1,0:T(8,128)}, u32[]{:S(2)}, u32[]{:S(2)}) collective-permute-start(f32[2,256,512]{2,1,0:T(8,128)} %copy-done.16), channel_id=1, source_target_pairs={{0,3},{1,2},{2,1},{3,0},{4,7},{5,6},{6,5},{7,4},{8,11},{9,10},{10,... | collective-permute-start | bytes 3145736 | tf_op jit(solution)/shard_map/ppermute | solution.py:35
  123.8 33.4 %collective-permute-start.24 = (f32[1024,256]{1,0:T(8,128)}, f32[1024,256]{1,0:T(8,128)}, u32[]{:S(2)}, u32[]{:S(2)}) collective-permute-start(f32[1024,256]{1,0:T(8,128)} %collective-permute-done.18.rest_2_), channel_id=1, source_target_pairs={{8,16},{12,20},{16,8},{20,12},{9,17},{13,21},{17,9},{21,13},{10,18... | collective-permute-start | bytes 3145736 | tf_op jit(solution)/shard_map/ppermute | solution.py:690
  125.4 31.8 %collective-permute-start.25 = (f32[1024,256]{1,0:T(8,128)}, f32[1024,256]{1,0:T(8,128)}, u32[]{:S(2)}, u32[]{:S(2)}) collective-permute-start(f32[1024,256]{1,0:T(8,128)} %collective-permute-done.22), channel_id=1, source_target_pairs={{8,0},{12,4},{16,24},{20,28},{9,1},{13,5},{17,25},{21,29},{10,2},{... | collective-permute-start | bytes 3145736 | tf_op jit(solution)/shard_map/ppermute | solution.py:690
  126.7 30.5 %collective-permute-start.26 = (f32[1024,256]{1,0:T(8,128)}, f32[1024,256]{1,0:T(8,128)}, u32[]{:S(2)}, u32[]{:S(2)}) collective-permute-start(f32[1024,256]{1,0:T(8,128)} %collective-permute-done.13.rest_1_), channel_id=1, source_target_pairs={{0,4},{4,0},{8,12},{12,8},{16,20},{20,16},{24,28},{28,24},{1,5},{5... | collective-permute-start | bytes 3145736 | tf_op jit(solution)/shard_map/ppermute | solution.py:690
  157.2 32.8 %collective-permute-start.28 = (f32[1024,256]{1,0:T(8,128)}, f32[1024,256]{1,0:T(8,128)S(1)}, u32[]{:S(2)}, u32[]{:S(2)}) collective-permute-start(f32[1024,256]{1,0:T(8,128)} %collective-permute-done.24.rest_4_), channel_id=1, source_target_pairs={{8,0},{12,4},{16,24},{20,28},{9,1},{13,5},{17,25},{21,29},{10,2},{... | collective-permute-start | bytes 3145736 | tf_op jit(solution)/shard_map/ppermute | solution.py:690
  159.9 30.2 %collective-permute-start.29 = (f32[1024,256]{1,0:T(8,128)S(1)}, f32[1024,256]{1,0:T(8,128)S(1)}, u32[]{:S(2)}, u32[]{:S(2)}) collective-permute-start(f32[1024,256]{1,0:T(8,128)S(1)} %broadcast_select_fusion), channel_id=1, source_target_pairs={{0,4},{4,0},{8,12},{12,8},{16,20},{20,16},{24,28},{28,24},{1,5},{5... | collective-permute-start | bytes 3145736 | tf_op jit(solution)/shard_map/ppermute | solution.py:690
  160.2 29.9 %collective-permute-start.30 = (f32[1024,256]{1,0:T(8,128)}, f32[1024,256]{1,0:T(8,128)S(1)}, u32[]{:S(2)}, u32[]{:S(2)}) collective-permute-start(f32[1024,256]{1,0:T(8,128)} %bitcast.3.rest_0_), channel_id=1, source_target_pairs={{8,16},{12,20},{16,8},{20,12},{9,17},{13,21},{17,9},{21,13},{10,18... | collective-permute-start | bytes 3145736 | tf_op jit(solution)/shard_map/ppermute | solution.py:690
  161.0 29.0 %collective-permute-start.27 = (f32[128,512]{1,0:T(8,128)S(1)}, f32[128,512]{1,0:T(8,128)S(1)}, u32[]{:S(2)}, u32[]{:S(2)}) collective-permute-start(f32[128,512]{1,0:T(8,128)S(1)} %constant_dynamic-slice_fusion.3), channel_id=1, source_target_pairs={{0,4},{4,0},{8,12},{12,8},{16,20},{20,16},{24,28},{28,24},{1,5},{5... | collective-permute-start | bytes 786440 | tf_op jit(solution)/shard_map/ppermute | solution.py:35
  191.1 15.8 %collective-permute-start.31 = (f32[128,512]{1,0:T(8,128)S(1)}, f32[128,512]{1,0:T(8,128)}, u32[]{:S(2)}, u32[]{:S(2)}) collective-permute-start(f32[128,512]{1,0:T(8,128)S(1)} %dynamic-slice_add_fusion.1), channel_id=1, source_target_pairs={{0,8},{4,12},{8,0},{12,4},{16,24},{20,28},{24,16},{28,20},{1,9},{5... | collective-permute-start | bytes 786440 | tf_op jit(solution)/shard_map/ppermute | solution.py:35
  207.9 14.0 %collective-permute-start.32 = (f32[128,512]{1,0:T(8,128)S(1)}, f32[128,512]{1,0:T(8,128)S(1)}, u32[]{:S(2)}, u32[]{:S(2)}) collective-permute-start(f32[128,512]{1,0:T(8,128)S(1)} %add.88), channel_id=1, source_target_pairs={{0,16},{4,20},{8,24},{12,28},{16,0},{20,4},{24,8},{28,12},{1,17},{... | collective-permute-start | bytes 786440 | tf_op jit(solution)/shard_map/ppermute | solution.py:35
  213.6 8.3 %collective-permute-start.34 = (f32[128,512]{1,0:T(8,128)S(1)}, f32[128,512]{1,0:T(8,128)S(1)}, u32[]{:S(2)}, u32[]{:S(2)}) collective-permute-start(f32[128,512]{1,0:T(8,128)S(1)} %constant_dynamic-slice_fusion.1), channel_id=1, source_target_pairs={{0,4},{4,0},{8,12},{12,8},{16,20},{20,16},{24,28},{28,24},{1,5},{5... | collective-permute-start | bytes 786440 | tf_op jit(solution)/shard_map/ppermute | solution.py:35
  229.5 14.2 %collective-permute-start.36 = (f32[128,512]{1,0:T(8,128)S(1)}, f32[128,512]{1,0:T(8,128)S(1)}, u32[]{:S(2)}, u32[]{:S(2)}) collective-permute-start(f32[128,512]{1,0:T(8,128)S(1)} %add.92), channel_id=1, source_target_pairs={{0,16},{4,20},{8,24},{12,28},{16,0},{20,4},{24,8},{28,12},{1,17},{... | collective-permute-start | bytes 786440 | tf_op jit(solution)/shard_map/ppermute | solution.py:35
  245.0 7.8 %collective-permute-start.37 = (f32[128,512]{1,0:T(8,128)S(1)}, f32[128,512]{1,0:T(8,128)S(1)}, u32[]{:S(2)}, u32[]{:S(2)}) collective-permute-start(f32[128,512]{1,0:T(8,128)S(1)} %add.93), channel_id=1, source_target_pairs={{0,4},{4,0},{8,12},{12,8},{16,20},{20,16},{24,28},{28,24},{1,5},{5... | collective-permute-start | bytes 786440 | tf_op jit(solution)/shard_map/ppermute | solution.py:35
  245.3 25.3 %collective-permute-start.50 = (f32[2,128,512]{2,1,0:T(8,128)S(1)}, f32[2,128,512]{2,1,0:T(8,128)S(1)}, u32[]{:S(2)}, u32[]{:S(2)}) collective-permute-start(f32[2,128,512]{2,1,0:T(8,128)S(1)} %bitcast.27), channel_id=1, source_target_pairs={{0,2},{1,3},{2,0},{3,1},{4,6},{5,7},{6,4},{7,5},{8,10},{9,11},{10,... | collective-permute-start | bytes 1572872 | tf_op jit(solution)/shard_map/ppermute | solution.py:35
  252.9 7.6 %collective-permute-start.39 = (f32[128,128]{1,0:T(8,128)S(1)}, f32[128,128]{1,0:T(8,128)S(1)}, u32[]{:S(2)}, u32[]{:S(2)}) collective-permute-start(f32[128,128]{1,0:T(8,128)S(1)} %dynamic-slice_add_fusion.3), channel_id=1, source_target_pairs={{0,8},{4,12},{8,0},{12,4},{16,24},{20,28},{24,16},{28,20},{1,9},{5... | collective-permute-start | bytes 196616 | tf_op jit(solution)/shard_map/ppermute | solution.py:35
  253.0 21.2 %collective-permute-start.53 = (f32[2,128,512]{2,1,0:T(8,128)S(1)}, f32[2,128,512]{2,1,0:T(8,128)S(1)}, u32[]{:S(2)}, u32[]{:S(2)}) collective-permute-start(f32[2,128,512]{2,1,0:T(8,128)S(1)} %bitcast.30), channel_id=1, source_target_pairs={{0,2},{1,3},{2,0},{3,1},{4,6},{5,7},{6,4},{7,5},{8,10},{9,11},{10,... | collective-permute-start | bytes 1572872 | tf_op jit(solution)/shard_map/ppermute | solution.py:35
  267.7 17.0 %collective-permute-start.49 = (f32[2,128,512]{2,1,0:T(8,128)S(1)}, f32[2,128,512]{2,1,0:T(8,128)S(1)}, u32[]{:S(2)}, u32[]{:S(2)}) collective-permute-start(f32[2,128,512]{2,1,0:T(8,128)S(1)} %bitcast.28), channel_id=1, source_target_pairs={{0,1},{1,0},{2,3},{3,2},{4,5},{5,4},{6,7},{7,6},{8,9},{9,8},{10,11... | collective-permute-start | bytes 1572872 | tf_op jit(solution)/shard_map/ppermute | solution.py:35
  270.5 14.2 %collective-permute-start.52 = (f32[2,128,512]{2,1,0:T(8,128)S(1)}, f32[2,128,512]{2,1,0:T(8,128)S(1)}, u32[]{:S(2)}, u32[]{:S(2)}) collective-permute-start(f32[2,128,512]{2,1,0:T(8,128)S(1)} %bitcast.32), channel_id=1, source_target_pairs={{0,1},{1,0},{2,3},{3,2},{4,5},{5,4},{6,7},{7,6},{8,9},{9,8},{10,11... | collective-permute-start | bytes 1572872 | tf_op jit(solution)/shard_map/ppermute | solution.py:35
  270.6 14.1 %collective-permute-start.51 = (f32[2,128,512]{2,1,0:T(8,128)S(1)}, f32[2,128,512]{2,1,0:T(8,128)S(1)}, u32[]{:S(2)}, u32[]{:S(2)}) collective-permute-start(f32[2,128,512]{2,1,0:T(8,128)S(1)} %collective-permute-done.50.refs_2_), channel_id=1, source_target_pairs={{0,1},{1,0},{2,3},{3,2},{4,5},{5,4},{6,7},{7,6},{8,9},{9,8},{10,11... | collective-permute-start | bytes 1572872 | tf_op jit(solution)/shard_map/ppermute | solution.py:35
  274.2 10.6 %collective-permute-start.54 = (f32[2,128,512]{2,1,0:T(8,128)S(1)}, f32[2,128,512]{2,1,0:T(8,128)S(1)}, u32[]{:S(2)}, u32[]{:S(2)}) collective-permute-start(f32[2,128,512]{2,1,0:T(8,128)S(1)} %collective-permute-done.53.refs_6_), channel_id=1, source_target_pairs={{0,1},{1,0},{2,3},{3,2},{4,5},{5,4},{6,7},{7,6},{8,9},{9,8},{10,11... | collective-permute-start | bytes 1572872 | tf_op jit(solution)/shard_map/ppermute | solution.py:35
  282.9 12.4 %collective-permute-start.43 = (f32[384,256]{1,0:T(8,128)S(1)}, f32[384,256]{1,0:T(8,128)S(1)}, u32[]{:S(2)}, u32[]{:S(2)}) collective-permute-start(f32[384,256]{1,0:T(8,128)S(1)} %get-tuple-element.238), channel_id=1, source_target_pairs={{0,2},{1,3},{2,0},{3,1},{4,6},{5,7},{6,4},{7,5},{8,10},{9,11},{10,... | collective-permute-start | bytes 1179656 | tf_op jit(solution)/shard_map/ppermute | solution.py:35
  289.9 13.5 %collective-permute-start.56 = (f32[384,256]{1,0:T(8,128)S(1)}, f32[384,256]{1,0:T(8,128)S(1)}, u32[]{:S(2)}, u32[]{:S(2)}) collective-permute-start(f32[384,256]{1,0:T(8,128)S(1)} %get-tuple-element.245), channel_id=1, source_target_pairs={{0,2},{1,3},{2,0},{3,1},{4,6},{5,7},{6,4},{7,5},{8,10},{9,11},{10,... | collective-permute-start | bytes 1179656 | tf_op jit(solution)/shard_map/ppermute | solution.py:35
  290.0 20.9 %collective-permute-start.42 = (f32[384,256]{1,0:T(8,128)S(1)}, f32[384,256]{1,0:T(8,128)S(1)}, u32[]{:S(2)}, u32[]{:S(2)}) collective-permute-start(f32[384,256]{1,0:T(8,128)S(1)} %get-tuple-element.237), channel_id=1, source_target_pairs={{0,1},{1,0},{2,3},{3,2},{4,5},{5,4},{6,7},{7,6},{8,9},{9,8},{10,11... | collective-permute-start | bytes 1179656 | tf_op jit(solution)/shard_map/ppermute | solution.py:35
  293.3 17.2 %collective-permute-start.44 = (f32[256,256]{1,0:T(8,128)S(1)}, f32[256,256]{1,0:T(8,128)S(1)}, u32[]{:S(2)}, u32[]{:S(2)}) collective-permute-start(f32[256,256]{1,0:T(8,128)S(1)} %get-tuple-element.239), channel_id=1, source_target_pairs={{0,3},{1,2},{2,1},{3,0},{4,7},{5,6},{6,5},{7,4},{8,11},{9,10},{10,... | collective-permute-start | bytes 786440 | tf_op jit(solution)/shard_map/ppermute | solution.py:35
  294.8 18.9 %collective-permute-start.55 = (f32[384,256]{1,0:T(8,128)S(1)}, f32[384,256]{1,0:T(8,128)S(1)}, u32[]{:S(2)}, u32[]{:S(2)}) collective-permute-start(f32[384,256]{1,0:T(8,128)S(1)} %get-tuple-element.244), channel_id=1, source_target_pairs={{0,1},{1,0},{2,3},{3,2},{4,5},{5,4},{6,7},{7,6},{8,9},{9,8},{10,11... | collective-permute-start | bytes 1179656 | tf_op jit(solution)/shard_map/ppermute | solution.py:35
  295.3 18.4 %collective-permute-start.57 = (f32[256,256]{1,0:T(8,128)S(1)}, f32[256,256]{1,0:T(8,128)S(1)}, u32[]{:S(2)}, u32[]{:S(2)}) collective-permute-start(f32[256,256]{1,0:T(8,128)S(1)} %get-tuple-element.246), channel_id=1, source_target_pairs={{0,3},{1,2},{2,1},{3,0},{4,7},{5,6},{6,5},{7,4},{8,11},{9,10},{10,... | collective-permute-start | bytes 786440 | tf_op jit(solution)/shard_map/ppermute | solution.py:35
  303.4 7.5 %collective-permute-start.58 = (f32[128,256]{1,0:T(8,128)S(1)}, f32[128,256]{1,0:T(8,128)S(1)}, u32[]{:S(2)}, u32[]{:S(2)}) collective-permute-start(f32[128,256]{1,0:T(8,128)S(1)} %slice.10), channel_id=1, source_target_pairs={{0,1},{1,0},{2,3},{3,2},{4,5},{5,4},{6,7},{7,6},{8,9},{9,8},{10,11... | collective-permute-start | bytes 393224 | tf_op jit(solution)/shard_map/ppermute | solution.py:35
  (36 other events, 256.4 us)

commit v4 on v3

--- a/solution.py
+++ b/solution.py
@@ -12,7 +12,7 @@
 BAND = 24
 PANEL = 32
 AHEAD = 8
-TOGETHER = 4
+TOGETHER = 8
 HALVED = 128
 
 F32 = jnp.float32
@@ -267,7 +267,7 @@
 
 def apply_late_kernel(counts, chosen, found, number, ends, begun, strips, *rest):
     pieces = rest[:sum(counts)]
-    image, raw, window, held, total, sems, strip_sems = rest[sum(counts):]
+    image, raw, window, held, total, before, sems, strip_sems = rest[sum(counts):]
     row_blocks, room, block, _ = held.shape
     rows, width = raw.shape[1], raw.shape[2]
 
@@ -288,12 +288,16 @@
         each(i, do)
         return carry
 
+    bring = pltpu.make_async_copy(begun, before, sems.at[len(counts)])
+    bring.start()
     lax.fori_loop(0, row_blocks, start, 0)
     load_window(pieces, counts, ends, raw, window, sems, block)
     window[len(counts) * rows * 2:, :] = jnp.zeros((2 * block, width), BF16)
 
+    bring.wait()
+
     def one(i, carry):
-        total[:block] = begun[aligned(i, block), :]
+        total[:block] = before[aligned(i, block), :]
         total[block:] = jnp.zeros((block, width), F32)
 
         def do(js):
@@ -320,14 +324,15 @@
     return pl.pallas_call(
         functools.partial(apply_late_kernel, counts),
         out_shape=jax.ShapeDtypeStruct((rows, width), F32),
-        in_specs=[SMEM] * 4 + [VMEM] + [ANY] * (1 + len(flat)),
+        in_specs=[SMEM] * 4 + [ANY] * (2 + len(flat)),
         out_specs=VMEM,
         scratch_shapes=[
             pltpu.VMEM((len(counts), rows, width), F32),
             pltpu.VMEM((len(counts) * rows * 2 + 2 * block, width), BF16),
             pltpu.VMEM((row_blocks, room, block, block), F32),
             pltpu.VMEM((2 * block, width), F32),
-            pltpu.SemaphoreType.DMA((len(counts),)),
+            pltpu.VMEM((rows, width), F32),
+            pltpu.SemaphoreType.DMA((len(counts) + 1,)),
             pltpu.SemaphoreType.DMA((row_blocks, room)),
         ],
         compiler_params=params(),
@@ -369,7 +374,7 @@
 def inner(image, at, basis_rows, g0, groups):
     rows, width = image.shape[0], groups * GROUP
     orders = sum(two[0].shape[0] for two in basis_rows)
-    tile = rows // 4
+    tile = rows // 2
     specs, arrays = group_specs(basis_rows, tile, g0, groups)
     shape = (groups, GROUP, orders * GROUP)
     return pl.pallas_call(
@@ -406,7 +411,7 @@
 def project(image, at, basis_rows, coeffs_t, g0, groups):
     orders = sum(two[0].shape[0] for two in basis_rows)
     rows, width = image.shape[0], groups * GROUP
-    tile = rows // 4
+    tile = rows // 2
     specs, arrays = group_specs(basis_rows, tile, g0, groups)
     return pl.pallas_call(
         functools.partial(project_kernel, orders),
@@ -783,14 +788,20 @@
         grams = [
             projected(c, Sum(inner(values["image", c], 0, basis_rows, *chunks[c])).result())
             for c in range(len(chunks))]
-    grams = [gram.result() for gram in grams]
+    def finished(c, gram):
+        out = list(finish(me, gram, residuals[c], parts))
+        if c and relayed:
+            for k in others[1:]:
+                out[k], blocks[0][k] = tied(out[k], blocks[0][k])
+        return [out[0]] + [swap(out[k], "rhs", k) for k in others]
+
+    if relayed:
+        blocks.append(finished(0, grams[0].result()))
     held = [x for got in all_coeffs for x in got]
-    grams[-1], *held = tied(grams[-1], *held)
+    gram, *held = tied(grams[-1].result(), *held)
     all_coeffs = [held[c * parts:(c + 1) * parts] for c in range(len(chunks))]
-    for residual, gram in zip(residuals, grams):
-        out = finish(me, gram, residual, parts)
-        got = [out[0]] + [swap(out[k], "rhs", k) for k in others]
-        blocks.append(got)
+    for c in range(len(blocks), len(chunks)):
+        blocks.append(finished(c, gram if c == last else grams[c].result()))
 
     coeffs = collect_coeffs(
         me, all_coeffs, chunks, (orders, total // GROUP, GROUP, GROUP), parts)

time: 316 us -> 314 us (level)
  Pallas kernels: 91.3 us -> 88 us
  transfers between devices with their start and end apart: 60 -> 60, of which waited for: 23 -> 23; matrix products, arithmetic and copies ran while one was open for 3% -> 3% of each run, Pallas kernels for 28% -> 27%
where the time goes in v4:
time: 314 us; the launch traced here: 313 us
  waiting for transfers between devices  120 us (38%)
  Pallas kernels  88 us (28%)
  starting transfers between devices  81.9 us (26%)
  local copies, waits for them, and re-layouts  15.1 us (5%)
  other arithmetic  7.18 us (2%)
    ppermute x42, waiting for transfers between devices, swap(): return lax.ppermute(value, axis, pairs_of(axis, k))  88.8 us
    ppermute x42, starting transfers between devices, swap(): return lax.ppermute(value, axis, pairs_of(axis, k))  56 us
    ppermute x18, waiting for transfers between devices, relay(): values[name, c] = lax.ppermute(value, 'blk', pairs)  31.1 us
    pallas_call x2, Pallas kernels, apply(): pl.pallas_call(functools.partial(apply_kernel, counts, near), grid=(row_b...  28.3 us
    ppermute x18, starting transfers between devices, relay(): values[name, c] = lax.ppermute(value, 'blk', pairs)  25.9 us
    pallas_call x2, Pallas kernels, project(): pl.pallas_call(functools.partial(project_kernel, orders), grid=(rows // t...  13.5 us
    unnamed x48, local copies, waits for them, and re-layouts  12 us
    pallas_call x2, Pallas kernels, finish(): pl.pallas_call(functools.partial(finish_kernel, groups, parts), out_shape...  10.2 us
  transfers between devices with their start and end apart: 60, of which 23 were waited for; matrix products, arithmetic and copies ran while one was open for 3% of the time, Pallas kernels for 27%

profile of v4, /device:TPU:1, one launch (start us, length us, event | category | flops | bytes accessed | tf_op | source)
XLA Modules:
  0.0 313.4 jit_solution(539960251087953498)
XLA Ops:
  2.4 2.7 collective-permute-start.1
  5.1 6.5 %collective-permute-done.1.refs_2_ = f32[1,256,256]{2,1,0:T(8,128)S(1)} collective-permute-done((f32[1,256,256]{2,1,0:T(8,128)S(1)}, f32[1,256,256]{2,1,0:T(8,128)S(1)}, u32[]{:S(2)}, u32[]{:S(2)}) %collective-permute-start.1) | collective-permute-done | bytes 262176 | tf_op jit(solution)/shard_map/ppermute | solution.py:35
  11.7 5.6 %collective-permute-done.2.refs_3_ = f32[1,256,256]{2,1,0:T(8,128)S(1)} collective-permute-done((f32[1,256,256]{2,1,0:T(8,128)S(1)}, f32[1,256,256]{2,1,0:T(8,128)S(1)}, u32[]{:S(2)}, u32[]{:S(2)}) %collective-permute-start.2) | collective-permute-done | bytes 262176 | tf_op jit(solution)/shard_map/ppermute | solution.py:35
  24.5 2.7 cut_columns.6
  27.3 2.9 cut_columns.7
  32.2 3.7 %collective-permute-done.8.refs_3_ = f32[1,256,256]{2,1,0:T(8,128)S(1)} collective-permute-done((f32[1,256,256]{2,1,0:T(8,128)S(1)}, f32[1,256,256]{2,1,0:T(8,128)S(1)}, u32[]{:S(2)}, u32[]{:S(2)}) %collective-permute-start.8) | collective-permute-done | bytes 262176 | tf_op jit(solution)/shard_map/ppermute | solution.py:35
  38.2 3.8 %collective-permute-done.3.rest_1_ = f32[1024,256]{1,0:T(8,128)S(1)} collective-permute-done((f32[1024,256]{1,0:T(8,128)S(1)}, f32[1024,256]{1,0:T(8,128)S(1)}, u32[]{:S(2)}, u32[]{:S(2)}) %collective-permute-start.3) | collective-permute-done | bytes 1048608 | tf_op jit(solution)/shard_map/ppermute | solution.py:695
  47.1 4.6 %collective-permute-start.13 = (f32[1024,256]{1,0:T(8,128)}, f32[1024,256]{1,0:T(8,128)}, u32[]{:S(2)}, u32[]{:S(2)}) collective-permute-start(f32[1024,256]{1,0:T(8,128)} %bitcast.3.rest_0_), channel_id=1, source_target_pairs={{0,8},{4,12},{8,0},{12,4},{16,24},{20,28},{24,16},{28,20},{1,9},{5... | collective-permute-start | bytes 3145736 | tf_op jit(solution)/shard_map/ppermute | solution.py:695
  51.8 2.5 collective-permute-start.14
  54.3 6.6 %collective-permute-done.10.refs_2_ = f32[2,256,512]{2,1,0:T(8,128)S(1)} collective-permute-done((f32[2,256,512]{2,1,0:T(8,128)S(1)}, f32[2,256,512]{2,1,0:T(8,128)S(1)}, u32[]{:S(2)}, u32[]{:S(2)}) %collective-permute-start.10) | collective-permute-done | bytes 1048608 | tf_op jit(solution)/shard_map/ppermute | solution.py:35
  63.6 4.7 %collective-permute-done.12.rest_3_ = f32[1024,256]{1,0:T(8,128)S(1)} collective-permute-done((f32[1024,256]{1,0:T(8,128)S(1)}, f32[1024,256]{1,0:T(8,128)S(1)}, u32[]{:S(2)}, u32[]{:S(2)}) %collective-permute-start.12) | collective-permute-done | bytes 1048608 | tf_op jit(solution)/shard_map/ppermute | solution.py:695
  68.3 5.0 %collective-permute-done.13.rest_1_ = f32[1024,256]{1,0:T(8,128)} collective-permute-done((f32[1024,256]{1,0:T(8,128)}, f32[1024,256]{1,0:T(8,128)}, u32[]{:S(2)}, u32[]{:S(2)}) %collective-permute-start.13) | collective-permute-done | bytes 1048608 | tf_op jit(solution)/shard_map/ppermute | solution.py:695
  78.8 9.2 %collective-permute-done.15.refs_3_ = f32[2,256,512]{2,1,0:T(8,128)} collective-permute-done((f32[2,256,512]{2,1,0:T(8,128)}, f32[2,256,512]{2,1,0:T(8,128)}, u32[]{:S(2)}, u32[]{:S(2)}) %collective-permute-start.15) | collective-permute-done | bytes 1048608 | tf_op jit(solution)/shard_map/ppermute | solution.py:35
  88.0 11.0 %collective-permute-done.17.rest_5_ = f32[1024,256]{1,0:T(8,128)} collective-permute-done((f32[1024,256]{1,0:T(8,128)}, f32[1024,256]{1,0:T(8,128)}, u32[]{:S(2)}, u32[]{:S(2)}) %collective-permute-start.17) | collective-permute-done | bytes 1048608 | tf_op jit(solution)/shard_map/ppermute | solution.py:695
  100.2 2.4 broadcast_select_fusion.1
  105.6 5.2 %collective-permute-start.23 = (f32[2,256,512]{2,1,0:T(8,128)}, f32[2,256,512]{2,1,0:T(8,128)}, u32[]{:S(2)}, u32[]{:S(2)}) collective-permute-start(f32[2,256,512]{2,1,0:T(8,128)} %copy-done.16), channel_id=1, source_target_pairs={{0,3},{1,2},{2,1},{3,0},{4,7},{5,6},{6,5},{7,4},{8,11},{9,10},{10,... | collective-permute-start | bytes 3145736 | tf_op jit(solution)/shard_map/ppermute | solution.py:35
  111.5 1.9 gather_fusion
  114.9 3.5 %join_rows.6 = (bf16[2,1024,512]{2,1,0:T(8,128)(2,1)}, bf16[2,1024,512]{2,1,0:T(8,128)(2,1)}) custom-call(s32[1]{0:T(128)} %bitcast.me_ref.me, f32[4,256,2048]{2,1,0:T(8,128)} %refs_0_.7, f32[2,256,512]{2,1,0:T(8,128)S(1)} %collective-permute-done.9.refs_1_, f32[2,256,512]{2,1,0:T(8,128)S(1)} %copy-done.7, f32[2,256,512]{2,1,0:T(8,128)} %collective-permute-done.15.refs_3_), custom_call_target="tpu_custom_call" | custom-call | tf_op jit(solution)/shard_map/join_rows/pallas_call | solution.py:101
  118.5 3.6 %collective-permute-done.20.rest_7_ = f32[1024,256]{1,0:T(8,128)} collective-permute-done((f32[1024,256]{1,0:T(8,128)}, f32[1024,256]{1,0:T(8,128)}, u32[]{:S(2)}, u32[]{:S(2)}) %collective-permute-start.20) | collective-permute-done | bytes 1048608 | tf_op jit(solution)/shard_map/ppermute | solution.py:695
  129.0 6.1 %collective-permute-done.23.refs_3_ = f32[2,256,512]{2,1,0:T(8,128)} collective-permute-done((f32[2,256,512]{2,1,0:T(8,128)}, f32[2,256,512]{2,1,0:T(8,128)}, u32[]{:S(2)}, u32[]{:S(2)}) %collective-permute-start.23) | collective-permute-done | bytes 1048608 | tf_op jit(solution)/shard_map/ppermute | solution.py:35
  135.1 3.6 %join_rows.7 = (bf16[2,1024,512]{2,1,0:T(8,128)(2,1)}, bf16[2,1024,512]{2,1,0:T(8,128)(2,1)}) custom-call(s32[1]{0:T(128)} %bitcast.me_ref.me, f32[4,256,2048]{2,1,0:T(8,128)} %refs_0_.7, f32[2,256,512]{2,1,0:T(8,128)S(1)} %collective-permute-done.14.refs_1_, f32[2,256,512]{2,1,0:T(8,128)S(1)} %collective-permute-done.19.refs_2_, ...), custom_call_target="tpu_custom_call" | custom-call | tf_op jit(solution)/shard_map/join_rows/pallas_call | solution.py:101
  138.7 14.3 %apply.2.image = f32[1024,256]{1,0:T(8,128)S(1)} custom-call(s32[8,25]{1,0:T(8,128)S(1)} %get-tuple-element.270.places, s32[1]{0:T(128)} %bitcast.5.ends, f32[8,25,128,128]{3,2,1,0:T(8,128)} %strips.5, f32[1024,256]{1,0:T(8,128)S(1)} %bitcast.41, f32[1024,256]{1,0:T(8,128)S(1)} %copy-done.15, f32[1024,256]{1,0:T(8,128)} %collective-permute-done.4.rest_2_, ...), custom_call_target="tpu_custom_call" | custom-call | flops 6710886400 | bytes 21495808 | tf_op jit(solution)/shard_map/apply/pallas_call | solution.py:248
  153.0 3.2 %inner.2 = f32[2,128,512]{2,1,0:T(8,128)S(1)} custom-call(f32[1024,256]{1,0:T(8,128)S(1)} %apply.2.image, bf16[2,1024,512]{2,1,0:T(8,128)(2,1)S(1)} %copy-done, bf16[2,1024,512]{2,1,0:T(8,128)(2,1)S(1)} %copy-done, bf16[2,1024,512]{2,1,0:T(8,128)(2,1)} %get-tuple-element.226.rest_2_.rest_3_.rest_10_.rest_11_, ...), custom_call_target="tpu_custom_call" | custom-call | flops 805306368 | bytes 5242880 | tf_op jit(solution)/shard_map/inner/pallas_call | solution.py:380
  161.4 14.0 %apply.3.begun = f32[1024,256]{1,0:T(8,128)S(1)} custom-call(s32[8,25]{1,0:T(8,128)S(1)} %get-tuple-element.269.places, s32[1]{0:T(128)} %bitcast.5.ends, f32[8,25,128,128]{3,2,1,0:T(8,128)} %strips.5, f32[1024,256]{1,0:T(8,128)} %bitcast.3.rest_0_, f32[1024,256]{1,0:T(8,128)} %collective-permute-done.13.rest_1_, ...), custom_call_target="tpu_custom_call" | custom-call | flops 6710886400 | bytes 21495808 | tf_op jit(solution)/shard_map/apply/pallas_call | solution.py:248
  176.4 11.8 %collective-permute-done.27 = f32[128,512]{1,0:T(8,128)S(1)} collective-permute-done((f32[128,512]{1,0:T(8,128)S(1)}, f32[128,512]{1,0:T(8,128)S(1)}, u32[]{:S(2)}, u32[]{:S(2)}) %collective-permute-start.27) | collective-permute-done | bytes 262176 | tf_op jit(solution)/shard_map/ppermute | solution.py:35
  189.2 4.2 %collective-permute-start.31 = (f32[128,512]{1,0:T(8,128)S(1)}, f32[128,512]{1,0:T(8,128)}, u32[]{:S(2)}, u32[]{:S(2)}) collective-permute-start(f32[128,512]{1,0:T(8,128)S(1)} %dynamic-slice_add_fusion.1), channel_id=1, source_target_pairs={{0,8},{4,12},{8,0},{12,4},{16,24},{20,28},{24,16},{28,20},{1,9},{5... | collective-permute-start | bytes 786440 | tf_op jit(solution)/shard_map/ppermute | solution.py:35
  196.1 9.7 %apply_late.1.image = f32[1024,256]{1,0:T(8,128)S(1)} custom-call(s32[8,16]{1,0:T(8,128)S(1)} %bitcast.48, s32[8,16]{1,0:T(8,128)S(1)} %bitcast_select_fusion.found, s32[8]{0:T(128)S(1)} %convert_reduce_fusion.number, s32[1]{0:T(128)} %bitcast.5.ends, f32[1024,256]{1,0:T(8,128)S(1)} %copy-done.11, f32[8,25,128,128]{3,2,1,0:T(8,128)} %strips.5, ...), custom_call_target="tpu_custom_call" | custom-call | flops 2147483648 | bytes 8388608 | tf_op jit(solution)/shard_map/apply_late/pallas_call | solution.py:324
  206.9 2.9 inner.3
  211.2 9.6 %collective-permute-done.32 = f32[128,512]{1,0:T(8,128)S(1)} collective-permute-done((f32[128,512]{1,0:T(8,128)S(1)}, f32[128,512]{1,0:T(8,128)S(1)}, u32[]{:S(2)}, u32[]{:S(2)}) %collective-permute-start.32) | collective-permute-done | bytes 262176 | tf_op jit(solution)/shard_map/ppermute | solution.py:35
  222.0 6.0 %collective-permute-done.33 = f32[128,512]{1,0:T(8,128)S(1)} collective-permute-done((f32[128,512]{1,0:T(8,128)S(1)}, f32[128,512]{1,0:T(8,128)S(1)}, u32[]{:S(2)}, u32[]{:S(2)}) %collective-permute-start.33) | collective-permute-done | bytes 262176 | tf_op jit(solution)/shard_map/ppermute | solution.py:35
  229.3 6.7 %project.2 = (f32[1024,256]{1,0:T(8,128)S(1)}, f32[2,128,128]{2,1,0:T(8,128)S(1)}) custom-call(f32[1024,256]{1,0:T(8,128)S(1)} %copy-done.4, f32[2,128,512]{2,1,0:T(8,128)S(1)} %bitcast.26, bf16[2,1024,512]{2,1,0:T(8,128)(2,1)} %get-tuple-element.225.rest_0_.rest_1_.rest_8_.rest_9_, bf16[2,1024,512]{2,1,0:T(8,128)(2,1)} %get-tuple-element.225.rest_0_.rest_1_.rest_8_.rest_9_, ...), custom_call_target="tpu_custom_call" | custom-call | flops 1006632960 | bytes 6291456 | tf_op jit(solution)/shard_map/project/pallas_call | solution.py:416
  236.0 8.0 %collective-permute-done.36 = f32[128,512]{1,0:T(8,128)S(1)} collective-permute-done((f32[128,512]{1,0:T(8,128)S(1)}, f32[128,512]{1,0:T(8,128)S(1)}, u32[]{:S(2)}, u32[]{:S(2)}) %collective-permute-start.36) | collective-permute-done | bytes 262176 | tf_op jit(solution)/shard_map/ppermute | solution.py:35
  247.2 6.1 %collective-permute-done.37 = f32[128,512]{1,0:T(8,128)S(1)} collective-permute-done((f32[128,512]{1,0:T(8,128)S(1)}, f32[128,512]{1,0:T(8,128)S(1)}, u32[]{:S(2)}, u32[]{:S(2)}) %collective-permute-start.37) | collective-permute-done | bytes 262176 | tf_op jit(solution)/shard_map/ppermute | solution.py:35
  253.6 6.9 %project.3 = (f32[1024,256]{1,0:T(8,128)S(1)}, f32[2,128,128]{2,1,0:T(8,128)S(1)}) custom-call(f32[1024,256]{1,0:T(8,128)S(1)} %apply_late.1.image, f32[2,128,512]{2,1,0:T(8,128)S(1)} %bitcast.31, bf16[2,1024,512]{2,1,0:T(8,128)(2,1)} %get-tuple-element.225.rest_0_.rest_1_.rest_8_.rest_9_, ...), custom_call_target="tpu_custom_call" | custom-call | flops 1006632960 | bytes 6291456 | tf_op jit(solution)/shard_map/project/pallas_call | solution.py:416
  266.1 3.1 collective-permute-start.47
  271.8 2.8 collective-permute-start.52
  275.4 5.1 %finish.2 = (f32[384,256]{1,0:T(8,128)S(1)}, f32[384,256]{1,0:T(8,128)S(1)}, f32[384,256]{1,0:T(8,128)S(1)}, f32[256,256]{1,0:T(8,128)S(1)}) custom-call(s32[1]{0:T(128)} %bitcast.me_ref.me, f32[2,128,128]{2,1,0:T(8,128)S(1)} %bitcast.43, f32[1024,256]{1,0:T(8,128)S(1)} %get-tuple-element.239.residual), custom_call_target="tpu_custom_call" | custom-call | flops 201326592 | bytes 4194304 | tf_op jit(solution)/shard_map/finish/pallas_call | solution.py:504
  280.5 1.8 collective-permute-start.53
  282.4 3.3 %collective-permute-start.54 = (f32[256,256]{1,0:T(8,128)S(1)}, f32[256,256]{1,0:T(8,128)S(1)}, u32[]{:S(2)}, u32[]{:S(2)}) collective-permute-start(f32[256,256]{1,0:T(8,128)S(1)} %get-tuple-element.249), channel_id=1, source_target_pairs={{0,3},{1,2},{2,1},{3,0},{4,7},{5,6},{6,5},{7,4},{8,11},{9,10},{10,... | collective-permute-start | bytes 786440 | tf_op jit(solution)/shard_map/ppermute | solution.py:35
  285.7 5.1 %finish.3 = (f32[384,256]{1,0:T(8,128)S(1)}, f32[384,256]{1,0:T(8,128)S(1)}, f32[384,256]{1,0:T(8,128)S(1)}, f32[256,256]{1,0:T(8,128)S(1)}) custom-call(s32[1]{0:T(128)} %bitcast.me_ref.me, f32[2,128,128]{2,1,0:T(8,128)S(1)} %bitcast.42, f32[1024,256]{1,0:T(8,128)S(1)} %get-tuple-element.244.residual), custom_call_target="tpu_custom_call" | custom-call | flops 201326592 | bytes 4194304 | tf_op jit(solution)/shard_map/finish/pallas_call | solution.py:504
  290.9 1.8 collective-permute-start.56
  292.6 5.1 %collective-permute-start.42 = (f32[384,256]{1,0:T(8,128)S(1)}, f32[384,256]{1,0:T(8,128)S(1)}, u32[]{:S(2)}, u32[]{:S(2)}) collective-permute-start(f32[384,256]{1,0:T(8,128)S(1)} %get-tuple-element.241), channel_id=1, source_target_pairs={{0,1},{1,0},{2,3},{3,2},{4,5},{5,4},{6,7},{7,6},{8,9},{9,8},{10,11... | collective-permute-start | bytes 1179656 | tf_op jit(solution)/shard_map/ppermute | solution.py:35
  297.8 2.8 collective-permute-done.54.refs_3_
  300.6 2.3 collective-permute-start.58
  302.9 4.2 %collect_coeffs.1 = f32[4,16,128,128]{3,2,1,0:T(8,128)} custom-call(s32[1]{0:T(128)} %bitcast.me_ref.me, f32[2,128,512]{2,1,0:T(8,128)S(1)} %bitcast.29, f32[2,128,512]{2,1,0:T(8,128)S(1)} %collective-permute-done.47.refs_1_, f32[2,128,512]{2,1,0:T(8,128)S(1)} %collective-permute-done.48.refs_2_, f32[2,128,512]{2,1,0:T(8,128)S(1)} %collective-permute-done.49.refs_3_, ...), custom_call_target="tpu_custom_call" | custom-call | tf_op jit(solution)/shard_map/collect_coeffs/pallas_call | solution.py:560
  307.1 1.7 collective-permute-start.59
  308.8 2.5 collective-permute-done.57.refs_7_
  311.4 2.0 collect_blocks.1
  (187 shorter events, 67.0 us)
Async XLA Ops:
  2.4 9.3 %collective-permute-start.1 = (f32[1,256,256]{2,1,0:T(8,128)S(1)}, f32[1,256,256]{2,1,0:T(8,128)S(1)}, u32[]{:S(2)}, u32[]{:S(2)}) collective-permute-start(f32[1,256,256]{2,1,0:T(8,128)S(1)} %get-tuple-element.136), channel_id=1, source_target_pairs={{0,2},{1,3},{2,0},{3,1},{4,6},{5,7},{6,4},{7,5},{8,10},{9,11},{10,... | collective-permute-start | bytes 786440 | tf_op jit(solution)/shard_map/ppermute | solution.py:35
  5.1 12.2 %collective-permute-start.2 = (f32[1,256,256]{2,1,0:T(8,128)S(1)}, f32[1,256,256]{2,1,0:T(8,128)S(1)}, u32[]{:S(2)}, u32[]{:S(2)}) collective-permute-start(f32[1,256,256]{2,1,0:T(8,128)S(1)} %get-tuple-element.137), channel_id=1, source_target_pairs={{0,3},{1,2},{2,1},{3,0},{4,7},{5,6},{6,5},{7,4},{8,11},{9,10},{10,... | collective-permute-start | bytes 786440 | tf_op jit(solution)/shard_map/ppermute | solution.py:35
  17.4 24.7 %collective-permute-start.3 = (f32[1024,256]{1,0:T(8,128)S(1)}, f32[1024,256]{1,0:T(8,128)S(1)}, u32[]{:S(2)}, u32[]{:S(2)}) collective-permute-start(f32[1024,256]{1,0:T(8,128)S(1)} %bitcast.38), channel_id=1, source_target_pairs={{0,8},{4,12},{8,0},{12,4},{16,24},{20,28},{24,16},{28,20},{1,9},{5... | collective-permute-start | bytes 3145736 | tf_op jit(solution)/shard_map/ppermute | solution.py:695
  19.0 24.3 %collective-permute-start.4 = (f32[1024,256]{1,0:T(8,128)S(1)}, f32[1024,256]{1,0:T(8,128)}, u32[]{:S(2)}, u32[]{:S(2)}) collective-permute-start(f32[1024,256]{1,0:T(8,128)S(1)} %bitcast.39), channel_id=1, source_target_pairs={{0,4},{4,0},{8,12},{12,8},{16,20},{20,16},{24,28},{28,24},{1,5},{5... | collective-permute-start | bytes 3145736 | tf_op jit(solution)/shard_map/ppermute | solution.py:695
  20.2 23.1 %collective-permute-start.5 = (f32[1024,256]{1,0:T(8,128)S(1)}, f32[1024,256]{1,0:T(8,128)S(1)}, u32[]{:S(2)}, u32[]{:S(2)}) collective-permute-start(f32[1024,256]{1,0:T(8,128)S(1)} %bitcast.40), channel_id=1, source_target_pairs={{8,16},{12,20},{16,8},{20,12},{9,17},{13,21},{17,9},{21,13},{10,18... | collective-permute-start | bytes 3145736 | tf_op jit(solution)/shard_map/ppermute | solution.py:695
  21.9 10.2 %collective-permute-start.7 = (f32[1,256,256]{2,1,0:T(8,128)S(1)}, f32[1,256,256]{2,1,0:T(8,128)S(1)}, u32[]{:S(2)}, u32[]{:S(2)}) collective-permute-start(f32[1,256,256]{2,1,0:T(8,128)S(1)} %get-tuple-element.139), channel_id=1, source_target_pairs={{0,2},{1,3},{2,0},{3,1},{4,6},{5,7},{6,4},{7,5},{8,10},{9,11},{10,... | collective-permute-start | bytes 786440 | tf_op jit(solution)/shard_map/ppermute | solution.py:35
  23.1 12.8 %collective-permute-start.8 = (f32[1,256,256]{2,1,0:T(8,128)S(1)}, f32[1,256,256]{2,1,0:T(8,128)S(1)}, u32[]{:S(2)}, u32[]{:S(2)}) collective-permute-start(f32[1,256,256]{2,1,0:T(8,128)S(1)} %get-tuple-element.140), channel_id=1, source_target_pairs={{0,3},{1,2},{2,1},{3,0},{4,7},{5,6},{6,5},{7,4},{8,11},{9,10},{10,... | collective-permute-start | bytes 786440 | tf_op jit(solution)/shard_map/ppermute | solution.py:35
  32.1 19.7 %collective-permute-start.9 = (f32[2,256,512]{2,1,0:T(8,128)S(1)}, f32[2,256,512]{2,1,0:T(8,128)S(1)}, u32[]{:S(2)}, u32[]{:S(2)}) collective-permute-start(f32[2,256,512]{2,1,0:T(8,128)S(1)} %get-tuple-element.141), channel_id=1, source_target_pairs={{0,1},{1,0},{2,3},{3,2},{4,5},{5,4},{6,7},{7,6},{8,9},{9,8},{10,11... | collective-permute-start | bytes 3145736 | tf_op jit(solution)/shard_map/ppermute | solution.py:35
  35.9 25.0 %collective-permute-start.10 = (f32[2,256,512]{2,1,0:T(8,128)S(1)}, f32[2,256,512]{2,1,0:T(8,128)S(1)}, u32[]{:S(2)}, u32[]{:S(2)}) collective-permute-start(f32[2,256,512]{2,1,0:T(8,128)S(1)} %get-tuple-element.142), channel_id=1, source_target_pairs={{0,2},{1,3},{2,0},{3,1},{4,6},{5,7},{6,4},{7,5},{8,10},{9,11},{10,... | collective-permute-start | bytes 3145736 | tf_op jit(solution)/shard_map/ppermute | solution.py:35
  43.3 20.3 %collective-permute-start.11 = (f32[1024,256]{1,0:T(8,128)S(1)}, f32[1024,256]{1,0:T(8,128)}, u32[]{:S(2)}, u32[]{:S(2)}) collective-permute-start(f32[1024,256]{1,0:T(8,128)S(1)} %collective-permute-done.3.rest_1_), channel_id=1, source_target_pairs={{8,16},{12,20},{16,8},{20,12},{9,17},{13,21},{17,9},{21,13},{10,18... | collective-permute-start | bytes 3145736 | tf_op jit(solution)/shard_map/ppermute | solution.py:695
  44.9 23.4 %collective-permute-start.12 = (f32[1024,256]{1,0:T(8,128)S(1)}, f32[1024,256]{1,0:T(8,128)S(1)}, u32[]{:S(2)}, u32[]{:S(2)}) collective-permute-start(f32[1024,256]{1,0:T(8,128)S(1)} %collective-permute-done.3.rest_1_), channel_id=1, source_target_pairs={{0,4},{4,0},{8,12},{12,8},{16,20},{20,16},{24,28},{28,24},{1,5},{5... | collective-permute-start | bytes 3145736 | tf_op jit(solution)/shard_map/ppermute | solution.py:695
  47.1 26.2 %collective-permute-start.13 = (f32[1024,256]{1,0:T(8,128)}, f32[1024,256]{1,0:T(8,128)}, u32[]{:S(2)}, u32[]{:S(2)}) collective-permute-start(f32[1024,256]{1,0:T(8,128)} %bitcast.3.rest_0_), channel_id=1, source_target_pairs={{0,8},{4,12},{8,0},{12,4},{16,24},{20,28},{24,16},{28,20},{1,9},{5... | collective-permute-start | bytes 3145736 | tf_op jit(solution)/shard_map/ppermute | solution.py:695
  51.8 25.8 %collective-permute-start.14 = (f32[2,256,512]{2,1,0:T(8,128)}, f32[2,256,512]{2,1,0:T(8,128)S(1)}, u32[]{:S(2)}, u32[]{:S(2)}) collective-permute-start(f32[2,256,512]{2,1,0:T(8,128)} %get-tuple-element.148), channel_id=1, source_target_pairs={{0,1},{1,0},{2,3},{3,2},{4,5},{5,4},{6,7},{7,6},{8,9},{9,8},{10,11... | collective-permute-start | bytes 3145736 | tf_op jit(solution)/shard_map/ppermute | solution.py:35
  61.9 26.1 %collective-permute-start.15 = (f32[2,256,512]{2,1,0:T(8,128)}, f32[2,256,512]{2,1,0:T(8,128)}, u32[]{:S(2)}, u32[]{:S(2)}) collective-permute-start(f32[2,256,512]{2,1,0:T(8,128)} %get-tuple-element.147), channel_id=1, source_target_pairs={{0,3},{1,2},{2,1},{3,0},{4,7},{5,6},{6,5},{7,4},{8,11},{9,10},{10,... | collective-permute-start | bytes 3145736 | tf_op jit(solution)/shard_map/ppermute | solution.py:35
  73.3 14.7 %collective-permute-start.16 = (f32[1024,256]{1,0:T(8,128)}, f32[1024,256]{1,0:T(8,128)}, u32[]{:S(2)}, u32[]{:S(2)}) collective-permute-start(f32[1024,256]{1,0:T(8,128)} %collective-permute-done.4.rest_2_), channel_id=1, source_target_pairs={{8,16},{12,20},{16,8},{20,12},{9,17},{13,21},{17,9},{21,13},{10,18... | collective-permute-start | bytes 3145736 | tf_op jit(solution)/shard_map/ppermute | solution.py:695
  75.0 24.0 %collective-permute-start.17 = (f32[1024,256]{1,0:T(8,128)}, f32[1024,256]{1,0:T(8,128)}, u32[]{:S(2)}, u32[]{:S(2)}) collective-permute-start(f32[1024,256]{1,0:T(8,128)} %collective-permute-done.11), channel_id=1, source_target_pairs={{8,0},{12,4},{16,24},{20,28},{9,1},{13,5},{17,25},{21,29},{10,2},{... | collective-permute-start | bytes 3145736 | tf_op jit(solution)/shard_map/ppermute | solution.py:695
  76.3 22.7 %collective-permute-start.18 = (f32[1024,256]{1,0:T(8,128)}, f32[1024,256]{1,0:T(8,128)}, u32[]{:S(2)}, u32[]{:S(2)}) collective-permute-start(f32[1024,256]{1,0:T(8,128)} %bitcast.3.rest_0_), channel_id=1, source_target_pairs={{0,4},{4,0},{8,12},{12,8},{16,20},{20,16},{24,28},{28,24},{1,5},{5... | collective-permute-start | bytes 3145736 | tf_op jit(solution)/shard_map/ppermute | solution.py:695
  77.6 40.9 %collective-permute-start.19 = (f32[2,256,512]{2,1,0:T(8,128)}, f32[2,256,512]{2,1,0:T(8,128)S(1)}, u32[]{:S(2)}, u32[]{:S(2)}) collective-permute-start(f32[2,256,512]{2,1,0:T(8,128)} %copy-done.17), channel_id=1, source_target_pairs={{0,2},{1,3},{2,0},{3,1},{4,6},{5,7},{6,4},{7,5},{8,10},{9,11},{10,... | collective-permute-start | bytes 3145736 | tf_op jit(solution)/shard_map/ppermute | solution.py:35
  99.0 23.1 %collective-permute-start.20 = (f32[1024,256]{1,0:T(8,128)}, f32[1024,256]{1,0:T(8,128)}, u32[]{:S(2)}, u32[]{:S(2)}) collective-permute-start(f32[1024,256]{1,0:T(8,128)} %collective-permute-done.16.rest_4_), channel_id=1, source_target_pairs={{8,0},{12,4},{16,24},{20,28},{9,1},{13,5},{17,25},{21,29},{10,2},{... | collective-permute-start | bytes 3145736 | tf_op jit(solution)/shard_map/ppermute | solution.py:695
  102.6 21.2 %collective-permute-start.21 = (f32[1024,256]{1,0:T(8,128)}, f32[1024,256]{1,0:T(8,128)}, u32[]{:S(2)}, u32[]{:S(2)}) collective-permute-start(f32[1024,256]{1,0:T(8,128)} %broadcast_select_fusion.1), channel_id=1, source_target_pairs={{0,4},{4,0},{8,12},{12,8},{16,20},{20,16},{24,28},{28,24},{1,5},{5... | collective-permute-start | bytes 3145736 | tf_op jit(solution)/shard_map/ppermute | solution.py:695
  103.9 19.9 %collective-permute-start.22 = (f32[1024,256]{1,0:T(8,128)}, f32[1024,256]{1,0:T(8,128)}, u32[]{:S(2)}, u32[]{:S(2)}) collective-permute-start(f32[1024,256]{1,0:T(8,128)} %collective-permute-done.13.rest_1_), channel_id=1, source_target_pairs={{8,16},{12,20},{16,8},{20,12},{9,17},{13,21},{17,9},{21,13},{10,18... | collective-permute-start | bytes 3145736 | tf_op jit(solution)/shard_map/ppermute | solution.py:695
  105.6 29.5 %collective-permute-start.23 = (f32[2,256,512]{2,1,0:T(8,128)}, f32[2,256,512]{2,1,0:T(8,128)}, u32[]{:S(2)}, u32[]{:S(2)}) collective-permute-start(f32[2,256,512]{2,1,0:T(8,128)} %copy-done.16), channel_id=1, source_target_pairs={{0,3},{1,2},{2,1},{3,0},{4,7},{5,6},{6,5},{7,4},{8,11},{9,10},{10,... | collective-permute-start | bytes 3145736 | tf_op jit(solution)/shard_map/ppermute | solution.py:35
  123.8 32.4 %collective-permute-start.24 = (f32[1024,256]{1,0:T(8,128)}, f32[1024,256]{1,0:T(8,128)}, u32[]{:S(2)}, u32[]{:S(2)}) collective-permute-start(f32[1024,256]{1,0:T(8,128)} %collective-permute-done.18.rest_2_), channel_id=1, source_target_pairs={{8,16},{12,20},{16,8},{20,12},{9,17},{13,21},{17,9},{21,13},{10,18... | collective-permute-start | bytes 3145736 | tf_op jit(solution)/shard_map/ppermute | solution.py:695
  125.4 30.8 %collective-permute-start.25 = (f32[1024,256]{1,0:T(8,128)}, f32[1024,256]{1,0:T(8,128)}, u32[]{:S(2)}, u32[]{:S(2)}) collective-permute-start(f32[1024,256]{1,0:T(8,128)} %collective-permute-done.22), channel_id=1, source_target_pairs={{8,0},{12,4},{16,24},{20,28},{9,1},{13,5},{17,25},{21,29},{10,2},{... | collective-permute-start | bytes 3145736 | tf_op jit(solution)/shard_map/ppermute | solution.py:695
  126.7 29.5 %collective-permute-start.26 = (f32[1024,256]{1,0:T(8,128)}, f32[1024,256]{1,0:T(8,128)}, u32[]{:S(2)}, u32[]{:S(2)}) collective-permute-start(f32[1024,256]{1,0:T(8,128)} %collective-permute-done.13.rest_1_), channel_id=1, source_target_pairs={{0,4},{4,0},{8,12},{12,8},{16,20},{20,16},{24,28},{28,24},{1,5},{5... | collective-permute-start | bytes 3145736 | tf_op jit(solution)/shard_map/ppermute | solution.py:695
  156.2 31.9 %collective-permute-start.28 = (f32[1024,256]{1,0:T(8,128)}, f32[1024,256]{1,0:T(8,128)S(1)}, u32[]{:S(2)}, u32[]{:S(2)}) collective-permute-start(f32[1024,256]{1,0:T(8,128)} %collective-permute-done.24.rest_4_), channel_id=1, source_target_pairs={{8,0},{12,4},{16,24},{20,28},{9,1},{13,5},{17,25},{21,29},{10,2},{... | collective-permute-start | bytes 3145736 | tf_op jit(solution)/shard_map/ppermute | solution.py:695
  158.9 29.3 %collective-permute-start.29 = (f32[1024,256]{1,0:T(8,128)S(1)}, f32[1024,256]{1,0:T(8,128)S(1)}, u32[]{:S(2)}, u32[]{:S(2)}) collective-permute-start(f32[1024,256]{1,0:T(8,128)S(1)} %broadcast_select_fusion), channel_id=1, source_target_pairs={{0,4},{4,0},{8,12},{12,8},{16,20},{20,16},{24,28},{28,24},{1,5},{5... | collective-permute-start | bytes 3145736 | tf_op jit(solution)/shard_map/ppermute | solution.py:695
  159.2 29.1 %collective-permute-start.30 = (f32[1024,256]{1,0:T(8,128)}, f32[1024,256]{1,0:T(8,128)S(1)}, u32[]{:S(2)}, u32[]{:S(2)}) collective-permute-start(f32[1024,256]{1,0:T(8,128)} %bitcast.3.rest_0_), channel_id=1, source_target_pairs={{8,16},{12,20},{16,8},{20,12},{9,17},{13,21},{17,9},{21,13},{10,18... | collective-permute-start | bytes 3145736 | tf_op jit(solution)/shard_map/ppermute | solution.py:695
  160.0 28.1 %collective-permute-start.27 = (f32[128,512]{1,0:T(8,128)S(1)}, f32[128,512]{1,0:T(8,128)S(1)}, u32[]{:S(2)}, u32[]{:S(2)}) collective-permute-start(f32[128,512]{1,0:T(8,128)S(1)} %constant_dynamic-slice_fusion.3), channel_id=1, source_target_pairs={{0,4},{4,0},{8,12},{12,8},{16,20},{20,16},{24,28},{28,24},{1,5},{5... | collective-permute-start | bytes 786440 | tf_op jit(solution)/shard_map/ppermute | solution.py:35
  189.2 16.5 %collective-permute-start.31 = (f32[128,512]{1,0:T(8,128)S(1)}, f32[128,512]{1,0:T(8,128)}, u32[]{:S(2)}, u32[]{:S(2)}) collective-permute-start(f32[128,512]{1,0:T(8,128)S(1)} %dynamic-slice_add_fusion.1), channel_id=1, source_target_pairs={{0,8},{4,12},{8,0},{12,4},{16,24},{20,28},{24,16},{28,20},{1,9},{5... | collective-permute-start | bytes 786440 | tf_op jit(solution)/shard_map/ppermute | solution.py:35
  206.8 14.1 %collective-permute-start.32 = (f32[128,512]{1,0:T(8,128)S(1)}, f32[128,512]{1,0:T(8,128)S(1)}, u32[]{:S(2)}, u32[]{:S(2)}) collective-permute-start(f32[128,512]{1,0:T(8,128)S(1)} %add.88), channel_id=1, source_target_pairs={{0,16},{4,20},{8,24},{12,28},{16,0},{20,4},{24,8},{28,12},{1,17},{... | collective-permute-start | bytes 786440 | tf_op jit(solution)/shard_map/ppermute | solution.py:35
  210.6 10.3 %collective-permute-start.34 = (f32[128,512]{1,0:T(8,128)S(1)}, f32[128,512]{1,0:T(8,128)S(1)}, u32[]{:S(2)}, u32[]{:S(2)}) collective-permute-start(f32[128,512]{1,0:T(8,128)S(1)} %constant_dynamic-slice_fusion.1), channel_id=1, source_target_pairs={{0,4},{4,0},{8,12},{12,8},{16,20},{20,16},{24,28},{28,24},{1,5},{5... | collective-permute-start | bytes 786440 | tf_op jit(solution)/shard_map/ppermute | solution.py:35
  220.9 7.2 %collective-permute-start.33 = (f32[128,512]{1,0:T(8,128)S(1)}, f32[128,512]{1,0:T(8,128)S(1)}, u32[]{:S(2)}, u32[]{:S(2)}) collective-permute-start(f32[128,512]{1,0:T(8,128)S(1)} %add.90), channel_id=1, source_target_pairs={{0,4},{4,0},{8,12},{12,8},{16,20},{20,16},{24,28},{28,24},{1,5},{5... | collective-permute-start | bytes 786440 | tf_op jit(solution)/shard_map/ppermute | solution.py:35
  229.2 14.8 %collective-permute-start.36 = (f32[128,512]{1,0:T(8,128)S(1)}, f32[128,512]{1,0:T(8,128)S(1)}, u32[]{:S(2)}, u32[]{:S(2)}) collective-permute-start(f32[128,512]{1,0:T(8,128)S(1)} %add.92), channel_id=1, source_target_pairs={{0,16},{4,20},{8,24},{12,28},{16,0},{20,4},{24,8},{28,12},{1,17},{... | collective-permute-start | bytes 786440 | tf_op jit(solution)/shard_map/ppermute | solution.py:35
  245.2 8.1 %collective-permute-start.37 = (f32[128,512]{1,0:T(8,128)S(1)}, f32[128,512]{1,0:T(8,128)S(1)}, u32[]{:S(2)}, u32[]{:S(2)}) collective-permute-start(f32[128,512]{1,0:T(8,128)S(1)} %add.93), channel_id=1, source_target_pairs={{0,4},{4,0},{8,12},{12,8},{16,20},{20,16},{24,28},{28,24},{1,5},{5... | collective-permute-start | bytes 786440 | tf_op jit(solution)/shard_map/ppermute | solution.py:35
  245.6 23.7 %collective-permute-start.48 = (f32[2,128,512]{2,1,0:T(8,128)S(1)}, f32[2,128,512]{2,1,0:T(8,128)S(1)}, u32[]{:S(2)}, u32[]{:S(2)}) collective-permute-start(f32[2,128,512]{2,1,0:T(8,128)S(1)} %bitcast.27), channel_id=1, source_target_pairs={{0,2},{1,3},{2,0},{3,1},{4,6},{5,7},{6,4},{7,5},{8,10},{9,11},{10,... | collective-permute-start | bytes 1572872 | tf_op jit(solution)/shard_map/ppermute | solution.py:35
  253.5 18.4 %collective-permute-start.51 = (f32[2,128,512]{2,1,0:T(8,128)S(1)}, f32[2,128,512]{2,1,0:T(8,128)S(1)}, u32[]{:S(2)}, u32[]{:S(2)}) collective-permute-start(f32[2,128,512]{2,1,0:T(8,128)S(1)} %bitcast.30), channel_id=1, source_target_pairs={{0,2},{1,3},{2,0},{3,1},{4,6},{5,7},{6,4},{7,5},{8,10},{9,11},{10,... | collective-permute-start | bytes 1572872 | tf_op jit(solution)/shard_map/ppermute | solution.py:35
  266.1 16.2 %collective-permute-start.47 = (f32[2,128,512]{2,1,0:T(8,128)S(1)}, f32[2,128,512]{2,1,0:T(8,128)S(1)}, u32[]{:S(2)}, u32[]{:S(2)}) collective-permute-start(f32[2,128,512]{2,1,0:T(8,128)S(1)} %bitcast.28), channel_id=1, source_target_pairs={{0,1},{1,0},{2,3},{3,2},{4,5},{5,4},{6,7},{7,6},{8,9},{9,8},{10,11... | collective-permute-start | bytes 1572872 | tf_op jit(solution)/shard_map/ppermute | solution.py:35
  269.2 16.5 %collective-permute-start.50 = (f32[2,128,512]{2,1,0:T(8,128)S(1)}, f32[2,128,512]{2,1,0:T(8,128)S(1)}, u32[]{:S(2)}, u32[]{:S(2)}) collective-permute-start(f32[2,128,512]{2,1,0:T(8,128)S(1)} %bitcast.32), channel_id=1, source_target_pairs={{0,1},{1,0},{2,3},{3,2},{4,5},{5,4},{6,7},{7,6},{8,9},{9,8},{10,11... | collective-permute-start | bytes 1572872 | tf_op jit(solution)/shard_map/ppermute | solution.py:35
  269.2 16.5 %collective-permute-start.49 = (f32[2,128,512]{2,1,0:T(8,128)S(1)}, f32[2,128,512]{2,1,0:T(8,128)S(1)}, u32[]{:S(2)}, u32[]{:S(2)}) collective-permute-start(f32[2,128,512]{2,1,0:T(8,128)S(1)} %collective-permute-done.48.refs_2_), channel_id=1, source_target_pairs={{0,1},{1,0},{2,3},{3,2},{4,5},{5,4},{6,7},{7,6},{8,9},{9,8},{10,11... | collective-permute-start | bytes 1572872 | tf_op jit(solution)/shard_map/ppermute | solution.py:35
  271.8 13.9 %collective-permute-start.52 = (f32[2,128,512]{2,1,0:T(8,128)S(1)}, f32[2,128,512]{2,1,0:T(8,128)S(1)}, u32[]{:S(2)}, u32[]{:S(2)}) collective-permute-start(f32[2,128,512]{2,1,0:T(8,128)S(1)} %collective-permute-done.51.refs_6_), channel_id=1, source_target_pairs={{0,1},{1,0},{2,3},{3,2},{4,5},{5,4},{6,7},{7,6},{8,9},{9,8},{10,11... | collective-permute-start | bytes 1572872 | tf_op jit(solution)/shard_map/ppermute | solution.py:35
  280.5 10.3 %collective-permute-start.53 = (f32[384,256]{1,0:T(8,128)S(1)}, f32[384,256]{1,0:T(8,128)S(1)}, u32[]{:S(2)}, u32[]{:S(2)}) collective-permute-start(f32[384,256]{1,0:T(8,128)S(1)} %get-tuple-element.246), channel_id=1, source_target_pairs={{0,2},{1,3},{2,0},{3,1},{4,6},{5,7},{6,4},{7,5},{8,10},{9,11},{10,... | collective-permute-start | bytes 1179656 | tf_op jit(solution)/shard_map/ppermute | solution.py:35
  282.4 18.2 %collective-permute-start.54 = (f32[256,256]{1,0:T(8,128)S(1)}, f32[256,256]{1,0:T(8,128)S(1)}, u32[]{:S(2)}, u32[]{:S(2)}) collective-permute-start(f32[256,256]{1,0:T(8,128)S(1)} %get-tuple-element.249), channel_id=1, source_target_pairs={{0,3},{1,2},{2,1},{3,0},{4,7},{5,6},{6,5},{7,4},{8,11},{9,10},{10,... | collective-permute-start | bytes 786440 | tf_op jit(solution)/shard_map/ppermute | solution.py:35
  290.9 16.3 %collective-permute-start.56 = (f32[384,256]{1,0:T(8,128)S(1)}, f32[384,256]{1,0:T(8,128)S(1)}, u32[]{:S(2)}, u32[]{:S(2)}) collective-permute-start(f32[384,256]{1,0:T(8,128)S(1)} %get-tuple-element.253), channel_id=1, source_target_pairs={{0,2},{1,3},{2,0},{3,1},{4,6},{5,7},{6,4},{7,5},{8,10},{9,11},{10,... | collective-permute-start | bytes 1179656 | tf_op jit(solution)/shard_map/ppermute | solution.py:35
  292.6 16.2 %collective-permute-start.42 = (f32[384,256]{1,0:T(8,128)S(1)}, f32[384,256]{1,0:T(8,128)S(1)}, u32[]{:S(2)}, u32[]{:S(2)}) collective-permute-start(f32[384,256]{1,0:T(8,128)S(1)} %get-tuple-element.241), channel_id=1, source_target_pairs={{0,1},{1,0},{2,3},{3,2},{4,5},{5,4},{6,7},{7,6},{8,9},{9,8},{10,11... | collective-permute-start | bytes 1179656 | tf_op jit(solution)/shard_map/ppermute | solution.py:35
  297.8 13.6 %collective-permute-start.55 = (f32[384,256]{1,0:T(8,128)S(1)}, f32[384,256]{1,0:T(8,128)S(1)}, u32[]{:S(2)}, u32[]{:S(2)}) collective-permute-start(f32[384,256]{1,0:T(8,128)S(1)} %get-tuple-element.252), channel_id=1, source_target_pairs={{0,1},{1,0},{2,3},{3,2},{4,5},{5,4},{6,7},{7,6},{8,9},{9,8},{10,11... | collective-permute-start | bytes 1179656 | tf_op jit(solution)/shard_map/ppermute | solution.py:35
  300.6 10.8 %collective-permute-start.57 = (f32[256,256]{1,0:T(8,128)S(1)}, f32[256,256]{1,0:T(8,128)S(1)}, u32[]{:S(2)}, u32[]{:S(2)}) collective-permute-start(f32[256,256]{1,0:T(8,128)S(1)} %get-tuple-element.254), channel_id=1, source_target_pairs={{0,3},{1,2},{2,1},{3,0},{4,7},{5,6},{6,5},{7,4},{8,11},{9,10},{10,... | collective-permute-start | bytes 786440 | tf_op jit(solution)/shard_map/ppermute | solution.py:35
  300.6 8.2 %collective-permute-start.58 = (f32[128,256]{1,0:T(8,128)S(1)}, f32[128,256]{1,0:T(8,128)S(1)}, u32[]{:S(2)}, u32[]{:S(2)}) collective-permute-start(f32[128,256]{1,0:T(8,128)S(1)} %slice.6), channel_id=1, source_target_pairs={{0,1},{1,0},{2,3},{3,2},{4,5},{5,4},{6,7},{7,6},{8,9},{9,8},{10,11... | collective-permute-start | bytes 393224 | tf_op jit(solution)/shard_map/ppermute | solution.py:35
  (36 other events, 260.9 us)

commit v5 on v4

--- a/solution.py
+++ b/solution.py
@@ -162,12 +162,12 @@
 
 
 ROUNDS = (
-    (("q1", 0), ("y1", 0), ("q2", 0)),
-    (("q3", 0), ("y2", 0), ("q1", 1)),
-    (("q5", 0), ("q4", 0), ("y1", 1)),
-    (("q6", 0), ("y3", 0), ("q3", 1)),
-    (("q5", 1), ("q4", 1), ("y2", 1)),
-    (("q6", 1), ("y3", 1), ("q2", 1)),
+    (("y1", 0), ("q1", 0), ("q2", 0)),
+    (("q1", 1), ("y2", 0), ("q3", 0)),
+    (("q4", 0), ("y1", 1), ("q5", 0)),
+    (("q6", 0), ("q3", 1), ("y3", 0)),
+    (("q4", 1), ("y2", 1), ("q5", 1)),
+    (("q6", 1), ("q2", 1), ("y3", 1)),
 )
 PLACES = (("own",), ("q1",), ("y1",), ("y2",), ("q5", "q4"), ("q2", "q6"), ("y3",))
 

time: 314 us -> 311 us (level)
  waiting for transfers between devices: 120 us -> 114 us
  starting transfers between devices: 81.9 us -> 85.2 us
    ppermute x42, starting transfers between devices: 56 us -> 61 us  [swap(): return lax.ppermute(value, axis, pairs_of(axis, k))]
    ppermute x18, waiting for transfers between devices: 31.1 us -> 26.8 us  [relay(): values[name, c] = lax.ppermute(value, 'blk', pairs)]
where the time goes in v5:
time: 311 us; the launch traced here: 310 us
  waiting for transfers between devices  114 us (37%)
  Pallas kernels  87.4 us (28%)
  starting transfers between devices  85.2 us (27%)
  local copies, waits for them, and re-layouts  15.3 us (5%)
  other arithmetic  7.12 us (2%)
    ppermute x42, waiting for transfers between devices, swap(): return lax.ppermute(value, axis, pairs_of(axis, k))  87.1 us
    ppermute x42, starting transfers between devices, swap(): return lax.ppermute(value, axis, pairs_of(axis, k))  61 us
    pallas_call x2, Pallas kernels, apply(): pl.pallas_call(functools.partial(apply_kernel, counts, near), grid=(row_b...  28.3 us
    ppermute x18, waiting for transfers between devices, relay(): values[name, c] = lax.ppermute(value, 'blk', pairs)  26.8 us
    ppermute x18, starting transfers between devices, relay(): values[name, c] = lax.ppermute(value, 'blk', pairs)  24.2 us
    pallas_call x2, Pallas kernels, project(): pl.pallas_call(functools.partial(project_kernel, orders), grid=(rows // t...  13.5 us
    unnamed x48, local copies, waits for them, and re-layouts  12.1 us
    pallas_call x2, Pallas kernels, finish(): pl.pallas_call(functools.partial(finish_kernel, groups, parts), out_shape...  10.2 us
  transfers between devices with their start and end apart: 60, of which 23 were waited for; matrix products, arithmetic and copies ran while one was open for 3% of the time, Pallas kernels for 27%

profile of v5, /device:TPU:1, one launch (start us, length us, event | category | flops | bytes accessed | tf_op | source)
XLA Modules:
  0.0 310.2 jit_solution(4948851709705648362)
XLA Ops:
  2.4 2.7 collective-permute-start.1
  5.1 6.5 %collective-permute-done.1.refs_2_ = f32[1,256,256]{2,1,0:T(8,128)S(1)} collective-permute-done((f32[1,256,256]{2,1,0:T(8,128)S(1)}, f32[1,256,256]{2,1,0:T(8,128)S(1)}, u32[]{:S(2)}, u32[]{:S(2)}) %collective-permute-start.1) | collective-permute-done | bytes 262176 | tf_op jit(solution)/shard_map/ppermute | solution.py:35
  11.7 5.6 %collective-permute-done.2.refs_3_ = f32[1,256,256]{2,1,0:T(8,128)S(1)} collective-permute-done((f32[1,256,256]{2,1,0:T(8,128)S(1)}, f32[1,256,256]{2,1,0:T(8,128)S(1)}, u32[]{:S(2)}, u32[]{:S(2)}) %collective-permute-start.2) | collective-permute-done | bytes 262176 | tf_op jit(solution)/shard_map/ppermute | solution.py:35
  24.5 2.7 cut_columns.6
  27.3 2.9 cut_columns.7
  32.2 3.7 %collective-permute-done.8.refs_3_ = f32[1,256,256]{2,1,0:T(8,128)S(1)} collective-permute-done((f32[1,256,256]{2,1,0:T(8,128)S(1)}, f32[1,256,256]{2,1,0:T(8,128)S(1)}, u32[]{:S(2)}, u32[]{:S(2)}) %collective-permute-start.8) | collective-permute-done | bytes 262176 | tf_op jit(solution)/shard_map/ppermute | solution.py:35
  38.2 3.7 %collective-permute-done.3.rest_2_ = f32[1024,256]{1,0:T(8,128)} collective-permute-done((f32[1024,256]{1,0:T(8,128)S(1)}, f32[1024,256]{1,0:T(8,128)}, u32[]{:S(2)}, u32[]{:S(2)}) %collective-permute-start.3) | collective-permute-done | bytes 1048608 | tf_op jit(solution)/shard_map/ppermute | solution.py:695
  43.1 4.3 %collective-permute-start.11 = (f32[1024,256]{1,0:T(8,128)}, f32[1024,256]{1,0:T(8,128)}, u32[]{:S(2)}, u32[]{:S(2)}) collective-permute-start(f32[1024,256]{1,0:T(8,128)} %bitcast.3.rest_0_), channel_id=1, source_target_pairs={{0,8},{4,12},{8,0},{12,4},{16,24},{20,28},{24,16},{28,20},{1,9},{5... | collective-permute-start | bytes 3145736 | tf_op jit(solution)/shard_map/ppermute | solution.py:695
  50.4 1.9 collective-permute-start.14
  52.3 8.6 %collective-permute-done.10.refs_2_ = f32[2,256,512]{2,1,0:T(8,128)S(1)} collective-permute-done((f32[2,256,512]{2,1,0:T(8,128)S(1)}, f32[2,256,512]{2,1,0:T(8,128)S(1)}, u32[]{:S(2)}, u32[]{:S(2)}) %collective-permute-start.10) | collective-permute-done | bytes 1048608 | tf_op jit(solution)/shard_map/ppermute | solution.py:35
  63.6 6.3 %collective-permute-done.11.rest_1_ = f32[1024,256]{1,0:T(8,128)} collective-permute-done((f32[1024,256]{1,0:T(8,128)}, f32[1024,256]{1,0:T(8,128)}, u32[]{:S(2)}, u32[]{:S(2)}) %collective-permute-start.11) | collective-permute-done | bytes 1048608 | tf_op jit(solution)/shard_map/ppermute | solution.py:695
  75.0 12.9 %collective-permute-done.15.refs_3_ = f32[2,256,512]{2,1,0:T(8,128)} collective-permute-done((f32[2,256,512]{2,1,0:T(8,128)}, f32[2,256,512]{2,1,0:T(8,128)}, u32[]{:S(2)}, u32[]{:S(2)}) %collective-permute-start.15) | collective-permute-done | bytes 1048608 | tf_op jit(solution)/shard_map/ppermute | solution.py:35
  88.0 7.0 %collective-permute-done.16.rest_5_ = f32[1024,256]{1,0:T(8,128)} collective-permute-done((f32[1024,256]{1,0:T(8,128)}, f32[1024,256]{1,0:T(8,128)}, u32[]{:S(2)}, u32[]{:S(2)}) %collective-permute-start.16) | collective-permute-done | bytes 1048608 | tf_op jit(solution)/shard_map/ppermute | solution.py:695
  98.0 2.3 broadcast_select_fusion.1
  101.8 4.6 %collective-permute-start.23 = (f32[2,256,512]{2,1,0:T(8,128)}, f32[2,256,512]{2,1,0:T(8,128)}, u32[]{:S(2)}, u32[]{:S(2)}) collective-permute-start(f32[2,256,512]{2,1,0:T(8,128)} %copy-done.16), channel_id=1, source_target_pairs={{0,3},{1,2},{2,1},{3,0},{4,7},{5,6},{6,5},{7,4},{8,11},{9,10},{10,... | collective-permute-start | bytes 3145736 | tf_op jit(solution)/shard_map/ppermute | solution.py:35
  107.1 1.9 gather_fusion
  110.5 3.5 %join_rows.6 = (bf16[2,1024,512]{2,1,0:T(8,128)(2,1)}, bf16[2,1024,512]{2,1,0:T(8,128)(2,1)}) custom-call(s32[1]{0:T(128)} %bitcast.me_ref.me, f32[4,256,2048]{2,1,0:T(8,128)} %refs_0_.7, f32[2,256,512]{2,1,0:T(8,128)S(1)} %collective-permute-done.9.refs_1_, f32[2,256,512]{2,1,0:T(8,128)S(1)} %copy-done.7, f32[2,256,512]{2,1,0:T(8,128)} %collective-permute-done.15.refs_3_), custom_call_target="tpu_custom_call" | custom-call | tf_op jit(solution)/shard_map/join_rows/pallas_call | solution.py:101
  114.1 7.4 %collective-permute-done.20.rest_7_ = f32[1024,256]{1,0:T(8,128)} collective-permute-done((f32[1024,256]{1,0:T(8,128)}, f32[1024,256]{1,0:T(8,128)}, u32[]{:S(2)}, u32[]{:S(2)}) %collective-permute-start.20) | collective-permute-done | bytes 1048608 | tf_op jit(solution)/shard_map/ppermute | solution.py:695
  127.4 5.4 %collective-permute-done.23.refs_3_ = f32[2,256,512]{2,1,0:T(8,128)} collective-permute-done((f32[2,256,512]{2,1,0:T(8,128)}, f32[2,256,512]{2,1,0:T(8,128)}, u32[]{:S(2)}, u32[]{:S(2)}) %collective-permute-start.23) | collective-permute-done | bytes 1048608 | tf_op jit(solution)/shard_map/ppermute | solution.py:35
  132.8 3.6 %join_rows.7 = (bf16[2,1024,512]{2,1,0:T(8,128)(2,1)}, bf16[2,1024,512]{2,1,0:T(8,128)(2,1)}) custom-call(s32[1]{0:T(128)} %bitcast.me_ref.me, f32[4,256,2048]{2,1,0:T(8,128)} %refs_0_.7, f32[2,256,512]{2,1,0:T(8,128)S(1)} %collective-permute-done.14.refs_1_, f32[2,256,512]{2,1,0:T(8,128)S(1)} %collective-permute-done.19.refs_2_, ...), custom_call_target="tpu_custom_call" | custom-call | tf_op jit(solution)/shard_map/join_rows/pallas_call | solution.py:101
  136.4 14.3 %apply.2.image = f32[1024,256]{1,0:T(8,128)S(1)} custom-call(s32[8,25]{1,0:T(8,128)S(1)} %get-tuple-element.270.places, s32[1]{0:T(128)} %bitcast.5.ends, f32[8,25,128,128]{3,2,1,0:T(8,128)} %strips.5, f32[1024,256]{1,0:T(8,128)S(1)} %bitcast.41, f32[1024,256]{1,0:T(8,128)S(1)} %copy-done.15, f32[1024,256]{1,0:T(8,128)} %collective-permute-done.3.rest_2_, ...), custom_call_target="tpu_custom_call" | custom-call | flops 6710886400 | bytes 21495808 | tf_op jit(solution)/shard_map/apply/pallas_call | solution.py:248
  150.7 3.2 %inner.2 = f32[2,128,512]{2,1,0:T(8,128)S(1)} custom-call(f32[1024,256]{1,0:T(8,128)S(1)} %apply.2.image, bf16[2,1024,512]{2,1,0:T(8,128)(2,1)S(1)} %copy-done, bf16[2,1024,512]{2,1,0:T(8,128)(2,1)S(1)} %copy-done, bf16[2,1024,512]{2,1,0:T(8,128)(2,1)} %get-tuple-element.226.rest_2_.rest_3_.rest_10_.rest_11_, ...), custom_call_target="tpu_custom_call" | custom-call | flops 805306368 | bytes 5242880 | tf_op jit(solution)/shard_map/inner/pallas_call | solution.py:380
  159.1 14.0 %apply.3.begun = f32[1024,256]{1,0:T(8,128)S(1)} custom-call(s32[8,25]{1,0:T(8,128)S(1)} %get-tuple-element.269.places, s32[1]{0:T(128)} %bitcast.5.ends, f32[8,25,128,128]{3,2,1,0:T(8,128)} %strips.5, f32[1024,256]{1,0:T(8,128)} %bitcast.3.rest_0_, f32[1024,256]{1,0:T(8,128)} %collective-permute-done.11.rest_1_, ...), custom_call_target="tpu_custom_call" | custom-call | flops 6710886400 | bytes 21495808 | tf_op jit(solution)/shard_map/apply/pallas_call | solution.py:248
  174.1 13.4 %collective-permute-done.27 = f32[128,512]{1,0:T(8,128)S(1)} collective-permute-done((f32[128,512]{1,0:T(8,128)S(1)}, f32[128,512]{1,0:T(8,128)S(1)}, u32[]{:S(2)}, u32[]{:S(2)}) %collective-permute-start.27) | collective-permute-done | bytes 262176 | tf_op jit(solution)/shard_map/ppermute | solution.py:35
  188.7 4.3 %collective-permute-start.31 = (f32[128,512]{1,0:T(8,128)S(1)}, f32[128,512]{1,0:T(8,128)}, u32[]{:S(2)}, u32[]{:S(2)}) collective-permute-start(f32[128,512]{1,0:T(8,128)S(1)} %dynamic-slice_add_fusion.1), channel_id=1, source_target_pairs={{0,8},{4,12},{8,0},{12,4},{16,24},{20,28},{24,16},{28,20},{1,9},{5... | collective-permute-start | bytes 786440 | tf_op jit(solution)/shard_map/ppermute | solution.py:35
  195.6 9.1 %apply_late.1.image = f32[1024,256]{1,0:T(8,128)S(1)} custom-call(s32[8,16]{1,0:T(8,128)S(1)} %bitcast.48, s32[8,16]{1,0:T(8,128)S(1)} %bitcast_select_fusion.found, s32[8]{0:T(128)S(1)} %convert_reduce_fusion.number, s32[1]{0:T(128)} %bitcast.5.ends, f32[1024,256]{1,0:T(8,128)S(1)} %copy-done.11, f32[8,25,128,128]{3,2,1,0:T(8,128)} %strips.5, ...), custom_call_target="tpu_custom_call" | custom-call | flops 2147483648 | bytes 8388608 | tf_op jit(solution)/shard_map/apply_late/pallas_call | solution.py:324
  206.7 2.9 inner.3
  212.2 6.9 %collective-permute-done.32 = f32[128,512]{1,0:T(8,128)S(1)} collective-permute-done((f32[128,512]{1,0:T(8,128)S(1)}, f32[128,512]{1,0:T(8,128)S(1)}, u32[]{:S(2)}, u32[]{:S(2)}) %collective-permute-start.32) | collective-permute-done | bytes 262176 | tf_op jit(solution)/shard_map/ppermute | solution.py:35
  221.2 3.9 %collective-permute-done.33 = f32[128,512]{1,0:T(8,128)S(1)} collective-permute-done((f32[128,512]{1,0:T(8,128)S(1)}, f32[128,512]{1,0:T(8,128)S(1)}, u32[]{:S(2)}, u32[]{:S(2)}) %collective-permute-start.33) | collective-permute-done | bytes 262176 | tf_op jit(solution)/shard_map/ppermute | solution.py:35
  227.8 6.6 %project.2 = (f32[1024,256]{1,0:T(8,128)S(1)}, f32[2,128,128]{2,1,0:T(8,128)S(1)}) custom-call(f32[1024,256]{1,0:T(8,128)S(1)} %copy-done.4, f32[2,128,512]{2,1,0:T(8,128)S(1)} %bitcast.26, bf16[2,1024,512]{2,1,0:T(8,128)(2,1)} %get-tuple-element.225.rest_0_.rest_1_.rest_8_.rest_9_, bf16[2,1024,512]{2,1,0:T(8,128)(2,1)} %get-tuple-element.225.rest_0_.rest_1_.rest_8_.rest_9_, ...), custom_call_target="tpu_custom_call" | custom-call | flops 1006632960 | bytes 6291456 | tf_op jit(solution)/shard_map/project/pallas_call | solution.py:416
  234.4 5.8 %collective-permute-done.36 = f32[128,512]{1,0:T(8,128)S(1)} collective-permute-done((f32[128,512]{1,0:T(8,128)S(1)}, f32[128,512]{1,0:T(8,128)S(1)}, u32[]{:S(2)}, u32[]{:S(2)}) %collective-permute-start.36) | collective-permute-done | bytes 262176 | tf_op jit(solution)/shard_map/ppermute | solution.py:35
  243.5 4.5 %collective-permute-done.37 = f32[128,512]{1,0:T(8,128)S(1)} collective-permute-done((f32[128,512]{1,0:T(8,128)S(1)}, f32[128,512]{1,0:T(8,128)S(1)}, u32[]{:S(2)}, u32[]{:S(2)}) %collective-permute-start.37) | collective-permute-done | bytes 262176 | tf_op jit(solution)/shard_map/ppermute | solution.py:35
  248.2 6.9 %project.3 = (f32[1024,256]{1,0:T(8,128)S(1)}, f32[2,128,128]{2,1,0:T(8,128)S(1)}) custom-call(f32[1024,256]{1,0:T(8,128)S(1)} %apply_late.1.image, f32[2,128,512]{2,1,0:T(8,128)S(1)} %bitcast.31, bf16[2,1024,512]{2,1,0:T(8,128)(2,1)} %get-tuple-element.225.rest_0_.rest_1_.rest_8_.rest_9_, ...), custom_call_target="tpu_custom_call" | custom-call | flops 1006632960 | bytes 6291456 | tf_op jit(solution)/shard_map/project/pallas_call | solution.py:416
  256.0 3.2 %collective-permute-start.40 = (f32[128,128]{1,0:T(8,128)S(1)}, f32[128,128]{1,0:T(8,128)S(1)}, u32[]{:S(2)}, u32[]{:S(2)}) collective-permute-start(f32[128,128]{1,0:T(8,128)S(1)} %add.95), channel_id=1, source_target_pairs={{0,16},{4,20},{8,24},{12,28},{16,0},{20,4},{24,8},{28,12},{1,17},{... | collective-permute-start | bytes 196616 | tf_op jit(solution)/shard_map/ppermute | solution.py:35
  261.7 3.5 %collective-permute-start.47 = (f32[2,128,512]{2,1,0:T(8,128)S(1)}, f32[2,128,512]{2,1,0:T(8,128)S(1)}, u32[]{:S(2)}, u32[]{:S(2)}) collective-permute-start(f32[2,128,512]{2,1,0:T(8,128)S(1)} %bitcast.28), channel_id=1, source_target_pairs={{0,1},{1,0},{2,3},{3,2},{4,5},{5,4},{6,7},{7,6},{8,9},{9,8},{10,11... | collective-permute-start | bytes 1572872 | tf_op jit(solution)/shard_map/ppermute | solution.py:35
  266.4 2.9 collective-permute-start.45
  269.2 2.1 collective-permute-start.52
  272.2 5.1 %finish.2 = (f32[384,256]{1,0:T(8,128)S(1)}, f32[384,256]{1,0:T(8,128)S(1)}, f32[384,256]{1,0:T(8,128)S(1)}, f32[256,256]{1,0:T(8,128)S(1)}) custom-call(s32[1]{0:T(128)} %bitcast.me_ref.me, f32[2,128,128]{2,1,0:T(8,128)S(1)} %bitcast.43, f32[1024,256]{1,0:T(8,128)S(1)} %get-tuple-element.239.residual), custom_call_target="tpu_custom_call" | custom-call | flops 201326592 | bytes 4194304 | tf_op jit(solution)/shard_map/finish/pallas_call | solution.py:504
  277.3 1.8 collective-permute-start.53
  279.2 2.5 collective-permute-start.54
  281.7 5.1 %finish.3 = (f32[384,256]{1,0:T(8,128)S(1)}, f32[384,256]{1,0:T(8,128)S(1)}, f32[384,256]{1,0:T(8,128)S(1)}, f32[256,256]{1,0:T(8,128)S(1)}) custom-call(s32[1]{0:T(128)} %bitcast.me_ref.me, f32[2,128,128]{2,1,0:T(8,128)S(1)} %bitcast.42, f32[1024,256]{1,0:T(8,128)S(1)} %get-tuple-element.244.residual), custom_call_target="tpu_custom_call" | custom-call | flops 201326592 | bytes 4194304 | tf_op jit(solution)/shard_map/finish/pallas_call | solution.py:504
  288.6 5.4 %collective-permute-start.42 = (f32[384,256]{1,0:T(8,128)S(1)}, f32[384,256]{1,0:T(8,128)S(1)}, u32[]{:S(2)}, u32[]{:S(2)}) collective-permute-start(f32[384,256]{1,0:T(8,128)S(1)} %get-tuple-element.241), channel_id=1, source_target_pairs={{0,1},{1,0},{2,3},{3,2},{4,5},{5,4},{6,7},{7,6},{8,9},{9,8},{10,11... | collective-permute-start | bytes 1179656 | tf_op jit(solution)/shard_map/ppermute | solution.py:35
  294.0 2.9 collective-permute-done.54.refs_3_
  296.9 2.2 collective-permute-start.58
  299.1 4.2 %collect_coeffs.1 = f32[4,16,128,128]{3,2,1,0:T(8,128)} custom-call(s32[1]{0:T(128)} %bitcast.me_ref.me, f32[2,128,512]{2,1,0:T(8,128)S(1)} %bitcast.29, f32[2,128,512]{2,1,0:T(8,128)S(1)} %collective-permute-done.47.refs_1_, f32[2,128,512]{2,1,0:T(8,128)S(1)} %collective-permute-done.48.refs_2_, f32[2,128,512]{2,1,0:T(8,128)S(1)} %collective-permute-done.49.refs_3_, ...), custom_call_target="tpu_custom_call" | custom-call | tf_op jit(solution)/shard_map/collect_coeffs/pallas_call | solution.py:560
  303.3 2.8 collective-permute-start.59
  306.1 2.1 collective-permute-done.57.refs_7_
  308.2 2.0 collect_blocks.1
  (187 shorter events, 67.5 us)
Async XLA Ops:
  2.4 9.3 %collective-permute-start.1 = (f32[1,256,256]{2,1,0:T(8,128)S(1)}, f32[1,256,256]{2,1,0:T(8,128)S(1)}, u32[]{:S(2)}, u32[]{:S(2)}) collective-permute-start(f32[1,256,256]{2,1,0:T(8,128)S(1)} %get-tuple-element.136), channel_id=1, source_target_pairs={{0,2},{1,3},{2,0},{3,1},{4,6},{5,7},{6,4},{7,5},{8,10},{9,11},{10,... | collective-permute-start | bytes 786440 | tf_op jit(solution)/shard_map/ppermute | solution.py:35
  5.1 12.2 %collective-permute-start.2 = (f32[1,256,256]{2,1,0:T(8,128)S(1)}, f32[1,256,256]{2,1,0:T(8,128)S(1)}, u32[]{:S(2)}, u32[]{:S(2)}) collective-permute-start(f32[1,256,256]{2,1,0:T(8,128)S(1)} %get-tuple-element.137), channel_id=1, source_target_pairs={{0,3},{1,2},{2,1},{3,0},{4,7},{5,6},{6,5},{7,4},{8,11},{9,10},{10,... | collective-permute-start | bytes 786440 | tf_op jit(solution)/shard_map/ppermute | solution.py:35
  17.4 24.6 %collective-permute-start.3 = (f32[1024,256]{1,0:T(8,128)S(1)}, f32[1024,256]{1,0:T(8,128)}, u32[]{:S(2)}, u32[]{:S(2)}) collective-permute-start(f32[1024,256]{1,0:T(8,128)S(1)} %bitcast.38), channel_id=1, source_target_pairs={{0,4},{4,0},{8,12},{12,8},{16,20},{20,16},{24,28},{28,24},{1,5},{5... | collective-permute-start | bytes 3145736 | tf_op jit(solution)/shard_map/ppermute | solution.py:695
  18.9 24.2 %collective-permute-start.4 = (f32[1024,256]{1,0:T(8,128)S(1)}, f32[1024,256]{1,0:T(8,128)S(1)}, u32[]{:S(2)}, u32[]{:S(2)}) collective-permute-start(f32[1024,256]{1,0:T(8,128)S(1)} %bitcast.39), channel_id=1, source_target_pairs={{0,8},{4,12},{8,0},{12,4},{16,24},{20,28},{24,16},{28,20},{1,9},{5... | collective-permute-start | bytes 3145736 | tf_op jit(solution)/shard_map/ppermute | solution.py:695
  20.2 22.9 %collective-permute-start.5 = (f32[1024,256]{1,0:T(8,128)S(1)}, f32[1024,256]{1,0:T(8,128)S(1)}, u32[]{:S(2)}, u32[]{:S(2)}) collective-permute-start(f32[1024,256]{1,0:T(8,128)S(1)} %bitcast.40), channel_id=1, source_target_pairs={{8,16},{12,20},{16,8},{20,12},{9,17},{13,21},{17,9},{21,13},{10,18... | collective-permute-start | bytes 3145736 | tf_op jit(solution)/shard_map/ppermute | solution.py:695
  21.9 10.2 %collective-permute-start.7 = (f32[1,256,256]{2,1,0:T(8,128)S(1)}, f32[1,256,256]{2,1,0:T(8,128)S(1)}, u32[]{:S(2)}, u32[]{:S(2)}) collective-permute-start(f32[1,256,256]{2,1,0:T(8,128)S(1)} %get-tuple-element.139), channel_id=1, source_target_pairs={{0,2},{1,3},{2,0},{3,1},{4,6},{5,7},{6,4},{7,5},{8,10},{9,11},{10,... | collective-permute-start | bytes 786440 | tf_op jit(solution)/shard_map/ppermute | solution.py:35
  23.1 12.8 %collective-permute-start.8 = (f32[1,256,256]{2,1,0:T(8,128)S(1)}, f32[1,256,256]{2,1,0:T(8,128)S(1)}, u32[]{:S(2)}, u32[]{:S(2)}) collective-permute-start(f32[1,256,256]{2,1,0:T(8,128)S(1)} %get-tuple-element.140), channel_id=1, source_target_pairs={{0,3},{1,2},{2,1},{3,0},{4,7},{5,6},{6,5},{7,4},{8,11},{9,10},{10,... | collective-permute-start | bytes 786440 | tf_op jit(solution)/shard_map/ppermute | solution.py:35
  32.1 18.3 %collective-permute-start.9 = (f32[2,256,512]{2,1,0:T(8,128)S(1)}, f32[2,256,512]{2,1,0:T(8,128)S(1)}, u32[]{:S(2)}, u32[]{:S(2)}) collective-permute-start(f32[2,256,512]{2,1,0:T(8,128)S(1)} %get-tuple-element.141), channel_id=1, source_target_pairs={{0,1},{1,0},{2,3},{3,2},{4,5},{5,4},{6,7},{7,6},{8,9},{9,8},{10,11... | collective-permute-start | bytes 3145736 | tf_op jit(solution)/shard_map/ppermute | solution.py:35
  35.9 25.0 %collective-permute-start.10 = (f32[2,256,512]{2,1,0:T(8,128)S(1)}, f32[2,256,512]{2,1,0:T(8,128)S(1)}, u32[]{:S(2)}, u32[]{:S(2)}) collective-permute-start(f32[2,256,512]{2,1,0:T(8,128)S(1)} %get-tuple-element.142), channel_id=1, source_target_pairs={{0,2},{1,3},{2,0},{3,1},{4,6},{5,7},{6,4},{7,5},{8,10},{9,11},{10,... | collective-permute-start | bytes 3145736 | tf_op jit(solution)/shard_map/ppermute | solution.py:35
  43.1 26.7 %collective-permute-start.11 = (f32[1024,256]{1,0:T(8,128)}, f32[1024,256]{1,0:T(8,128)}, u32[]{:S(2)}, u32[]{:S(2)}) collective-permute-start(f32[1024,256]{1,0:T(8,128)} %bitcast.3.rest_0_), channel_id=1, source_target_pairs={{0,8},{4,12},{8,0},{12,4},{16,24},{20,28},{24,16},{28,20},{1,9},{5... | collective-permute-start | bytes 3145736 | tf_op jit(solution)/shard_map/ppermute | solution.py:695
  47.4 23.1 %collective-permute-start.12 = (f32[1024,256]{1,0:T(8,128)S(1)}, f32[1024,256]{1,0:T(8,128)S(1)}, u32[]{:S(2)}, u32[]{:S(2)}) collective-permute-start(f32[1024,256]{1,0:T(8,128)S(1)} %collective-permute-done.4.rest_1_), channel_id=1, source_target_pairs={{0,4},{4,0},{8,12},{12,8},{16,20},{20,16},{24,28},{28,24},{1,5},{5... | collective-permute-start | bytes 3145736 | tf_op jit(solution)/shard_map/ppermute | solution.py:695
  47.7 22.9 %collective-permute-start.13 = (f32[1024,256]{1,0:T(8,128)S(1)}, f32[1024,256]{1,0:T(8,128)}, u32[]{:S(2)}, u32[]{:S(2)}) collective-permute-start(f32[1024,256]{1,0:T(8,128)S(1)} %collective-permute-done.4.rest_1_), channel_id=1, source_target_pairs={{8,16},{12,20},{16,8},{20,12},{9,17},{13,21},{17,9},{21,13},{10,18... | collective-permute-start | bytes 3145736 | tf_op jit(solution)/shard_map/ppermute | solution.py:695
  50.4 23.4 %collective-permute-start.14 = (f32[2,256,512]{2,1,0:T(8,128)}, f32[2,256,512]{2,1,0:T(8,128)S(1)}, u32[]{:S(2)}, u32[]{:S(2)}) collective-permute-start(f32[2,256,512]{2,1,0:T(8,128)} %get-tuple-element.148), channel_id=1, source_target_pairs={{0,1},{1,0},{2,3},{3,2},{4,5},{5,4},{6,7},{7,6},{8,9},{9,8},{10,11... | collective-permute-start | bytes 3145736 | tf_op jit(solution)/shard_map/ppermute | solution.py:35
  61.9 26.1 %collective-permute-start.15 = (f32[2,256,512]{2,1,0:T(8,128)}, f32[2,256,512]{2,1,0:T(8,128)}, u32[]{:S(2)}, u32[]{:S(2)}) collective-permute-start(f32[2,256,512]{2,1,0:T(8,128)} %get-tuple-element.147), channel_id=1, source_target_pairs={{0,3},{1,2},{2,1},{3,0},{4,7},{5,6},{6,5},{7,4},{8,11},{9,10},{10,... | collective-permute-start | bytes 3145736 | tf_op jit(solution)/shard_map/ppermute | solution.py:35
  70.6 24.4 %collective-permute-start.16 = (f32[1024,256]{1,0:T(8,128)}, f32[1024,256]{1,0:T(8,128)}, u32[]{:S(2)}, u32[]{:S(2)}) collective-permute-start(f32[1024,256]{1,0:T(8,128)} %collective-permute-done.13), channel_id=1, source_target_pairs={{8,0},{12,4},{16,24},{20,28},{9,1},{13,5},{17,25},{21,29},{10,2},{... | collective-permute-start | bytes 3145736 | tf_op jit(solution)/shard_map/ppermute | solution.py:695
  71.9 23.1 %collective-permute-start.17 = (f32[1024,256]{1,0:T(8,128)}, f32[1024,256]{1,0:T(8,128)}, u32[]{:S(2)}, u32[]{:S(2)}) collective-permute-start(f32[1024,256]{1,0:T(8,128)} %bitcast.3.rest_0_), channel_id=1, source_target_pairs={{0,4},{4,0},{8,12},{12,8},{16,20},{20,16},{24,28},{28,24},{1,5},{5... | collective-permute-start | bytes 3145736 | tf_op jit(solution)/shard_map/ppermute | solution.py:695
  72.2 22.8 %collective-permute-start.18 = (f32[1024,256]{1,0:T(8,128)}, f32[1024,256]{1,0:T(8,128)}, u32[]{:S(2)}, u32[]{:S(2)}) collective-permute-start(f32[1024,256]{1,0:T(8,128)} %collective-permute-done.3.rest_2_), channel_id=1, source_target_pairs={{8,16},{12,20},{16,8},{20,12},{9,17},{13,21},{17,9},{21,13},{10,18... | collective-permute-start | bytes 3145736 | tf_op jit(solution)/shard_map/ppermute | solution.py:695
  73.8 40.3 %collective-permute-start.19 = (f32[2,256,512]{2,1,0:T(8,128)}, f32[2,256,512]{2,1,0:T(8,128)S(1)}, u32[]{:S(2)}, u32[]{:S(2)}) collective-permute-start(f32[2,256,512]{2,1,0:T(8,128)} %copy-done.17), channel_id=1, source_target_pairs={{0,2},{1,3},{2,0},{3,1},{4,6},{5,7},{6,4},{7,5},{8,10},{9,11},{10,... | collective-permute-start | bytes 3145736 | tf_op jit(solution)/shard_map/ppermute | solution.py:35
  95.0 26.5 %collective-permute-start.20 = (f32[1024,256]{1,0:T(8,128)}, f32[1024,256]{1,0:T(8,128)}, u32[]{:S(2)}, u32[]{:S(2)}) collective-permute-start(f32[1024,256]{1,0:T(8,128)} %collective-permute-done.18.rest_4_), channel_id=1, source_target_pairs={{8,0},{12,4},{16,24},{20,28},{9,1},{13,5},{17,25},{21,29},{10,2},{... | collective-permute-start | bytes 3145736 | tf_op jit(solution)/shard_map/ppermute | solution.py:695
  96.3 25.2 %collective-permute-start.21 = (f32[1024,256]{1,0:T(8,128)}, f32[1024,256]{1,0:T(8,128)}, u32[]{:S(2)}, u32[]{:S(2)}) collective-permute-start(f32[1024,256]{1,0:T(8,128)} %collective-permute-done.11.rest_1_), channel_id=1, source_target_pairs={{8,16},{12,20},{16,8},{20,12},{9,17},{13,21},{17,9},{21,13},{10,18... | collective-permute-start | bytes 3145736 | tf_op jit(solution)/shard_map/ppermute | solution.py:695
  100.3 21.6 %collective-permute-start.22 = (f32[1024,256]{1,0:T(8,128)}, f32[1024,256]{1,0:T(8,128)}, u32[]{:S(2)}, u32[]{:S(2)}) collective-permute-start(f32[1024,256]{1,0:T(8,128)} %broadcast_select_fusion.1), channel_id=1, source_target_pairs={{0,4},{4,0},{8,12},{12,8},{16,20},{20,16},{24,28},{28,24},{1,5},{5... | collective-permute-start | bytes 3145736 | tf_op jit(solution)/shard_map/ppermute | solution.py:695
  101.8 31.0 %collective-permute-start.23 = (f32[2,256,512]{2,1,0:T(8,128)}, f32[2,256,512]{2,1,0:T(8,128)}, u32[]{:S(2)}, u32[]{:S(2)}) collective-permute-start(f32[2,256,512]{2,1,0:T(8,128)} %copy-done.16), channel_id=1, source_target_pairs={{0,3},{1,2},{2,1},{3,0},{4,7},{5,6},{6,5},{7,4},{8,11},{9,10},{10,... | collective-permute-start | bytes 3145736 | tf_op jit(solution)/shard_map/ppermute | solution.py:35
  121.9 32.0 %collective-permute-start.24 = (f32[1024,256]{1,0:T(8,128)}, f32[1024,256]{1,0:T(8,128)}, u32[]{:S(2)}, u32[]{:S(2)}) collective-permute-start(f32[1024,256]{1,0:T(8,128)} %collective-permute-done.21), channel_id=1, source_target_pairs={{8,0},{12,4},{16,24},{20,28},{9,1},{13,5},{17,25},{21,29},{10,2},{... | collective-permute-start | bytes 3145736 | tf_op jit(solution)/shard_map/ppermute | solution.py:695
  123.2 30.8 %collective-permute-start.25 = (f32[1024,256]{1,0:T(8,128)}, f32[1024,256]{1,0:T(8,128)}, u32[]{:S(2)}, u32[]{:S(2)}) collective-permute-start(f32[1024,256]{1,0:T(8,128)} %collective-permute-done.11.rest_1_), channel_id=1, source_target_pairs={{0,4},{4,0},{8,12},{12,8},{16,20},{20,16},{24,28},{28,24},{1,5},{5... | collective-permute-start | bytes 3145736 | tf_op jit(solution)/shard_map/ppermute | solution.py:695
  124.8 29.1 %collective-permute-start.26 = (f32[1024,256]{1,0:T(8,128)}, f32[1024,256]{1,0:T(8,128)}, u32[]{:S(2)}, u32[]{:S(2)}) collective-permute-start(f32[1024,256]{1,0:T(8,128)} %collective-permute-done.17.rest_2_), channel_id=1, source_target_pairs={{8,16},{12,20},{16,8},{20,12},{9,17},{13,21},{17,9},{21,13},{10,18... | collective-permute-start | bytes 3145736 | tf_op jit(solution)/shard_map/ppermute | solution.py:695
  154.0 33.6 %collective-permute-start.28 = (f32[1024,256]{1,0:T(8,128)}, f32[1024,256]{1,0:T(8,128)S(1)}, u32[]{:S(2)}, u32[]{:S(2)}) collective-permute-start(f32[1024,256]{1,0:T(8,128)} %collective-permute-done.26.rest_4_), channel_id=1, source_target_pairs={{8,0},{12,4},{16,24},{20,28},{9,1},{13,5},{17,25},{21,29},{10,2},{... | collective-permute-start | bytes 3145736 | tf_op jit(solution)/shard_map/ppermute | solution.py:695
  155.3 32.3 %collective-permute-start.29 = (f32[1024,256]{1,0:T(8,128)}, f32[1024,256]{1,0:T(8,128)S(1)}, u32[]{:S(2)}, u32[]{:S(2)}) collective-permute-start(f32[1024,256]{1,0:T(8,128)} %bitcast.3.rest_0_), channel_id=1, source_target_pairs={{8,16},{12,20},{16,8},{20,12},{9,17},{13,21},{17,9},{21,13},{10,18... | collective-permute-start | bytes 3145736 | tf_op jit(solution)/shard_map/ppermute | solution.py:695
  157.4 31.3 %collective-permute-start.30 = (f32[1024,256]{1,0:T(8,128)S(1)}, f32[1024,256]{1,0:T(8,128)S(1)}, u32[]{:S(2)}, u32[]{:S(2)}) collective-permute-start(f32[1024,256]{1,0:T(8,128)S(1)} %broadcast_select_fusion), channel_id=1, source_target_pairs={{0,4},{4,0},{8,12},{12,8},{16,20},{20,16},{24,28},{28,24},{1,5},{5... | collective-permute-start | bytes 3145736 | tf_op jit(solution)/shard_map/ppermute | solution.py:695
  157.8 29.7 %collective-permute-start.27 = (f32[128,512]{1,0:T(8,128)S(1)}, f32[128,512]{1,0:T(8,128)S(1)}, u32[]{:S(2)}, u32[]{:S(2)}) collective-permute-start(f32[128,512]{1,0:T(8,128)S(1)} %constant_dynamic-slice_fusion.3), channel_id=1, source_target_pairs={{0,4},{4,0},{8,12},{12,8},{16,20},{20,16},{24,28},{28,24},{1,5},{5... | collective-permute-start | bytes 786440 | tf_op jit(solution)/shard_map/ppermute | solution.py:35
  188.7 16.0 %collective-permute-start.31 = (f32[128,512]{1,0:T(8,128)S(1)}, f32[128,512]{1,0:T(8,128)}, u32[]{:S(2)}, u32[]{:S(2)}) collective-permute-start(f32[128,512]{1,0:T(8,128)S(1)} %dynamic-slice_add_fusion.1), channel_id=1, source_target_pairs={{0,8},{4,12},{8,0},{12,4},{16,24},{20,28},{24,16},{28,20},{1,9},{5... | collective-permute-start | bytes 786440 | tf_op jit(solution)/shard_map/ppermute | solution.py:35
  205.7 13.4 %collective-permute-start.32 = (f32[128,512]{1,0:T(8,128)S(1)}, f32[128,512]{1,0:T(8,128)S(1)}, u32[]{:S(2)}, u32[]{:S(2)}) collective-permute-start(f32[128,512]{1,0:T(8,128)S(1)} %add.88), channel_id=1, source_target_pairs={{0,16},{4,20},{8,24},{12,28},{16,0},{20,4},{24,8},{28,12},{1,17},{... | collective-permute-start | bytes 786440 | tf_op jit(solution)/shard_map/ppermute | solution.py:35
  210.5 9.7 %collective-permute-start.34 = (f32[128,512]{1,0:T(8,128)S(1)}, f32[128,512]{1,0:T(8,128)S(1)}, u32[]{:S(2)}, u32[]{:S(2)}) collective-permute-start(f32[128,512]{1,0:T(8,128)S(1)} %constant_dynamic-slice_fusion.1), channel_id=1, source_target_pairs={{0,4},{4,0},{8,12},{12,8},{16,20},{20,16},{24,28},{28,24},{1,5},{5... | collective-permute-start | bytes 786440 | tf_op jit(solution)/shard_map/ppermute | solution.py:35
  226.8 13.4 %collective-permute-start.36 = (f32[128,512]{1,0:T(8,128)S(1)}, f32[128,512]{1,0:T(8,128)S(1)}, u32[]{:S(2)}, u32[]{:S(2)}) collective-permute-start(f32[128,512]{1,0:T(8,128)S(1)} %add.92), channel_id=1, source_target_pairs={{0,16},{4,20},{8,24},{12,28},{16,0},{20,4},{24,8},{28,12},{1,17},{... | collective-permute-start | bytes 786440 | tf_op jit(solution)/shard_map/ppermute | solution.py:35
  240.4 7.6 %collective-permute-start.37 = (f32[128,512]{1,0:T(8,128)S(1)}, f32[128,512]{1,0:T(8,128)S(1)}, u32[]{:S(2)}, u32[]{:S(2)}) collective-permute-start(f32[128,512]{1,0:T(8,128)S(1)} %add.93), channel_id=1, source_target_pairs={{0,4},{4,0},{8,12},{12,8},{16,20},{20,16},{24,28},{28,24},{1,5},{5... | collective-permute-start | bytes 786440 | tf_op jit(solution)/shard_map/ppermute | solution.py:35
  241.8 23.4 %collective-permute-start.48 = (f32[2,128,512]{2,1,0:T(8,128)S(1)}, f32[2,128,512]{2,1,0:T(8,128)S(1)}, u32[]{:S(2)}, u32[]{:S(2)}) collective-permute-start(f32[2,128,512]{2,1,0:T(8,128)S(1)} %bitcast.27), channel_id=1, source_target_pairs={{0,2},{1,3},{2,0},{3,1},{4,6},{5,7},{6,4},{7,5},{8,10},{9,11},{10,... | collective-permute-start | bytes 1572872 | tf_op jit(solution)/shard_map/ppermute | solution.py:35
  248.0 7.1 %collective-permute-start.39 = (f32[128,128]{1,0:T(8,128)S(1)}, f32[128,128]{1,0:T(8,128)S(1)}, u32[]{:S(2)}, u32[]{:S(2)}) collective-permute-start(f32[128,128]{1,0:T(8,128)S(1)} %dynamic-slice_add_fusion.3), channel_id=1, source_target_pairs={{0,8},{4,12},{8,0},{12,4},{16,24},{20,28},{24,16},{28,20},{1,9},{5... | collective-permute-start | bytes 196616 | tf_op jit(solution)/shard_map/ppermute | solution.py:35
  248.1 21.1 %collective-permute-start.51 = (f32[2,128,512]{2,1,0:T(8,128)S(1)}, f32[2,128,512]{2,1,0:T(8,128)S(1)}, u32[]{:S(2)}, u32[]{:S(2)}) collective-permute-start(f32[2,128,512]{2,1,0:T(8,128)S(1)} %bitcast.30), channel_id=1, source_target_pairs={{0,2},{1,3},{2,0},{3,1},{4,6},{5,7},{6,4},{7,5},{8,10},{9,11},{10,... | collective-permute-start | bytes 1572872 | tf_op jit(solution)/shard_map/ppermute | solution.py:35
  261.7 17.5 %collective-permute-start.47 = (f32[2,128,512]{2,1,0:T(8,128)S(1)}, f32[2,128,512]{2,1,0:T(8,128)S(1)}, u32[]{:S(2)}, u32[]{:S(2)}) collective-permute-start(f32[2,128,512]{2,1,0:T(8,128)S(1)} %bitcast.28), channel_id=1, source_target_pairs={{0,1},{1,0},{2,3},{3,2},{4,5},{5,4},{6,7},{7,6},{8,9},{9,8},{10,11... | collective-permute-start | bytes 1572872 | tf_op jit(solution)/shard_map/ppermute | solution.py:35
  265.2 16.5 %collective-permute-start.50 = (f32[2,128,512]{2,1,0:T(8,128)S(1)}, f32[2,128,512]{2,1,0:T(8,128)S(1)}, u32[]{:S(2)}, u32[]{:S(2)}) collective-permute-start(f32[2,128,512]{2,1,0:T(8,128)S(1)} %bitcast.32), channel_id=1, source_target_pairs={{0,1},{1,0},{2,3},{3,2},{4,5},{5,4},{6,7},{7,6},{8,9},{9,8},{10,11... | collective-permute-start | bytes 1572872 | tf_op jit(solution)/shard_map/ppermute | solution.py:35
  265.2 16.5 %collective-permute-start.49 = (f32[2,128,512]{2,1,0:T(8,128)S(1)}, f32[2,128,512]{2,1,0:T(8,128)S(1)}, u32[]{:S(2)}, u32[]{:S(2)}) collective-permute-start(f32[2,128,512]{2,1,0:T(8,128)S(1)} %collective-permute-done.48.refs_2_), channel_id=1, source_target_pairs={{0,1},{1,0},{2,3},{3,2},{4,5},{5,4},{6,7},{7,6},{8,9},{9,8},{10,11... | collective-permute-start | bytes 1572872 | tf_op jit(solution)/shard_map/ppermute | solution.py:35
  269.2 12.4 %collective-permute-start.52 = (f32[2,128,512]{2,1,0:T(8,128)S(1)}, f32[2,128,512]{2,1,0:T(8,128)S(1)}, u32[]{:S(2)}, u32[]{:S(2)}) collective-permute-start(f32[2,128,512]{2,1,0:T(8,128)S(1)} %collective-permute-done.51.refs_6_), channel_id=1, source_target_pairs={{0,1},{1,0},{2,3},{3,2},{4,5},{5,4},{6,7},{7,6},{8,9},{9,8},{10,11... | collective-permute-start | bytes 1572872 | tf_op jit(solution)/shard_map/ppermute | solution.py:35
  277.3 9.5 %collective-permute-start.53 = (f32[384,256]{1,0:T(8,128)S(1)}, f32[384,256]{1,0:T(8,128)S(1)}, u32[]{:S(2)}, u32[]{:S(2)}) collective-permute-start(f32[384,256]{1,0:T(8,128)S(1)} %get-tuple-element.246), channel_id=1, source_target_pairs={{0,2},{1,3},{2,0},{3,1},{4,6},{5,7},{6,4},{7,5},{8,10},{9,11},{10,... | collective-permute-start | bytes 1179656 | tf_op jit(solution)/shard_map/ppermute | solution.py:35
  279.2 17.7 %collective-permute-start.54 = (f32[256,256]{1,0:T(8,128)S(1)}, f32[256,256]{1,0:T(8,128)S(1)}, u32[]{:S(2)}, u32[]{:S(2)}) collective-permute-start(f32[256,256]{1,0:T(8,128)S(1)} %get-tuple-element.249), channel_id=1, source_target_pairs={{0,3},{1,2},{2,1},{3,0},{4,7},{5,6},{6,5},{7,4},{8,11},{9,10},{10,... | collective-permute-start | bytes 786440 | tf_op jit(solution)/shard_map/ppermute | solution.py:35
  286.8 16.5 %collective-permute-start.56 = (f32[384,256]{1,0:T(8,128)S(1)}, f32[384,256]{1,0:T(8,128)S(1)}, u32[]{:S(2)}, u32[]{:S(2)}) collective-permute-start(f32[384,256]{1,0:T(8,128)S(1)} %get-tuple-element.253), channel_id=1, source_target_pairs={{0,2},{1,3},{2,0},{3,1},{4,6},{5,7},{6,4},{7,5},{8,10},{9,11},{10,... | collective-permute-start | bytes 1179656 | tf_op jit(solution)/shard_map/ppermute | solution.py:35
  288.6 17.5 %collective-permute-start.42 = (f32[384,256]{1,0:T(8,128)S(1)}, f32[384,256]{1,0:T(8,128)S(1)}, u32[]{:S(2)}, u32[]{:S(2)}) collective-permute-start(f32[384,256]{1,0:T(8,128)S(1)} %get-tuple-element.241), channel_id=1, source_target_pairs={{0,1},{1,0},{2,3},{3,2},{4,5},{5,4},{6,7},{7,6},{8,9},{9,8},{10,11... | collective-permute-start | bytes 1179656 | tf_op jit(solution)/shard_map/ppermute | solution.py:35
  294.0 14.2 %collective-permute-start.55 = (f32[384,256]{1,0:T(8,128)S(1)}, f32[384,256]{1,0:T(8,128)S(1)}, u32[]{:S(2)}, u32[]{:S(2)}) collective-permute-start(f32[384,256]{1,0:T(8,128)S(1)} %get-tuple-element.252), channel_id=1, source_target_pairs={{0,1},{1,0},{2,3},{3,2},{4,5},{5,4},{6,7},{7,6},{8,9},{9,8},{10,11... | collective-permute-start | bytes 1179656 | tf_op jit(solution)/shard_map/ppermute | solution.py:35
  296.9 11.3 %collective-permute-start.57 = (f32[256,256]{1,0:T(8,128)S(1)}, f32[256,256]{1,0:T(8,128)S(1)}, u32[]{:S(2)}, u32[]{:S(2)}) collective-permute-start(f32[256,256]{1,0:T(8,128)S(1)} %get-tuple-element.254), channel_id=1, source_target_pairs={{0,3},{1,2},{2,1},{3,0},{4,7},{5,6},{6,5},{7,4},{8,11},{9,10},{10,... | collective-permute-start | bytes 786440 | tf_op jit(solution)/shard_map/ppermute | solution.py:35
  296.9 9.2 %collective-permute-start.58 = (f32[128,256]{1,0:T(8,128)S(1)}, f32[128,256]{1,0:T(8,128)S(1)}, u32[]{:S(2)}, u32[]{:S(2)}) collective-permute-start(f32[128,256]{1,0:T(8,128)S(1)} %slice.6), channel_id=1, source_target_pairs={{0,1},{1,0},{2,3},{3,2},{4,5},{5,4},{6,7},{7,6},{8,9},{9,8},{10,11... | collective-permute-start | bytes 393224 | tf_op jit(solution)/shard_map/ppermute | solution.py:35
  (36 other events, 253.9 us)
